TPU v7x, 512 devices: a whole 4x8x8 slice. The times are simulated.
512 devices in a mesh: pair: 128 (over z, y, core), blk: 4 (over x).
Axes of the slice: x: 4, y: 8, z: 8, core: 2. Of those that a mesh axis runs over, the one named last changes fastest.
Arguments:
- amplitudes: bfloat16 [512, 102400], P(('pair', 'blk')), may hold values from -6 to 6
- integrals: bfloat16 [102400, 3200], P('pair', 'blk'), may hold values from -0.02734375 to 0.02734375
- residual_in: bfloat16 [512, 3200], P(('pair', 'blk')), may hold values from -6 to 6
- pair_irrep: int32 [512], P(('pair', 'blk')), may hold values from 0 to 7, as said below
- slab_irrep: int32 [128], replicated, may hold values from 0 to 7, as said below
- upper_irrep: int32 [4], replicated, may hold values from 0 to 7, as said below
- virt_irrep: int32 [800], replicated, may hold values from 0 to 7, as said below
Outputs:
- residual_out: bfloat16 [512, 3200], P(('pair', 'blk'))
Inputs may be any that keep to these rules, and one draw needn't show every extreme that they name: `pair_irrep`: D2h irrep label of each occupied pair. `slab_irrep`: D2h irrep label of each lower slab orbital. `upper_irrep`: D2h irrep label of each upper slab orbital. `virt_irrep`: D2h irrep label of each virtual orbital.
All inputs are finite; a program needn't handle non-finite values.
Results may differ from a plain program's by a relative error of at most 0.00105.
Values may be sent and summed in bfloat16 or wider, within the bound.
No kernel may reach another device: no remote copies, remote signals or barrier semaphores. Data moves between devices by JAX's collectives and lax.ppermute only.
A program may use at most 64 MiB of HBM per device.

v0:
```python
import jax
import jax.numpy as jnp
from jax import lax
from jax.sharding import PartitionSpec as P


def passed_along(block, axis, distance):
    devices = range(lax.axis_size(axis))
    route = [((i - distance) % len(devices), i) for i in devices]
    return lax.ppermute(block, axis, route)


def per_device(amplitudes, integrals, residual_in, pair_irrep, slab_irrep, upper_irrep, virt_irrep):
    num_blk = lax.axis_size("blk")
    pair_pos = lax.axis_index("pair")
    blk_pos = lax.axis_index("blk")
    cd_rows = integrals.shape[0]
    slab_width = integrals.shape[1]
    cd_irrep = jnp.bitwise_xor(slab_irrep[:, None], virt_irrep[None, :]).reshape(-1)
    ab_irrep = jnp.bitwise_xor(upper_irrep[:, None], virt_irrep[None, :]).reshape(-1)
    kept_amp = jnp.where(
        pair_irrep[:, None] == cd_irrep[None, :], amplitudes, jnp.zeros((), amplitudes.dtype)
    )
    regrouped = lax.all_to_all(kept_amp, "pair", split_axis=1, concat_axis=0, tiled=True)
    my_cd = lax.dynamic_slice_in_dim(cd_irrep, pair_pos * cd_rows, cd_rows, 0)
    my_ab = lax.dynamic_slice_in_dim(ab_irrep, blk_pos * slab_width, slab_width, 0)
    kept_int = jnp.where(
        my_cd[:, None] == my_ab[None, :], integrals, jnp.zeros((), integrals.dtype)
    )
    order = (blk_pos - jnp.arange(num_blk, dtype=jnp.int32)) % num_blk
    holding = regrouped
    products = []
    for turn in range(num_blk):
        if turn > 0:
            holding = passed_along(holding, "blk", 1)
        products.append(jnp.dot(holding, kept_int, preferred_element_type=jnp.float32))
    summed = lax.psum_scatter(jnp.stack(products), "pair", scatter_dimension=1, tiled=True)
    by_group = jnp.take(summed, order, axis=0)
    returned = lax.all_to_all(by_group, "blk", split_axis=0, concat_axis=2, tiled=True)
    ladder = returned.reshape(returned.shape[1], returned.shape[2])
    return (residual_in.astype(jnp.float32) + ladder).astype(jnp.bfloat16)


def solution(mesh):
    return jax.shard_map(
        per_device,
        mesh=mesh,
        in_specs=(
            P(("pair", "blk"), None),
            P("pair", "blk"),
            P(("pair", "blk"), None),
            P(("pair", "blk")),
            P(),
            P(),
            P(),
        ),
        out_specs=P(("pair", "blk"), None),
        check_vma=False,
    )
```

profile of v0, /device:TPU:1, one launch (start us, length us, event | category | flops | bytes accessed | tf_op | source)
XLA Modules:
  0.0 288.6 jit_solution(5227247557696260367)
XLA Ops:
  7.2 0.8 broadcast_compare_fusion
  8.0 0.5 eq.39
  8.5 2.6 select_reduce_fusion
  11.0 0.0 copy-start
  11.1 0.0 copy-start.3
  11.1 0.0 copy-start.2
  11.1 0.4 all_to_all.23
  11.5 0.5 broadcast.149
  12.0 2.1 reduce.3
  14.1 1.0 reshape.148
  15.0 18.4 %all-to-all-start = ((bf16[128,2,400]{2,1,0:T(2,128)(2,1)}), bf16[128,2,400]{2,1,0:T(2,128)(2,1)S(1)}, u32[]{:S(2)}, u32[]{:S(2)}) async-start(bf16[128,2,400]{2,1,0:T(2,128)(2,1)} %reshape.148), calls=%async_computation | async-start | bytes 524288 | tf_op jit(solution)/shard_map/all_to_all | solution.py:24
  33.4 0.0 copy-start.4
  33.5 0.0 all-reduce.3.cloned.1.call-start
  33.5 0.0 copy-done
  33.5 0.0 copy-done.3
  33.5 0.1 broadcast_xor_fusion.1
  33.6 0.1 xor.50
  33.7 0.0 copy-done.2
  33.7 0.1 broadcast_xor_fusion
  33.8 0.3 xor.46
  34.1 0.1 dynamic_slice.7
  34.2 0.1 dynamic_slice.6
  34.3 14.4 %all-to-all-done = bf16[128,2,400]{2,1,0:T(2,128)(2,1)S(1)} async-done(((bf16[128,2,400]{2,1,0:T(2,128)(2,1)}), bf16[128,2,400]{2,1,0:T(2,128)(2,1)S(1)}, u32[]{:S(2)}, u32[]{:S(2)}) %all-to-all-start) | async-done | bytes 204832 | tf_op jit(solution)/shard_map/all_to_all | solution.py:24
  48.7 0.5 reshape.149
  49.2 0.7 copy.12
  49.9 3.1 %collective-permute-start = (bf16[128,800]{0,1:T(8,128)(2,1)S(1)}, bf16[128,800]{0,1:T(8,128)(2,1)S(1)}, u32[]{:S(2)}, u32[]{:S(2)}) collective-permute-start(bf16[128,800]{0,1:T(8,128)(2,1)S(1)} %bitcast.27), channel_id=1, source_target_pairs={{3,0},{0,1},{1,2},{2,3},{7,4},{4,5},{5,6},{6,7},{11,8},{8,9},{9,10... | collective-permute-start | bytes 614408 | tf_op jit(solution)/shard_map/ppermute | solution.py:10
  53.0 0.0 copy-done.4
  53.1 0.9 convolution_bitcast_fusion.3
  54.0 5.3 %collective-permute-done = bf16[128,800]{0,1:T(8,128)(2,1)S(1)} collective-permute-done((bf16[128,800]{0,1:T(8,128)(2,1)S(1)}, bf16[128,800]{0,1:T(8,128)(2,1)S(1)}, u32[]{:S(2)}, u32[]{:S(2)}) %collective-permute-start) | collective-permute-done | bytes 204832 | tf_op jit(solution)/shard_map/ppermute | solution.py:10
  59.3 1.9 collective-permute-start.1
  61.2 0.9 convolution_bitcast_fusion.2
  62.2 5.6 %collective-permute-done.1 = bf16[128,800]{0,1:T(8,128)(2,1)S(1)} collective-permute-done((bf16[128,800]{0,1:T(8,128)(2,1)S(1)}, bf16[128,800]{0,1:T(8,128)(2,1)S(1)}, u32[]{:S(2)}, u32[]{:S(2)}) %collective-permute-start.1) | collective-permute-done | bytes 204832 | tf_op jit(solution)/shard_map/ppermute | solution.py:10
  67.8 2.1 collective-permute-start.2
  69.9 0.9 convolution_bitcast_fusion.1
  70.8 4.7 %collective-permute-done.2 = bf16[128,800]{0,1:T(8,128)(2,1)S(1)} collective-permute-done((bf16[128,800]{0,1:T(8,128)(2,1)S(1)}, bf16[128,800]{0,1:T(8,128)(2,1)S(1)}, u32[]{:S(2)}, u32[]{:S(2)}) %collective-permute-start.2) | collective-permute-done | bytes 204832 | tf_op jit(solution)/shard_map/ppermute | solution.py:10
  75.5 0.9 convolution_bitcast_fusion
  76.4 0.1 pad_maximum_fusion
  76.5 2.0 copy.13
  78.5 0.0 all-reduce.3.cloned.1.call-update
  78.6 1.3 dynamic-slice
  79.9 191.1 %all-reduce.3.cloned.1.call-done = f32[4,128,800]{2,0,1:T(4,128)} async-done(((f32[4,128,800]{2,0,1:T(4,128)}), f32[4,128,800]{2,0,1:T(4,128)}) %all-reduce.3.cloned.1.call-update) | async-done | bytes 1638416
  271.0 1.4 dynamic-slice_bitcast_fusion
  272.3 0.6 gather_fusion
  272.9 0.1 bitcast_select_fusion
  273.0 8.0 %all_to_all.26 = f32[4,1,800]{2,1,0:T(1,128)S(1)} all-to-all(f32[4,1,800]{2,1,0:T(1,128)S(1)} %copy.14), channel_id=1, replica_groups=mesh['pair'=128,'blk'=4] {'blk'}, dimensions={0} | all-to-all | bytes 25600 | tf_op jit(solution)/shard_map/all_to_all | solution.py:39
  281.0 0.1 reshape.134
  281.1 0.0 copy-done.1
  281.1 0.6 add_convert_fusion
  (6 shorter events, 0.1 us)
Async XLA Ops:
  11.0 22.5 %copy-start = (s32[800]{0:T(1024)S(1)}, s32[800]{0:T(1024)}, u32[]{:S(2)}) copy-start(s32[800]{0:T(1024)} %param.13) | copy-start | bytes 9604
  11.1 22.5 %copy-start.3 = (s32[4]{0:T(128)S(1)}, s32[4]{0:T(128)}, u32[]{:S(2)}) copy-start(s32[4]{0:T(128)} %param.12) | copy-start | bytes 52
  11.1 22.6 %copy-start.2 = (s32[128]{0:T(128)S(1)}, s32[128]{0:T(128)}, u32[]{:S(2)}) copy-start(s32[128]{0:T(128)} %param.11) | copy-start | bytes 1540
  15.0 33.7 %all-to-all-start = ((bf16[128,2,400]{2,1,0:T(2,128)(2,1)}), bf16[128,2,400]{2,1,0:T(2,128)(2,1)S(1)}, u32[]{:S(2)}, u32[]{:S(2)}) async-start(bf16[128,2,400]{2,1,0:T(2,128)(2,1)} %reshape.148), calls=%async_computation | async-start | bytes 524288 | tf_op jit(solution)/shard_map/all_to_all | solution.py:24
  33.4 19.6 %copy-start.4 = (bf16[800,800]{1,0:T(8,128)(2,1)S(1)}, bf16[800,800]{1,0:T(8,128)(2,1)}, u32[]{:S(2)}) copy-start(bf16[800,800]{1,0:T(8,128)(2,1)} %param.8) | copy-start | bytes 3840004
  33.5 237.5 %all-reduce.3.cloned.1.call-start = ((), (), s32[]{:S(2)}) async-start(), calls=%async_computation.2 | async-start | bytes 3670016
  49.9 9.4 %collective-permute-start = (bf16[128,800]{0,1:T(8,128)(2,1)S(1)}, bf16[128,800]{0,1:T(8,128)(2,1)S(1)}, u32[]{:S(2)}, u32[]{:S(2)}) collective-permute-start(bf16[128,800]{0,1:T(8,128)(2,1)S(1)} %bitcast.27), channel_id=1, source_target_pairs={{3,0},{0,1},{1,2},{2,3},{7,4},{4,5},{5,6},{6,7},{11,8},{8,9},{9,10... | collective-permute-start | bytes 614408 | tf_op jit(solution)/shard_map/ppermute | solution.py:10
  59.3 8.5 %collective-permute-start.1 = (bf16[128,800]{0,1:T(8,128)(2,1)S(1)}, bf16[128,800]{0,1:T(8,128)(2,1)S(1)}, u32[]{:S(2)}, u32[]{:S(2)}) collective-permute-start(bf16[128,800]{0,1:T(8,128)(2,1)S(1)} %collective-permute-done), channel_id=1, source_target_pairs={{3,0},{0,1},{1,2},{2,3},{7,4},{4,5},{5,6},{6,7},{11,8},{8,9},{9,10... | collective-permute-start | bytes 614408 | tf_op jit(solution)/shard_map/ppermute | solution.py:10
  67.8 7.7 %collective-permute-start.2 = (bf16[128,800]{0,1:T(8,128)(2,1)S(1)}, bf16[128,800]{0,1:T(8,128)(2,1)S(1)}, u32[]{:S(2)}, u32[]{:S(2)}) collective-permute-start(bf16[128,800]{0,1:T(8,128)(2,1)S(1)} %collective-permute-done.1), channel_id=1, source_target_pairs={{3,0},{0,1},{1,2},{2,3},{7,4},{4,5},{5,6},{6,7},{11,8},{8,9},{9,10... | collective-permute-start | bytes 614408 | tf_op jit(solution)/shard_map/ppermute | solution.py:10
  78.5 202.6 %copy-start.1 = (bf16[1,3200]{1,0:T(2,128)(2,1)S(1)}, bf16[1,3200]{1,0:T(2,128)(2,1)}, u32[]{:S(2)}) copy-start(bf16[1,3200]{1,0:T(2,128)(2,1)} %param.9) | copy-start | bytes 19204
Sparse Core Ops, SparseCore 0:
  78.7 192.2 all-reduce.2
where the time goes:
time: 291 us; the launch traced here: 289 us
  waiting for transfers between devices  221 us (76%)
  starting transfers between devices  25.6 us (9%)
  between operations  14.3 us (5%)
  local copies, waits for them, and re-layouts  9.4 us (3%)
  blocking collectives  7.97 us (3%)
  other arithmetic  6.5 us (2%)
  matrix products  3.79 us (1%)
    unnamed x2, waiting for transfers between devices  191 us
    all_to_all x1, starting transfers between devices, per_device(): lax.all_to_all(kept_amp, 'pair', split_axis=1, concat_axis=0, tiled=True)  18.4 us
    ppermute x3, waiting for transfers between devices, passed_along(): return lax.ppermute(block, axis, route)  15.6 us
    all_to_all x1, waiting for transfers between devices, per_device(): lax.all_to_all(kept_amp, 'pair', split_axis=1, concat_axis=0, tiled=True)  14.4 us
    all_to_all x1, blocking collectives, per_device(): lax.all_to_all(by_group, 'blk', split_axis=0, concat_axis=2, tiled=True)  7.97 us
    ppermute x3, starting transfers between devices, passed_along(): return lax.ppermute(block, axis, route)  7.12 us
  transfers between devices with their start and end apart: 5, of which 5 were waited for; matrix products, arithmetic and copies ran while one was open for 2% of the time, Pallas kernels for 0%

commit v1 on v0

v1 whole, which is shorter than its diff:
```python
import jax
import jax.numpy as jnp
from jax import lax
from jax.sharding import Mesh
from jax.sharding import PartitionSpec as P

AXES = ("z", "y", "core", "x1", "x0")
SCALE = 64.0


def per_device(amplitudes, integrals, residual_in, pair_irrep, slab_irrep, upper_irrep, virt_irrep):
    bf16, f32, f16 = jnp.bfloat16, jnp.float32, jnp.float16
    nv = virt_irrep.shape[0]
    core = lax.axis_index("core")
    x1 = lax.axis_index("x1")
    x0 = lax.axis_index("x0")
    x = 2 * x1 + x0
    slab = lax.axis_index(("z", "y", "core"))
    zy = lax.axis_size("z") * lax.axis_size("y")

    partner_v = lax.ppermute(integrals, ("x1", "x0"), [(0, 3), (3, 0), (1, 2), (2, 1)])

    chunks = amplitudes.reshape(zy, 2, nv).swapaxes(0, 1).reshape(2 * zy, nv)
    mine = lax.all_to_all(chunks, ("core", "z", "y"), 0, 0, tiled=True)
    other = lax.ppermute(mine, "x0", [(0, 1), (1, 0)])

    rows = jnp.stack([mine, other]).reshape(2, 2, zy, nv)
    keep_rows = lax.dynamic_index_in_dim(rows, core, 1, keepdims=False).reshape(2 * zy, nv)
    send_rows = lax.dynamic_index_in_dim(rows, 1 - core, 1, keepdims=False).reshape(2 * zy, nv)

    cd_irrep = jnp.bitwise_xor(lax.dynamic_index_in_dim(slab_irrep, slab, 0), virt_irrep)
    zero = jnp.zeros((), bf16)

    def kept(block, a):
        ab = jnp.bitwise_xor(lax.dynamic_index_in_dim(upper_irrep, a, 0), virt_irrep)
        return jnp.where(cd_irrep[:, None] == ab[None, :], block, zero)

    v = jnp.concatenate([kept(integrals, x), kept(partner_v, 3 - x)], axis=1)
    send = jnp.dot(send_rows, v, preferred_element_type=f32)
    got = lax.ppermute(send, "core", [(0, 1), (1, 0)])
    keep = jnp.dot(keep_rows, v, preferred_element_type=f32)
    part = ((keep + got) * SCALE).astype(f16).reshape(2, zy, 2 * nv)
    part = jnp.where(x0 == 0, part, part[::-1])
    back = lax.all_to_all(part.reshape(2 * zy, 2 * nv), ("x0", "z", "y"), 0, 0, tiled=True)
    sums = jnp.sum(back.reshape(2, zy, 2, nv).astype(f32), axis=1) * (1.0 / SCALE)
    order = jnp.stack([sums[0, 0], sums[1, 0], sums[1, 1], sums[0, 1]])
    ladder = jnp.where(x1 == 0, order, jnp.roll(order, 2, axis=0))
    ab_irrep = jnp.bitwise_xor(upper_irrep[:, None], virt_irrep[None, :])
    ladder = jnp.where(ab_irrep == pair_irrep[0], ladder, 0.0).reshape(1, -1)
    return (residual_in.astype(f32) + ladder).astype(bf16)


def solution(mesh):
    fine = Mesh(mesh.devices.reshape(8, 8, 2, 2, 2), AXES)
    return jax.shard_map(
        per_device,
        mesh=fine,
        in_specs=(P(AXES, None), P(AXES[:3], AXES[3:]), P(AXES, None), P(AXES), P(), P(), P()),
        out_specs=P(AXES, None),
        check_vma=False,
    )
```

time: 291 us -> 102 us (0.35)
  waiting for transfers between devices: 221 us -> 37.6 us
  between operations: 14.3 us -> 0.97 us
  starting transfers between devices: 25.6 us -> 35.6 us
  blocking collectives: 7.97 us -> 0 us
  other arithmetic: 6.5 us -> 11.3 us
    unnamed x2 -> x0, waiting for transfers between devices: 191 us -> none
    all_to_all x1 -> x2, waiting for transfers between devices: 14.4 us -> 32.3 us  [the longest x1 18 us: per_device(): lax.all_to_all(part.reshape(2 * zy, 2 * nv), ('x0', 'z', 'y'), 0, 0, tile...]
    ppermute x3, waiting for transfers between devices: 15.6 us -> 5.31 us  [the longest x1 3.38 us: per_device(): other = lax.ppermute(mine, 'x0', [(0, 1), (1, 0)])]
    all_to_all x1 -> x0, blocking collectives: 7.97 us -> none  [per_device(): lax.all_to_all(by_group, 'blk', split_axis=0, concat_axis=2, tiled=True)]
    all_to_all x1 -> x2, starting transfers between devices: 18.4 us -> 24.5 us  [the longest x1 18.2 us: per_device(): mine = lax.all_to_all(chunks, ('core', 'z', 'y'), 0, 0, tiled=True)]
    ppermute x3, starting transfers between devices: 7.12 us -> 11.1 us  [the longest x1 5.34 us: per_device(): lax.ppermute(integrals, ('x1', 'x0'), [(0, 3), (3, 0), (1, 2), (2, 1)])]
  transfers between devices with their start and end apart: 5 -> 5, of which waited for: 5 -> 4; matrix products, arithmetic and copies ran while one was open for 2% -> 11% of each run, Pallas kernels for 0% -> 0%
where the time goes in v1:
time: 102 us; the launch traced here: 101 us
  waiting for transfers between devices  37.6 us (37%)
  starting transfers between devices  35.6 us (35%)
  other arithmetic  11.3 us (11%)
  local copies, waits for them, and re-layouts  9.57 us (9%)
  matrix products  5.76 us (6%)
    all_to_all x1, starting transfers between devices, per_device(): mine = lax.all_to_all(chunks, ('core', 'z', 'y'), 0, 0, tiled=True)  18.2 us
    all_to_all x1, waiting for transfers between devices, per_device(): lax.all_to_all(part.reshape(2 * zy, 2 * nv), ('x0', 'z', 'y'), 0, 0, tile...  18 us
    all_to_all x1, waiting for transfers between devices, per_device(): mine = lax.all_to_all(chunks, ('core', 'z', 'y'), 0, 0, tiled=True)  14.3 us
    all_to_all x1, starting transfers between devices, per_device(): lax.all_to_all(part.reshape(2 * zy, 2 * nv), ('x0', 'z', 'y'), 0, 0, tile...  6.35 us
    ppermute x1, starting transfers between devices, per_device(): lax.ppermute(integrals, ('x1', 'x0'), [(0, 3), (3, 0), (1, 2), (2, 1)])  5.34 us
    ppermute x1, starting transfers between devices, per_device(): got = lax.ppermute(send, 'core', [(0, 1), (1, 0)])  3.82 us
    dot_general x1, matrix products, per_device(): keep = jnp.dot(keep_rows, v, preferred_element_type=f32)  3.77 us
    unnamed x23, local copies, waits for them, and re-layouts  3.55 us
  transfers between devices with their start and end apart: 5, of which 4 were waited for; matrix products, arithmetic and copies ran while one was open for 11% of the time, Pallas kernels for 0%

profile of v1, /device:TPU:1, one launch (start us, length us, event | category | flops | bytes accessed | tf_op | source)
XLA Modules:
  0.0 100.8 jit_solution(9125525264999956861)
XLA Ops:
  0.0 5.3 %collective-permute-start.1 = (bf16[800,800]{1,0:T(8,128)(2,1)}, bf16[800,800]{1,0:T(8,128)(2,1)S(1)}, u32[]{:S(2)}, u32[]{:S(2)}) collective-permute-start(bf16[800,800]{1,0:T(8,128)(2,1)} %param.8), channel_id=1, source_target_pairs={{0,3},{3,0},{1,2},{2,1},{4,7},{7,4},{5,6},{6,5},{8,11},{11,8},{9,1... | collective-permute-start | bytes 3840008 | tf_op jit(solution)/shard_map/ppermute | solution.py:21
  5.4 2.1 %reduce = bf16[102400]{0:T(1024)(128)(2,1)S(1)} reduce(bf16[1,102400]{1,0:T(2,128)(2,1)} %param.7, bf16[]{:T(256)} %constant.62), dimensions={0}, to_apply=%param.7.reduce_sub_computation | reduce | bytes 409602 | tf_op args[0]
  7.5 0.3 reshape.89
  7.9 0.5 broadcast.38
  8.4 0.7 reduce.3
  9.1 1.0 reshape.96
  10.1 18.2 %all-to-all-start = ((bf16[128,2,400]{2,1,0:T(2,128)(2,1)}), bf16[128,2,400]{2,1,0:T(2,128)(2,1)S(1)}, u32[]{:S(2)}, u32[]{:S(2)}) async-start(bf16[128,2,400]{2,1,0:T(2,128)(2,1)} %reshape.96), calls=%async_computation | async-start | bytes 524288 | tf_op jit(solution)/shard_map/all_to_all | solution.py:24
  28.3 0.0 copy-done.8
  28.3 0.7 dynamic_slice.19
  29.0 0.0 copy-done.6
  29.0 0.6 fusion.8
  29.6 14.3 %all-to-all-done = bf16[128,2,400]{2,1,0:T(2,128)(2,1)S(1)} async-done(((bf16[128,2,400]{2,1,0:T(2,128)(2,1)}), bf16[128,2,400]{2,1,0:T(2,128)(2,1)S(1)}, u32[]{:S(2)}, u32[]{:S(2)}) %all-to-all-start) | async-done | bytes 204832 | tf_op jit(solution)/shard_map/all_to_all | solution.py:24
  43.9 0.5 reshape.97
  44.4 0.0 copy-start
  44.4 1.1 %copy.14 = bf16[128,1,800]{0,2,1:T(8,128)(2,1)} copy(bf16[128,1,800]{2,1,0:T(2,128)(2,1)S(1)} %reshape.97) | data formatting | bytes 409600 | tf_op jit(solution)/shard_map/all_to_all | solution.py:24
  45.5 1.9 %collective-permute-start = (bf16[128,800]{0,1:T(8,128)(2,1)}, bf16[128,800]{0,1:T(8,128)(2,1)}, u32[]{:S(2)}, u32[]{:S(2)}) collective-permute-start(bf16[128,800]{0,1:T(8,128)(2,1)} %bitcast.3), channel_id=1, source_target_pairs={{0,1},{1,0},{2,3},{3,2},{4,5},{5,4},{6,7},{7,6},{8,9},{9,8},{10,11... | collective-permute-start | bytes 614408 | tf_op jit(solution)/shard_map/ppermute | solution.py:25
  47.4 0.0 copy-done.3
  47.4 2.4 %broadcast_xor_fusion.1 = (s32[800]{0:T(1024)}, s32[800]{0:T(1024)}, s32[800]{0:T(1024)}) fusion(s32[800]{0:T(1024)S(1)} %copy-done.3, s32[]{:T(128)} %bitcast.7, s32[]{:T(128)} %bitcast.6, s32[]{:T(128)} %bitcast.8), kind=kLoop, calls=%fused_computation.25 | loop fusion | flops 2400 | bytes 12812 | tf_op jit(solution)/shard_map/xor | solution.py:35
  49.9 3.4 %collective-permute-done = bf16[128,800]{0,1:T(8,128)(2,1)} collective-permute-done((bf16[128,800]{0,1:T(8,128)(2,1)}, bf16[128,800]{0,1:T(8,128)(2,1)}, u32[]{:S(2)}, u32[]{:S(2)}) %collective-permute-start) | collective-permute-done | bytes 204832 | tf_op jit(solution)/shard_map/ppermute | solution.py:25
  53.3 1.1 %copy.15 = bf16[128,800]{1,0:T(8,128)(2,1)S(1)} copy(bf16[128,800]{0,1:T(8,128)(2,1)} %collective-permute-done) | data formatting | bytes 409600 | tf_op jit(solution)/shard_map/ppermute | solution.py:25
  54.4 0.1 fusion.4
  54.4 0.0 collective-permute-done.1
  54.4 0.0 copy-done
  54.5 1.6 %compare_select_fusion.1 = (bf16[800,800]{1,0:T(8,128)(2,1)S(1)}, bf16[800,800]{1,0:T(8,128)(2,1)S(1)}) fusion(bf16[800,800]{1,0:T(8,128)(2,1)S(1)} %copy-done, s32[800]{0:T(1024)} %get-tuple-element.13, s32[800]{0:T(1024)} %get-tuple-element.14, bf16[800,800]{1,0:T(8,128)(2,1)S(1)} %collective-permute-done.1, s32[800]{0:T(1024)} %get-tuple-element.15), kind=kLoop, calls=%fused_computation.1 | loop fusion | flops 2560000 | bytes 5129600 | tf_op jit(solution)/shard_map/jit(_where)/select_n | solution.py:36
  56.0 0.0 copy-start.1
  56.1 0.0 copy-start.2
  56.1 2.0 %fusion.2 = f32[128,1600]{0,1:T(8,128)S(1)} fusion(bf16[128,800]{1,0:T(8,128)(2,1)S(1)} %bitcast.31, bf16[800,800]{1,0:T(8,128)(2,1)S(1)} %get-tuple-element.12, bf16[800,800]{1,0:T(8,128)(2,1)S(1)} %get-tuple-element.11), kind=kOutput, calls=%fused_computation.6 | convolution fusion | flops 332800000 | bytes 3584000 | tf_op jit(solution)/shard_map/dot_general | solution.py:39
  58.1 0.0 copy-done.1
  58.1 3.8 %collective-permute-start.2 = (f32[128,1600]{0,1:T(8,128)S(1)}, f32[128,1600]{0,1:T(8,128)S(1)}, u32[]{:S(2)}, u32[]{:S(2)}) collective-permute-start(f32[128,1600]{0,1:T(8,128)S(1)} %fusion.2), channel_id=1, source_target_pairs={{0,4},{4,0},{1,5},{5,1},{2,6},{6,2},{3,7},{7,3},{8,12},{12,8},{9,1... | collective-permute-start | bytes 2457608 | tf_op jit(solution)/shard_map/ppermute | solution.py:40
  61.9 1.9 %collective-permute-done.2 = f32[128,1600]{0,1:T(8,128)S(1)} collective-permute-done((f32[128,1600]{0,1:T(8,128)S(1)}, f32[128,1600]{0,1:T(8,128)S(1)}, u32[]{:S(2)}, u32[]{:S(2)}) %collective-permute-start.2) | collective-permute-done | bytes 819232 | tf_op jit(solution)/shard_map/ppermute | solution.py:40
  63.9 3.8 %fusion.1 = f16[128,1600]{0,1:T(8,128)(2,1)S(1)} fusion(f32[128,1600]{0,1:T(8,128)S(1)} %collective-permute-done.2, bf16[128,800]{1,0:T(8,128)(2,1)S(1)} %bitcast.30, bf16[800,800]{1,0:T(8,128)(2,1)} %copy-done.2, bf16[800,800]{1,0:T(8,128)(2,1)} %copy-done.1), kind=kOutput, calls=%fused_computation.5 | convolution fusion | flops 333414400 | bytes 3993600 | tf_op jit(solution)/shard_map/dot_general | solution.py:41
  67.6 0.4 copy.16
  68.0 0.1 reverse_select_fusion
  68.1 0.5 broadcast.39
  68.7 0.8 reduce.4
  69.5 1.3 %reshape.98 = f16[128,2,800]{2,1,0:T(2,128)(2,1)} reshape(f16[128,1600]{1,0:T(8,128)(2,1)S(1)} %reduce.4) | data formatting | bytes 819200
  70.8 6.4 %all-to-all-start.1 = ((f16[128,2,800]{2,1,0:T(2,128)(2,1)}), f16[128,2,800]{2,1,0:T(2,128)(2,1)S(1)}, u32[]{:S(2)}, u32[]{:S(2)}) async-start(f16[128,2,800]{2,1,0:T(2,128)(2,1)} %reshape.98), calls=%async_computation.1 | async-start | bytes 917504 | tf_op jit(solution)/shard_map/all_to_all | solution.py:44
  77.8 18.0 %all-to-all-done.1 = f16[128,2,800]{2,1,0:T(2,128)(2,1)S(1)} async-done(((f16[128,2,800]{2,1,0:T(2,128)(2,1)}), f16[128,2,800]{2,1,0:T(2,128)(2,1)S(1)}, u32[]{:S(2)}, u32[]{:S(2)}) %all-to-all-start.1) | async-done | bytes 409632 | tf_op jit(solution)/shard_map/all_to_all | solution.py:44
  95.7 0.7 reshape.99
  96.5 2.5 %convert_reduce_fusion = f32[128,1600]{1,0:T(8,128)S(1)} fusion(f16[128,1,1600]{2,1,0:T(2,128)(2,1)S(1)} %reshape.99), kind=kLoop, calls=%fused_computation.7 | loop fusion | flops 204800 | bytes 1228800 | tf_op jit(solution)/shard_map/convert_element_type | solution.py:45
  98.9 0.0 copy-start.4
  98.9 0.0 copy-start.7
  98.9 0.0 copy-start.5
  99.0 0.7 reshape.93
  99.6 0.3 reduce_sum.9
  100.0 0.1 fusion.5
  100.1 0.1 select_n.75
  100.2 0.6 add_convert_fusion
  (11 shorter events, 0.1 us)
Async XLA Ops:
  0.0 28.3 %copy-start.8 = (s32[128]{0:T(128)S(1)}, s32[128]{0:T(128)}, u32[]{:S(2)}) copy-start(s32[128]{0:T(128)} %param.11) | copy-start | bytes 1540
  0.0 29.0 %copy-start.6 = (s32[4]{0:T(128)S(1)}, s32[4]{0:T(128)}, u32[]{:S(2)}) copy-start(s32[4]{0:T(128)} %param.12) | copy-start | bytes 52
  0.0 54.4 %collective-permute-start.1 = (bf16[800,800]{1,0:T(8,128)(2,1)}, bf16[800,800]{1,0:T(8,128)(2,1)S(1)}, u32[]{:S(2)}, u32[]{:S(2)}) collective-permute-start(bf16[800,800]{1,0:T(8,128)(2,1)} %param.8), channel_id=1, source_target_pairs={{0,3},{3,0},{1,2},{2,1},{4,7},{7,4},{5,6},{6,5},{8,11},{11,8},{9,1... | collective-permute-start | bytes 3840008 | tf_op jit(solution)/shard_map/ppermute | solution.py:21
  8.4 39.0 %copy-start.3 = (s32[800]{0:T(1024)S(1)}, s32[800]{0:T(1024)}, u32[]{:S(2)}) copy-start(s32[800]{0:T(1024)} %param.13) | copy-start | bytes 9604
  10.1 33.8 %all-to-all-start = ((bf16[128,2,400]{2,1,0:T(2,128)(2,1)}), bf16[128,2,400]{2,1,0:T(2,128)(2,1)S(1)}, u32[]{:S(2)}, u32[]{:S(2)}) async-start(bf16[128,2,400]{2,1,0:T(2,128)(2,1)} %reshape.96), calls=%async_computation | async-start | bytes 524288 | tf_op jit(solution)/shard_map/all_to_all | solution.py:24
  44.4 10.1 %copy-start = (bf16[800,800]{1,0:T(8,128)(2,1)S(1)}, bf16[800,800]{1,0:T(8,128)(2,1)}, u32[]{:S(2)}) copy-start(bf16[800,800]{1,0:T(8,128)(2,1)} %param.8) | copy-start | bytes 3840004
  45.5 7.8 %collective-permute-start = (bf16[128,800]{0,1:T(8,128)(2,1)}, bf16[128,800]{0,1:T(8,128)(2,1)}, u32[]{:S(2)}, u32[]{:S(2)}) collective-permute-start(bf16[128,800]{0,1:T(8,128)(2,1)} %bitcast.3), channel_id=1, source_target_pairs={{0,1},{1,0},{2,3},{3,2},{4,5},{5,4},{6,7},{7,6},{8,9},{9,8},{10,11... | collective-permute-start | bytes 614408 | tf_op jit(solution)/shard_map/ppermute | solution.py:25
  56.0 2.0 %copy-start.1 = (bf16[800,800]{1,0:T(8,128)(2,1)}, bf16[800,800]{1,0:T(8,128)(2,1)S(1)}, u32[]{:S(2)}) copy-start(bf16[800,800]{1,0:T(8,128)(2,1)S(1)} %get-tuple-element.11) | copy-start | bytes 3840004
  56.1 2.0 %copy-start.2 = (bf16[800,800]{1,0:T(8,128)(2,1)}, bf16[800,800]{1,0:T(8,128)(2,1)S(1)}, u32[]{:S(2)}) copy-start(bf16[800,800]{1,0:T(8,128)(2,1)S(1)} %get-tuple-element.12) | copy-start | bytes 3840004
  58.1 5.8 %collective-permute-start.2 = (f32[128,1600]{0,1:T(8,128)S(1)}, f32[128,1600]{0,1:T(8,128)S(1)}, u32[]{:S(2)}, u32[]{:S(2)}) collective-permute-start(f32[128,1600]{0,1:T(8,128)S(1)} %fusion.2), channel_id=1, source_target_pairs={{0,4},{4,0},{1,5},{5,1},{2,6},{6,2},{3,7},{7,3},{8,12},{12,8},{9,1... | collective-permute-start | bytes 2457608 | tf_op jit(solution)/shard_map/ppermute | solution.py:40
  70.8 25.0 %all-to-all-start.1 = ((f16[128,2,800]{2,1,0:T(2,128)(2,1)}), f16[128,2,800]{2,1,0:T(2,128)(2,1)S(1)}, u32[]{:S(2)}, u32[]{:S(2)}) async-start(f16[128,2,800]{2,1,0:T(2,128)(2,1)} %reshape.98), calls=%async_computation.1 | async-start | bytes 917504 | tf_op jit(solution)/shard_map/all_to_all | solution.py:44
  98.9 1.1 %copy-start.4 = (s32[800]{0:T(1024)S(1)}, s32[800]{0:T(1024)}, u32[]{:S(2)}) copy-start(s32[800]{0:T(1024)} %param.13) | copy-start | bytes 9604
  98.9 1.1 %copy-start.7 = (s32[4]{0:T(128)S(1)}, s32[4]{0:T(128)}, u32[]{:S(2)}) copy-start(s32[4]{0:T(128)} %param.12) | copy-start | bytes 52
  98.9 1.3 %copy-start.5 = (bf16[1,3200]{1,0:T(2,128)(2,1)S(1)}, bf16[1,3200]{1,0:T(2,128)(2,1)}, u32[]{:S(2)}) copy-start(bf16[1,3200]{1,0:T(2,128)(2,1)} %param.9) | copy-start | bytes 19204

commit v2 on v1

v2 whole, which is shorter than its diff:
```python
import functools

import jax
import jax.numpy as jnp
from jax import lax
from jax.experimental import pallas as pl
from jax.experimental.pallas import tpu as pltpu
from jax.sharding import Mesh
from jax.sharding import PartitionSpec as P

AXES = ("z", "y", "core", "x1", "x0")
BF16, F32, F16 = jnp.bfloat16, jnp.float32, jnp.float16
NV = 800
LANES = 128
TILES = 7
WIDE = TILES * LANES
SCALE = 64.0

VMEM = pl.BlockSpec(memory_space=pltpu.VMEM)
SMEM = pl.BlockSpec(memory_space=pltpu.SMEM)


def call(body, out, ins, flops, nbytes, scratch=()):
    return pl.pallas_call(
        body,
        out_shape=out,
        in_specs=[SMEM if kind == "s" else VMEM for kind in ins],
        out_specs=VMEM,
        scratch_shapes=list(scratch),
        compiler_params=pltpu.CompilerParams(vmem_limit_bytes=32 * 1024 * 1024),
        cost_estimate=pl.CostEstimate(flops=flops, bytes_accessed=nbytes, transcendentals=0),
    )


def cut_body(row_ref, out_ref):
    filler = jnp.zeros((1, LANES), F32)

    def four(q, carry):
        for r in range(4):
            at = [pl.multiple_of(q * 3200 + (6 * r + t) * LANES, LANES) for t in range(TILES)]
            tiles = [row_ref[:, pl.ds(a, LANES)].astype(F32) for a in at]
            out_ref[r % 2, 2 * q + r // 2] = jnp.concatenate(tiles + [filler], axis=0).astype(BF16)
        return carry

    lax.fori_loop(0, 32, four, 0, unroll=4)


def kept_body(scalars_ref, virt_ref, block_ref, out_ref):
    slab, upper, shift = scalars_ref[0], scalars_ref[1], scalars_ref[2]
    label = lax.broadcasted_iota(jnp.int32, (16, NV), 0)
    virt = virt_ref[...]
    rows = jnp.where(label == jnp.bitwise_xor(virt, slab), 1.0, 0.0).astype(BF16)
    columns = jnp.where(label == jnp.bitwise_xor(virt, upper), 1.0, 0.0).astype(BF16)
    same = lax.dot_general(rows, columns, (((0,), (0,)), ((), ())), preferred_element_type=F32)
    out_ref[...] = jnp.zeros_like(out_ref)
    kept = jnp.where(same > 0.5, block_ref[...].astype(F32), 0.0).astype(BF16)
    out_ref[pl.ds(pl.multiple_of(shift, 32), NV), 0:NV] = kept


def ladder_body(flip, zy, scalars_ref, mine_ref, other_ref, own_ref, partner_ref, out_ref, rows, lhs):
    core, x0 = scalars_ref[0], scalars_ref[1]
    pick = 1 - core if flip else core
    first = pl.multiple_of(pick * (zy * 8), zy * 8)
    for block, source in ((0, mine_ref), (1, other_ref)):
        rows[...] = source[pl.ds(first, zy * 8), :].astype(F32)
        place = x0 if block == 0 else 1 - x0
        for t in range(TILES):
            lhs[pl.ds(pl.multiple_of(place * zy, zy), zy), t * LANES : (t + 1) * LANES] = rows[
                pl.ds(t, zy, stride=8), :
            ].astype(BF16)
    for half, v_ref in ((0, own_ref), (1, partner_ref)):
        sums = jnp.dot(lhs[...], v_ref[...], preferred_element_type=F32)
        for t in range(TILES):
            out_ref[pl.ds(8 * half + t, 2 * zy, stride=16), :] = sums[:, t * LANES : (t + 1) * LANES]
        out_ref[pl.ds(8 * half + TILES, 2 * zy, stride=16), :] = jnp.zeros((2 * zy, LANES), F32)


def finish_body(scalars_ref, sums_ref, virt_ref, old_ref, out_ref):
    swap = scalars_ref[0] == 1
    pair = scalars_ref[1]
    order = ((0, 0), (1, 0), (1, 1), (0, 1))
    virt = virt_ref[...]
    for a in range(4):
        s, h = order[a]
        s2, h2 = order[(a + 2) % 4]
        straight = sums_ref[s, 8 * h : 8 * h + 8, :]
        turned = sums_ref[s2, 8 * h2 : 8 * h2 + 8, :]
        tiles = jnp.where(swap, turned, straight) * (1.0 / SCALE)
        row = jnp.concatenate([tiles[t : t + 1, :] for t in range(TILES)], axis=1)[:, :NV]
        ab = jnp.bitwise_xor(virt, scalars_ref[2 + a])
        row = jnp.where(ab == pair, row, 0.0)
        old = old_ref[:, a * NV : (a + 1) * NV].astype(F32)
        out_ref[:, a * NV : (a + 1) * NV] = (old + row).astype(BF16)


def per_device(amplitudes, integrals, residual_in, pair_irrep, slab_irrep, upper_irrep, virt_irrep):
    core = lax.axis_index("core")
    x1 = lax.axis_index("x1")
    x0 = lax.axis_index("x0")
    x = 2 * x1 + x0
    slab = lax.axis_index(("z", "y", "core"))
    zy = lax.axis_size("z") * lax.axis_size("y")
    shape = jax.ShapeDtypeStruct
    virt = virt_irrep.reshape(1, NV)

    partner = lax.ppermute(integrals, ("x1", "x0"), [(0, 3), (3, 0), (1, 2), (2, 1)])

    cut = call(cut_body, shape((2, zy, 8, LANES), BF16), "v", 0, 700000)(amplitudes)
    mine = lax.all_to_all(cut.reshape(2 * zy, 8, LANES), ("core", "z", "y"), 0, 0, tiled=True)
    mine = mine.reshape(2 * zy * 8, LANES)
    other = lax.ppermute(mine, "x0", [(0, 1), (1, 0)])

    slab_label = lax.dynamic_index_in_dim(slab_irrep, slab, 0, keepdims=False)
    shift = 32 * (slab % 4)

    def kept(block, a):
        upper = lax.dynamic_index_in_dim(upper_irrep, a, 0, keepdims=False)
        scalars = jnp.stack([slab_label, upper, shift])
        return call(kept_body, shape((WIDE, WIDE), BF16), "svv", 20000000, 3000000)(scalars, virt, block)

    own_v = kept(integrals, x)
    partner_v = kept(partner, 3 - x)

    places = jnp.stack([core, x0])

    def ladder(flip):
        return call(
            functools.partial(ladder_body, flip, zy),
            shape((2 * zy * 16, LANES), F32),
            "svvvv",
            2 * 128 * 1792 * 896,
            5000000,
            [pltpu.VMEM((zy * 8, LANES), F32), pltpu.VMEM((2 * zy, WIDE), BF16)],
        )(places, mine, other, own_v, partner_v)

    got = lax.ppermute(ladder(True), "core", [(0, 1), (1, 0)])
    keep = ladder(False)
    part = ((keep + got) * SCALE).astype(F16).reshape(2 * zy, 16, LANES)
    back = lax.all_to_all(part, ("x0", "z", "y"), 0, 0, tiled=True)
    sums = jnp.sum(back.reshape(2, zy, 16, LANES).astype(F32), axis=1)
    scalars = jnp.concatenate([jnp.stack([x1, pair_irrep[0]]), upper_irrep])
    return call(finish_body, shape((1, 4 * NV), BF16), "svvv", 0, 50000)(scalars, sums, virt, residual_in)


def solution(mesh):
    fine = Mesh(mesh.devices.reshape(8, 8, 2, 2, 2), AXES)
    return jax.shard_map(
        per_device,
        mesh=fine,
        in_specs=(P(AXES, None), P(AXES[:3], AXES[3:]), P(AXES, None), P(AXES), P(), P(), P()),
        out_specs=P(AXES, None),
        check_vma=False,
    )
```

time: 102 us -> 87.6 us (0.86)
  blocking collectives: 0 us -> 33.6 us
  starting transfers between devices: 35.6 us -> 16.4 us
  waiting for transfers between devices: 37.6 us -> 19.9 us
  other arithmetic: 11.3 us -> 3.12 us
  Pallas kernels: 0 us -> 7.41 us
  matrix products: 5.76 us -> 0 us
  local copies, waits for them, and re-layouts: 9.57 us -> 5.68 us
    all_to_all x0 -> x1, blocking collectives: none -> 33.6 us  [per_device(): lax.all_to_all(cut.reshape(2 * zy, 8, LANES), ('core', 'z', 'y'), 0, 0, t...]
    all_to_all x2 -> x1, starting transfers between devices: 24.5 us -> 6.18 us  [per_device(): back = lax.all_to_all(part, ('x0', 'z', 'y'), 0, 0, tiled=True)]
    all_to_all x2 -> x1, waiting for transfers between devices: 32.3 us -> 19.2 us  [per_device(): back = lax.all_to_all(part, ('x0', 'z', 'y'), 0, 0, tiled=True)]
    pallas_call x0 -> x6, Pallas kernels: none -> 7.41 us  [the longest x2 3.08 us: ladder(): call(functools.partial(ladder_body, flip, zy), shape((2 * zy * 16, LANES)...]
    dot_general x2 -> x0, matrix products: 5.76 us -> none  [the longest x1 3.77 us: per_device(): keep = jnp.dot(keep_rows, v, preferred_element_type=f32)]
    ppermute x1, waiting for transfers between devices: 3.38 us -> 0.01 us  [per_device(): other = lax.ppermute(mine, 'x0', [(0, 1), (1, 0)])]
    xor x1 -> x0, other arithmetic: 2.44 us -> none  [kept(): jnp.bitwise_xor(lax.dynamic_index_in_dim(upper_irrep, a, 0), virt_irrep)]
    unnamed x1 -> x0, other arithmetic: 2.13 us -> none
  transfers between devices with their start and end apart: 5 -> 4, of which waited for: 4 -> 2; matrix products, arithmetic and copies ran while one was open for 11% -> 6% of each run, Pallas kernels for 0% -> 5%
where the time goes in v2:
time: 87.6 us; the launch traced here: 86.9 us
  blocking collectives  33.6 us (38%)
  waiting for transfers between devices  19.9 us (23%)
  starting transfers between devices  16.4 us (19%)
  Pallas kernels  7.41 us (8%)
  local copies, waits for them, and re-layouts  5.68 us (6%)
  other arithmetic  3.12 us (4%)
    all_to_all x1, blocking collectives, per_device(): lax.all_to_all(cut.reshape(2 * zy, 8, LANES), ('core', 'z', 'y'), 0, 0, t...  33.6 us
    all_to_all x1, waiting for transfers between devices, per_device(): back = lax.all_to_all(part, ('x0', 'z', 'y'), 0, 0, tiled=True)  19.2 us
    all_to_all x1, starting transfers between devices, per_device(): back = lax.all_to_all(part, ('x0', 'z', 'y'), 0, 0, tiled=True)  6.18 us
    ppermute x1, starting transfers between devices, per_device(): lax.ppermute(integrals, ('x1', 'x0'), [(0, 3), (3, 0), (1, 2), (2, 1)])  5.21 us
    ppermute x1, starting transfers between devices, per_device(): got = lax.ppermute(ladder(True), 'core', [(0, 1), (1, 0)])  3.12 us
    pallas_call x2, Pallas kernels, ladder(): call(functools.partial(ladder_body, flip, zy), shape((2 * zy * 16, LANES)...  3.08 us
    unnamed x8, local copies, waits for them, and re-layouts  2.37 us
    pallas_call x2, Pallas kernels, kept(): call(kept_body, shape((WIDE, WIDE), BF16), 'svv', 20000000, 3000000)  2.35 us
  transfers between devices with their start and end apart: 4, of which 2 were waited for; matrix products, arithmetic and copies ran while one was open for 6% of the time, Pallas kernels for 5%

profile of v2, /device:TPU:1, one launch (start us, length us, event | category | flops | bytes accessed | tf_op | source)
XLA Modules:
  0.0 86.9 jit_solution(670457471015156915)
XLA Ops:
  0.0 5.2 %collective-permute-start.1 = (bf16[800,800]{1,0:T(8,128)(2,1)}, bf16[800,800]{1,0:T(8,128)(2,1)S(1)}, u32[]{:S(2)}, u32[]{:S(2)}) collective-permute-start(bf16[800,800]{1,0:T(8,128)(2,1)} %block_ref.1), channel_id=1, source_target_pairs={{0,3},{3,0},{1,2},{2,1},{4,7},{7,4},{5,6},{6,5},{8,11},{11,8},{9,1... | collective-permute-start | bytes 3840008 | tf_op jit(solution)/shard_map/ppermute | solution.py:106
  5.2 0.0 copy-start.1
  5.2 1.0 %copy-done.1 = bf16[1,102400]{1,0:T(2,128)(2,1)S(1)} copy-done((bf16[1,102400]{1,0:T(2,128)(2,1)S(1)}, bf16[1,102400]{1,0:T(2,128)(2,1)}, u32[]{:S(2)}) %copy-start.1) | copy-done | bytes 204824
  6.2 0.7 shard_map.73
  7.0 33.6 %all_to_all.10 = bf16[128,8,128]{2,1,0:T(8,128)(2,1)S(1)} all-to-all(bf16[128,8,128]{2,1,0:T(8,128)(2,1)S(1)} %bitcast.13), channel_id=1, replica_groups=mesh['z'=8,'y'=8,'core'=2,'x1'=2,'x0'=2] {'core','z','y'}, dimensions={0} | all-to-all | bytes 524288 | tf_op jit(solution)/shard_map/all_to_all | solution.py:109
  40.6 1.9 %collective-permute-start = (bf16[1024,128]{1,0:T(8,128)(2,1)S(1)}, bf16[1024,128]{1,0:T(8,128)(2,1)S(1)}, u32[]{:S(2)}, u32[]{:S(2)}) collective-permute-start(bf16[1024,128]{1,0:T(8,128)(2,1)S(1)} %bitcast.10), channel_id=1, source_target_pairs={{0,1},{1,0},{2,3},{3,2},{4,5},{5,4},{6,7},{7,6},{8,9},{9,8},{10,11... | collective-permute-start | bytes 786440 | tf_op jit(solution)/shard_map/ppermute | solution.py:111
  42.5 0.7 reshape.17.virt_ref
  43.2 1.2 %dynamic_slice.11 = s32[1]{0:T(128)} dynamic-slice(s32[128]{0:T(128)} %param.11, s32[]{:T(128)S(6)} %select_n.18), dynamic_slice_sizes={1} | dynamic-slice | bytes 12 | tf_op jit(solution)/shard_map/jit(dynamic_index_in_dim)/dynamic_slice | solution.py:113
  44.4 1.4 %fusion = (s32[1]{0:T(128)}, s32[1]{0:T(128)}) fusion(s32[4]{0:T(128)} %param.12, s32[]{:T(128)S(6)} %select_n.21, s32[]{:T(128)S(6)} %select_n.19), kind=kLoop, calls=%fused_computation.6 | loop fusion | bytes 24 | tf_op jit(solution)/shard_map/jit(dynamic_index_in_dim)/dynamic_slice | solution.py:117
  45.8 1.9 %add_add_fusion = (s32[3]{0:T(128)S(1)}, s32[3]{0:T(128)S(1)}) fusion(s32[1]{0:T(128)} %get-tuple-element.6, s32[1]{0:T(128)} %bitcast.5, s32[1]{0:T(128)} %dynamic_slice.11, s32[1]{0:T(128)} %get-tuple-element.5), kind=kLoop, calls=%fused_computation.4 | loop fusion | flops 12 | bytes 40 | tf_op jit(solution)/shard_map/stack | solution.py:118
  47.7 0.0 copy-start
  47.7 1.4 %copy-done = bf16[800,800]{1,0:T(8,128)(2,1)S(1)} copy-done((bf16[800,800]{1,0:T(8,128)(2,1)S(1)}, bf16[800,800]{1,0:T(8,128)(2,1)}, u32[]{:S(2)}) %copy-start) | copy-done | bytes 1280024
  49.1 1.2 %shard_map.74.own_ref = bf16[896,896]{1,0:T(8,128)(2,1)S(1)} custom-call(s32[3]{0:T(128)S(1)} %get-tuple-element.7.scalars_ref, s32[1,800]{1,0:T(1,128)S(1)} %reshape.17.virt_ref, bf16[800,800]{1,0:T(8,128)(2,1)S(1)} %copy-done), custom_call_target="tpu_custom_call" | custom-call | flops 20000000 | bytes 3000000 | tf_op jit(solution)/shard_map/pallas_call | solution.py:119
  50.2 0.1 pad_add_fusion.1.scalars_ref
  50.3 0.0 collective-permute-done.1.block_ref
  50.3 1.2 %shard_map.75.partner_ref = bf16[896,896]{1,0:T(8,128)(2,1)S(1)} custom-call(s32[3]{0:T(128)S(1)} %get-tuple-element.8.scalars_ref, s32[1,800]{1,0:T(1,128)S(1)} %reshape.17.virt_ref, bf16[800,800]{1,0:T(8,128)(2,1)S(1)} %collective-permute-done.1.block_ref), custom_call_target="tpu_custom_call" | custom-call | flops 20000000 | bytes 3000000 | tf_op jit(solution)/shard_map/pallas_call | solution.py:119
  51.5 0.0 collective-permute-done.other_ref
  51.5 1.5 %shard_map.77 = f32[2048,128]{1,0:T(8,128)S(1)} custom-call(s32[2]{0:T(128)S(1)} %pad_add_fusion.1.scalars_ref, bf16[1024,128]{1,0:T(8,128)(2,1)S(1)} %bitcast.11, bf16[1024,128]{1,0:T(8,128)(2,1)S(1)} %collective-permute-done.other_ref, bf16[896,896]{1,0:T(8,128)(2,1)S(1)} %shard_map.74.own_ref, bf16[896,896]{1,0:T(8,128)(2,1)S(1)} %shard_map.75.partner_ref), custom_call_target="tpu_custom_call" | custom-call | flops 411041792 | bytes 5000000 | tf_op jit(solution)/shard_map/pallas_call | solution.py:127
  53.1 3.1 %collective-permute-start.2 = (f32[2048,128]{1,0:T(8,128)S(1)}, f32[2048,128]{1,0:T(8,128)S(1)}, u32[]{:S(2)}, u32[]{:S(2)}) collective-permute-start(f32[2048,128]{1,0:T(8,128)S(1)} %shard_map.77), channel_id=1, source_target_pairs={{0,4},{4,0},{1,5},{5,1},{2,6},{6,2},{3,7},{7,3},{8,12},{12,8},{9,1... | collective-permute-start | bytes 3145736 | tf_op jit(solution)/shard_map/ppermute | solution.py:136
  56.2 1.5 %shard_map.76 = f32[2048,128]{1,0:T(8,128)S(1)} custom-call(s32[2]{0:T(128)S(1)} %pad_add_fusion.1.scalars_ref, bf16[1024,128]{1,0:T(8,128)(2,1)S(1)} %bitcast.12, bf16[1024,128]{1,0:T(8,128)(2,1)S(1)} %collective-permute-done.other_ref, bf16[896,896]{1,0:T(8,128)(2,1)S(1)} %shard_map.74.own_ref, bf16[896,896]{1,0:T(8,128)(2,1)S(1)} %shard_map.75.partner_ref), custom_call_target="tpu_custom_call" | custom-call | flops 411041792 | bytes 5000000 | tf_op jit(solution)/shard_map/pallas_call | solution.py:127
  57.7 0.0 copy-start.3
  57.8 0.0 copy-start.2
  57.8 0.7 collective-permute-done.2
  58.5 1.0 %multiply_convert_fusion = f16[2048,128]{1,0:T(8,128)(2,1)} fusion(f32[2048,128]{1,0:T(8,128)S(1)} %shard_map.76, f32[2048,128]{1,0:T(8,128)S(1)} %collective-permute-done.2), kind=kLoop, calls=%fused_computation.1 | loop fusion | flops 786432 | bytes 2621440 | tf_op jit(solution)/shard_map/convert_element_type | solution.py:138
  59.4 6.2 %all-to-all-start.1 = ((f16[128,16,128]{2,1,0:T(8,128)(2,1)}), f16[128,16,128]{2,1,0:T(8,128)(2,1)S(1)}, u32[]{:S(2)}, u32[]{:S(2)}) async-start(f16[128,16,128]{2,1,0:T(8,128)(2,1)} %bitcast.6), calls=%async_computation.1 | async-start | bytes 1048576 | tf_op jit(solution)/shard_map/all_to_all | solution.py:139
  66.3 0.0 copy-done.3
  66.3 0.1 pad_add_fusion.scalars_ref
  66.4 19.2 %all-to-all-done.1 = f16[128,16,128]{2,1,0:T(8,128)(2,1)S(1)} async-done(((f16[128,16,128]{2,1,0:T(8,128)(2,1)}), f16[128,16,128]{2,1,0:T(8,128)(2,1)S(1)}, u32[]{:S(2)}, u32[]{:S(2)}) %all-to-all-start.1) | async-done | bytes 524320 | tf_op jit(solution)/shard_map/all_to_all | solution.py:139
  85.5 0.1 convert_reduce_fusion.sums_ref
  85.6 0.0 copy-done.2
  85.6 1.3 %shard_map.78 = bf16[1,3200]{1,0:T(2,128)(2,1)} custom-call(s32[6]{0:T(128)S(1)} %pad_add_fusion.scalars_ref, f32[2,16,128]{2,1,0:T(8,128)S(1)} %convert_reduce_fusion.sums_ref, s32[1,800]{1,0:T(1,128)S(1)} %reshape.17.virt_ref, bf16[1,3200]{1,0:T(2,128)(2,1)S(1)} %copy-done.2), custom_call_target="tpu_custom_call" | custom-call | bytes 50000 | tf_op jit(solution)/shard_map/pallas_call | solution.py:142
Async XLA Ops:
  0.0 50.3 %collective-permute-start.1 = (bf16[800,800]{1,0:T(8,128)(2,1)}, bf16[800,800]{1,0:T(8,128)(2,1)S(1)}, u32[]{:S(2)}, u32[]{:S(2)}) collective-permute-start(bf16[800,800]{1,0:T(8,128)(2,1)} %block_ref.1), channel_id=1, source_target_pairs={{0,3},{3,0},{1,2},{2,1},{4,7},{7,4},{5,6},{6,5},{8,11},{11,8},{9,1... | collective-permute-start | bytes 3840008 | tf_op jit(solution)/shard_map/ppermute | solution.py:106
  5.2 1.0 %copy-start.1 = (bf16[1,102400]{1,0:T(2,128)(2,1)S(1)}, bf16[1,102400]{1,0:T(2,128)(2,1)}, u32[]{:S(2)}) copy-start(bf16[1,102400]{1,0:T(2,128)(2,1)} %row_ref.1) | copy-start | bytes 614404
  40.6 10.9 %collective-permute-start = (bf16[1024,128]{1,0:T(8,128)(2,1)S(1)}, bf16[1024,128]{1,0:T(8,128)(2,1)S(1)}, u32[]{:S(2)}, u32[]{:S(2)}) collective-permute-start(bf16[1024,128]{1,0:T(8,128)(2,1)S(1)} %bitcast.10), channel_id=1, source_target_pairs={{0,1},{1,0},{2,3},{3,2},{4,5},{5,4},{6,7},{7,6},{8,9},{9,8},{10,11... | collective-permute-start | bytes 786440 | tf_op jit(solution)/shard_map/ppermute | solution.py:111
  47.7 1.4 %copy-start = (bf16[800,800]{1,0:T(8,128)(2,1)S(1)}, bf16[800,800]{1,0:T(8,128)(2,1)}, u32[]{:S(2)}) copy-start(bf16[800,800]{1,0:T(8,128)(2,1)} %block_ref.1) | copy-start | bytes 3840004
  53.1 5.4 %collective-permute-start.2 = (f32[2048,128]{1,0:T(8,128)S(1)}, f32[2048,128]{1,0:T(8,128)S(1)}, u32[]{:S(2)}, u32[]{:S(2)}) collective-permute-start(f32[2048,128]{1,0:T(8,128)S(1)} %shard_map.77), channel_id=1, source_target_pairs={{0,4},{4,0},{1,5},{5,1},{2,6},{6,2},{3,7},{7,3},{8,12},{12,8},{9,1... | collective-permute-start | bytes 3145736 | tf_op jit(solution)/shard_map/ppermute | solution.py:136
  57.7 8.5 %copy-start.3 = (s32[4]{0:T(128)S(1)}, s32[4]{0:T(128)}, u32[]{:S(2)}) copy-start(s32[4]{0:T(128)} %param.12) | copy-start | bytes 52
  57.8 27.9 %copy-start.2 = (bf16[1,3200]{1,0:T(2,128)(2,1)S(1)}, bf16[1,3200]{1,0:T(2,128)(2,1)}, u32[]{:S(2)}) copy-start(bf16[1,3200]{1,0:T(2,128)(2,1)} %old_ref.1) | copy-start | bytes 19204
  59.4 26.1 %all-to-all-start.1 = ((f16[128,16,128]{2,1,0:T(8,128)(2,1)}), f16[128,16,128]{2,1,0:T(8,128)(2,1)S(1)}, u32[]{:S(2)}, u32[]{:S(2)}) async-start(f16[128,16,128]{2,1,0:T(8,128)(2,1)} %bitcast.6), calls=%async_computation.1 | async-start | bytes 1048576 | tf_op jit(solution)/shard_map/all_to_all | solution.py:139

commit v3 on v2

--- a/solution.py
+++ b/solution.py
@@ -45,10 +45,11 @@
     lax.fori_loop(0, 32, four, 0, unroll=4)
 
 
-def kept_body(scalars_ref, virt_ref, block_ref, out_ref):
-    slab, upper, shift = scalars_ref[0], scalars_ref[1], scalars_ref[2]
+def kept_body(partner, places_ref, slab_ref, upper_ref, virt_ref, block_ref, out_ref):
+    x, c = 2 * places_ref[2] + places_ref[1], places_ref[3]
+    slab, upper, shift = slab_ref[c], upper_ref[3 - x if partner else x], 32 * (c % 4)
     label = lax.broadcasted_iota(jnp.int32, (16, NV), 0)
-    virt = virt_ref[...]
+    virt = virt_ref[...].reshape(1, NV)
     rows = jnp.where(label == jnp.bitwise_xor(virt, slab), 1.0, 0.0).astype(BF16)
     columns = jnp.where(label == jnp.bitwise_xor(virt, upper), 1.0, 0.0).astype(BF16)
     same = lax.dot_general(rows, columns, (((0,), (0,)), ((), ())), preferred_element_type=F32)
@@ -75,11 +76,11 @@
         out_ref[pl.ds(8 * half + TILES, 2 * zy, stride=16), :] = jnp.zeros((2 * zy, LANES), F32)
 
 
-def finish_body(scalars_ref, sums_ref, virt_ref, old_ref, out_ref):
-    swap = scalars_ref[0] == 1
-    pair = scalars_ref[1]
+def finish_body(places_ref, pair_ref, upper_ref, sums_ref, virt_ref, old_ref, out_ref):
+    swap = places_ref[2] == 1
+    pair = pair_ref[0]
     order = ((0, 0), (1, 0), (1, 1), (0, 1))
-    virt = virt_ref[...]
+    virt = virt_ref[...].reshape(1, NV)
     for a in range(4):
         s, h = order[a]
         s2, h2 = order[(a + 2) % 4]
@@ -87,7 +88,7 @@
         turned = sums_ref[s2, 8 * h2 : 8 * h2 + 8, :]
         tiles = jnp.where(swap, turned, straight) * (1.0 / SCALE)
         row = jnp.concatenate([tiles[t : t + 1, :] for t in range(TILES)], axis=1)[:, :NV]
-        ab = jnp.bitwise_xor(virt, scalars_ref[2 + a])
+        ab = jnp.bitwise_xor(virt, upper_ref[a])
         row = jnp.where(ab == pair, row, 0.0)
         old = old_ref[:, a * NV : (a + 1) * NV].astype(F32)
         out_ref[:, a * NV : (a + 1) * NV] = (old + row).astype(BF16)
@@ -97,31 +98,25 @@
     core = lax.axis_index("core")
     x1 = lax.axis_index("x1")
     x0 = lax.axis_index("x0")
-    x = 2 * x1 + x0
     slab = lax.axis_index(("z", "y", "core"))
     zy = lax.axis_size("z") * lax.axis_size("y")
     shape = jax.ShapeDtypeStruct
-    virt = virt_irrep.reshape(1, NV)
+    places = jnp.stack([core, x0, x1, slab])
 
     partner = lax.ppermute(integrals, ("x1", "x0"), [(0, 3), (3, 0), (1, 2), (2, 1)])
 
     cut = call(cut_body, shape((2, zy, 8, LANES), BF16), "v", 0, 700000)(amplitudes)
     mine = lax.all_to_all(cut.reshape(2 * zy, 8, LANES), ("core", "z", "y"), 0, 0, tiled=True)
     mine = mine.reshape(2 * zy * 8, LANES)
+
+    def kept(block, partner):
+        body = functools.partial(kept_body, partner)
+        fill = call(body, shape((WIDE, WIDE), BF16), "sssvv", 20000000, 3000000)
+        return fill(places, slab_irrep, upper_irrep, virt_irrep, block)
+
+    own_v, mine = lax.optimization_barrier((kept(integrals, False), mine))
     other = lax.ppermute(mine, "x0", [(0, 1), (1, 0)])
-
-    slab_label = lax.dynamic_index_in_dim(slab_irrep, slab, 0, keepdims=False)
-    shift = 32 * (slab % 4)
-
-    def kept(block, a):
-        upper = lax.dynamic_index_in_dim(upper_irrep, a, 0, keepdims=False)
-        scalars = jnp.stack([slab_label, upper, shift])
-        return call(kept_body, shape((WIDE, WIDE), BF16), "svv", 20000000, 3000000)(scalars, virt, block)
-
-    own_v = kept(integrals, x)
-    partner_v = kept(partner, 3 - x)
-
-    places = jnp.stack([core, x0])
+    partner_v = kept(partner, True)
 
     def ladder(flip):
         return call(
@@ -138,8 +133,8 @@
     part = ((keep + got) * SCALE).astype(F16).reshape(2 * zy, 16, LANES)
     back = lax.all_to_all(part, ("x0", "z", "y"), 0, 0, tiled=True)
     sums = jnp.sum(back.reshape(2, zy, 16, LANES).astype(F32), axis=1)
-    scalars = jnp.concatenate([jnp.stack([x1, pair_irrep[0]]), upper_irrep])
-    return call(finish_body, shape((1, 4 * NV), BF16), "svvv", 0, 50000)(scalars, sums, virt, residual_in)
+    finish = call(finish_body, shape((1, 4 * NV), BF16), "sssvvv", 0, 50000)
+    return finish(places, pair_irrep, upper_irrep, sums, virt_irrep, residual_in)
 
 
 def solution(mesh):

time: 87.6 us -> 86.9 us (level)
  blocking collectives: 33.6 us -> 0 us
  starting transfers between devices: 16.4 us -> 35.3 us
  waiting for transfers between devices: 19.9 us -> 36.5 us
  other arithmetic: 3.12 us -> 1.14 us
  local copies, waits for them, and re-layouts: 5.68 us -> 4.38 us
    all_to_all x1 -> x0, blocking collectives: 33.6 us -> none  [per_device(): lax.all_to_all(cut.reshape(2 * zy, 8, LANES), ('core', 'z', 'y'), 0, 0, t...]
    all_to_all x0 -> x1, starting transfers between devices: none -> 18.2 us  [per_device(): lax.all_to_all(cut.reshape(2 * zy, 8, LANES), ('core', 'z', 'y'), 0, 0, t...]
    all_to_all x0 -> x1, waiting for transfers between devices: none -> 10.9 us  [per_device(): lax.all_to_all(cut.reshape(2 * zy, 8, LANES), ('core', 'z', 'y'), 0, 0, t...]
    ppermute x1, waiting for transfers between devices: 0.01 us -> 5.53 us  [per_device(): other = lax.ppermute(mine, 'x0', [(0, 1), (1, 0)])]
    dynamic_slice x2 -> x0, local copies, waits for them, and re-layouts: 2.62 us -> none  [the longest x1 1.38 us: kept(): upper = lax.dynamic_index_in_dim(upper_irrep, a, 0, keepdims=False)]
    unnamed x8 -> x18, local copies, waits for them, and re-layouts: 2.37 us -> 4.38 us
    another operation x2 -> x1, other arithmetic: 1.97 us -> 0.08 us  [per_device(): places = jnp.stack([core, x0, x1, slab])]
  transfers between devices with their start and end apart: 4 -> 5, of which waited for: 2 -> 4; matrix products, arithmetic and copies ran while one was open for 6% -> 0% of each run, Pallas kernels for 5% -> 6%
where the time goes in v3:
time: 86.9 us; the launch traced here: 86.2 us
  waiting for transfers between devices  36.5 us (42%)
  starting transfers between devices  35.3 us (41%)
  Pallas kernels  8.13 us (9%)
  local copies, waits for them, and re-layouts  4.38 us (5%)
  other arithmetic  1.14 us (1%)
    all_to_all x1, waiting for transfers between devices, per_device(): back = lax.all_to_all(part, ('x0', 'z', 'y'), 0, 0, tiled=True)  19.3 us
    all_to_all x1, starting transfers between devices, per_device(): lax.all_to_all(cut.reshape(2 * zy, 8, LANES), ('core', 'z', 'y'), 0, 0, t...  18.2 us
    all_to_all x1, waiting for transfers between devices, per_device(): lax.all_to_all(cut.reshape(2 * zy, 8, LANES), ('core', 'z', 'y'), 0, 0, t...  10.9 us
    all_to_all x1, starting transfers between devices, per_device(): back = lax.all_to_all(part, ('x0', 'z', 'y'), 0, 0, tiled=True)  6.16 us
    ppermute x1, waiting for transfers between devices, per_device(): other = lax.ppermute(mine, 'x0', [(0, 1), (1, 0)])  5.53 us
    ppermute x1, starting transfers between devices, per_device(): lax.ppermute(integrals, ('x1', 'x0'), [(0, 3), (3, 0), (1, 2), (2, 1)])  5.21 us
    unnamed x18, local copies, waits for them, and re-layouts  4.38 us
    ppermute x1, starting transfers between devices, per_device(): got = lax.ppermute(ladder(True), 'core', [(0, 1), (1, 0)])  3.82 us
  transfers between devices with their start and end apart: 5, of which 4 were waited for; matrix products, arithmetic and copies ran while one was open for 0% of the time, Pallas kernels for 6%

profile of v3, /device:TPU:1, one launch (start us, length us, event | category | flops | bytes accessed | tf_op | source)
XLA Modules:
  0.0 86.2 jit_solution(974186327435512807)
XLA Ops:
  0.0 5.2 %collective-permute-start.1 = (bf16[800,800]{1,0:T(8,128)(2,1)}, bf16[800,800]{1,0:T(8,128)(2,1)S(1)}, u32[]{:S(2)}, u32[]{:S(2)}) collective-permute-start(bf16[800,800]{1,0:T(8,128)(2,1)} %block_ref.1), channel_id=1, source_target_pairs={{0,3},{3,0},{1,2},{2,1},{4,7},{7,4},{5,6},{6,5},{8,11},{11,8},{9,1... | collective-permute-start | bytes 3840008 | tf_op jit(solution)/shard_map/ppermute | solution.py:106
  5.2 0.0 copy-start.1
  5.2 1.0 %copy-done.1 = bf16[1,102400]{1,0:T(2,128)(2,1)S(1)} copy-done((bf16[1,102400]{1,0:T(2,128)(2,1)S(1)}, bf16[1,102400]{1,0:T(2,128)(2,1)}, u32[]{:S(2)}) %copy-start.1) | copy-done | bytes 204824
  6.2 1.4 %shard_map.74 = bf16[2,64,8,128]{3,2,1,0:T(8,128)(2,1)} custom-call(bf16[1,102400]{1,0:T(2,128)(2,1)S(1)} %copy-done.1), custom_call_target="tpu_custom_call" | custom-call | bytes 700000 | tf_op jit(solution)/shard_map/pallas_call | solution.py:108
  7.6 18.2 %all-to-all-start = ((bf16[128,8,128]{2,1,0:T(8,128)(2,1)}), bf16[128,8,128]{2,1,0:T(8,128)(2,1)S(1)}, u32[]{:S(2)}, u32[]{:S(2)}) async-start(bf16[128,8,128]{2,1,0:T(8,128)(2,1)} %bitcast.4), calls=%async_computation | async-start | bytes 524288 | tf_op jit(solution)/shard_map/all_to_all | solution.py:109
  25.8 0.0 copy-start.3
  25.9 0.0 copy-start.6
  25.9 0.0 copy-start.8
  25.9 0.1 pad_add_fusion.places_ref.scalars_ref
  26.0 0.0 copy-start
  26.0 1.4 %copy-done = bf16[800,800]{1,0:T(8,128)(2,1)S(1)} copy-done((bf16[800,800]{1,0:T(8,128)(2,1)S(1)}, bf16[800,800]{1,0:T(8,128)(2,1)}, u32[]{:S(2)}) %copy-start) | copy-done | bytes 1280024
  27.3 0.0 copy-start.2
  27.3 0.7 copy-done.2
  28.0 0.0 copy-start.5
  28.0 0.7 copy-done.5
  28.7 0.0 copy-start.7
  28.7 0.7 copy-done.7
  29.3 1.2 %shard_map.73.own_ref = bf16[896,896]{1,0:T(8,128)(2,1)S(1)} custom-call(s32[4]{0:T(128)S(1)} %pad_add_fusion.places_ref.scalars_ref, s32[128]{0:T(128)S(1)} %copy-done.7, s32[4]{0:T(128)S(1)} %copy-done.5, s32[800]{0:T(1024)S(1)} %copy-done.2, bf16[800,800]{1,0:T(8,128)(2,1)S(1)} %copy-done), custom_call_target="tpu_custom_call" | custom-call | flops 20000000 | bytes 3000000 | tf_op jit(solution)/shard_map/pallas_call | solution.py:115
  30.5 10.9 %all-to-all-done = bf16[128,8,128]{2,1,0:T(8,128)(2,1)S(1)} async-done(((bf16[128,8,128]{2,1,0:T(8,128)(2,1)}), bf16[128,8,128]{2,1,0:T(8,128)(2,1)S(1)}, u32[]{:S(2)}, u32[]{:S(2)}) %all-to-all-start) | async-done | bytes 262176 | tf_op jit(solution)/shard_map/all_to_all | solution.py:109
  41.5 1.9 %collective-permute-start = (bf16[1024,128]{1,0:T(8,128)(2,1)S(1)}, bf16[1024,128]{1,0:T(8,128)(2,1)S(1)}, u32[]{:S(2)}, u32[]{:S(2)}) collective-permute-start(bf16[1024,128]{1,0:T(8,128)(2,1)S(1)} %bitcast.10), channel_id=1, source_target_pairs={{0,1},{1,0},{2,3},{3,2},{4,5},{5,4},{6,7},{7,6},{8,9},{9,8},{10,11... | collective-permute-start | bytes 786440 | tf_op jit(solution)/shard_map/ppermute | solution.py:118
  43.4 0.0 collective-permute-done.1.block_ref
  43.4 0.0 copy-done.3
  43.4 0.0 copy-done.6
  43.4 0.0 copy-done.8
  43.4 1.2 %shard_map.75.partner_ref = bf16[896,896]{1,0:T(8,128)(2,1)S(1)} custom-call(s32[4]{0:T(128)S(1)} %pad_add_fusion.places_ref.scalars_ref, s32[128]{0:T(128)S(1)} %copy-done.8, s32[4]{0:T(128)S(1)} %copy-done.6, s32[800]{0:T(1024)S(1)} %copy-done.3, bf16[800,800]{1,0:T(8,128)(2,1)S(1)} %collective-permute-done.1.block_ref), custom_call_target="tpu_custom_call" | custom-call | flops 20000000 | bytes 3000000 | tf_op jit(solution)/shard_map/pallas_call | solution.py:115
  44.6 5.5 %collective-permute-done.other_ref = bf16[1024,128]{1,0:T(8,128)(2,1)S(1)} collective-permute-done((bf16[1024,128]{1,0:T(8,128)(2,1)S(1)}, bf16[1024,128]{1,0:T(8,128)(2,1)S(1)}, u32[]{:S(2)}, u32[]{:S(2)}) %collective-permute-start) | collective-permute-done | bytes 262176 | tf_op jit(solution)/shard_map/ppermute | solution.py:118
  50.2 1.5 %shard_map.77 = f32[2048,128]{1,0:T(8,128)S(1)} custom-call(s32[4]{0:T(128)S(1)} %pad_add_fusion.places_ref.scalars_ref, bf16[1024,128]{1,0:T(8,128)(2,1)S(1)} %bitcast.11, bf16[1024,128]{1,0:T(8,128)(2,1)S(1)} %collective-permute-done.other_ref, bf16[896,896]{1,0:T(8,128)(2,1)S(1)} %shard_map.73.own_ref, bf16[896,896]{1,0:T(8,128)(2,1)S(1)} %shard_map.75.partner_ref), custom_call_target="tpu_custom_call" | custom-call | flops 411041792 | bytes 5000000 | tf_op jit(solution)/shard_map/pallas_call | solution.py:122
  51.7 3.8 %collective-permute-start.2 = (f32[2048,128]{1,0:T(8,128)S(1)}, f32[2048,128]{1,0:T(8,128)S(1)}, u32[]{:S(2)}, u32[]{:S(2)}) collective-permute-start(f32[2048,128]{1,0:T(8,128)S(1)} %shard_map.77), channel_id=1, source_target_pairs={{0,4},{4,0},{1,5},{5,1},{2,6},{6,2},{3,7},{7,3},{8,12},{12,8},{9,1... | collective-permute-start | bytes 3145736 | tf_op jit(solution)/shard_map/ppermute | solution.py:131
  55.5 1.5 %shard_map.76 = f32[2048,128]{1,0:T(8,128)S(1)} custom-call(s32[4]{0:T(128)S(1)} %pad_add_fusion.places_ref.scalars_ref, bf16[1024,128]{1,0:T(8,128)(2,1)S(1)} %bitcast.12, bf16[1024,128]{1,0:T(8,128)(2,1)S(1)} %collective-permute-done.other_ref, bf16[896,896]{1,0:T(8,128)(2,1)S(1)} %shard_map.73.own_ref, bf16[896,896]{1,0:T(8,128)(2,1)S(1)} %shard_map.75.partner_ref), custom_call_target="tpu_custom_call" | custom-call | flops 411041792 | bytes 5000000 | tf_op jit(solution)/shard_map/pallas_call | solution.py:122
  57.1 0.0 copy-start.4
  57.1 0.7 collective-permute-done.2
  57.8 1.0 %multiply_convert_fusion = f16[2048,128]{1,0:T(8,128)(2,1)} fusion(f32[2048,128]{1,0:T(8,128)S(1)} %shard_map.76, f32[2048,128]{1,0:T(8,128)S(1)} %collective-permute-done.2), kind=kLoop, calls=%fused_computation.1 | loop fusion | flops 786432 | bytes 2621440 | tf_op jit(solution)/shard_map/convert_element_type | solution.py:133
  58.8 6.2 %all-to-all-start.1 = ((f16[128,16,128]{2,1,0:T(8,128)(2,1)}), f16[128,16,128]{2,1,0:T(8,128)(2,1)S(1)}, u32[]{:S(2)}, u32[]{:S(2)}) async-start(f16[128,16,128]{2,1,0:T(8,128)(2,1)} %bitcast.6), calls=%async_computation.1 | async-start | bytes 1048576 | tf_op jit(solution)/shard_map/all_to_all | solution.py:134
  65.6 19.3 %all-to-all-done.1 = f16[128,16,128]{2,1,0:T(8,128)(2,1)S(1)} async-done(((f16[128,16,128]{2,1,0:T(8,128)(2,1)}), f16[128,16,128]{2,1,0:T(8,128)(2,1)S(1)}, u32[]{:S(2)}, u32[]{:S(2)}) %all-to-all-start.1) | async-done | bytes 524320 | tf_op jit(solution)/shard_map/all_to_all | solution.py:134
  84.9 0.1 convert_reduce_fusion.sums_ref
  85.0 0.0 copy-done.4
  85.0 1.3 %shard_map.78 = bf16[1,3200]{1,0:T(2,128)(2,1)} custom-call(s32[4]{0:T(128)S(1)} %pad_add_fusion.places_ref.scalars_ref, s32[1]{0:T(128)S(6)} %copy.8.pair_ref, s32[4]{0:T(128)S(1)} %copy-done.6, f32[2,16,128]{2,1,0:T(8,128)S(1)} %convert_reduce_fusion.sums_ref, s32[800]{0:T(1024)S(1)} %copy-done.3, bf16[1,3200]{1,0:T(2,128)(2,1)S(1)} %copy-done.4), custom_call_target="tpu_custom_call" | custom-call | bytes 50000 | tf_op jit(solution)/shard_map/pallas_call | solution.py:137
Async XLA Ops:
  0.0 43.4 %collective-permute-start.1 = (bf16[800,800]{1,0:T(8,128)(2,1)}, bf16[800,800]{1,0:T(8,128)(2,1)S(1)}, u32[]{:S(2)}, u32[]{:S(2)}) collective-permute-start(bf16[800,800]{1,0:T(8,128)(2,1)} %block_ref.1), channel_id=1, source_target_pairs={{0,3},{3,0},{1,2},{2,1},{4,7},{7,4},{5,6},{6,5},{8,11},{11,8},{9,1... | collective-permute-start | bytes 3840008 | tf_op jit(solution)/shard_map/ppermute | solution.py:106
  5.2 1.0 %copy-start.1 = (bf16[1,102400]{1,0:T(2,128)(2,1)S(1)}, bf16[1,102400]{1,0:T(2,128)(2,1)}, u32[]{:S(2)}) copy-start(bf16[1,102400]{1,0:T(2,128)(2,1)} %row_ref.1) | copy-start | bytes 614404
  7.6 33.8 %all-to-all-start = ((bf16[128,8,128]{2,1,0:T(8,128)(2,1)}), bf16[128,8,128]{2,1,0:T(8,128)(2,1)S(1)}, u32[]{:S(2)}, u32[]{:S(2)}) async-start(bf16[128,8,128]{2,1,0:T(8,128)(2,1)} %bitcast.4), calls=%async_computation | async-start | bytes 524288 | tf_op jit(solution)/shard_map/all_to_all | solution.py:109
  25.8 17.5 %copy-start.3 = (s32[800]{0:T(1024)S(1)}, s32[800]{0:T(1024)}, u32[]{:S(2)}) copy-start(s32[800]{0:T(1024)} %virt_ref.5) | copy-start | bytes 9604
  25.9 17.5 %copy-start.6 = (s32[4]{0:T(128)S(1)}, s32[4]{0:T(128)}, u32[]{:S(2)}) copy-start(s32[4]{0:T(128)} %upper_ref.5) | copy-start | bytes 52
  25.9 17.5 %copy-start.8 = (s32[128]{0:T(128)S(1)}, s32[128]{0:T(128)}, u32[]{:S(2)}) copy-start(s32[128]{0:T(128)} %slab_ref.3) | copy-start | bytes 1540
  26.0 1.4 %copy-start = (bf16[800,800]{1,0:T(8,128)(2,1)S(1)}, bf16[800,800]{1,0:T(8,128)(2,1)}, u32[]{:S(2)}) copy-start(bf16[800,800]{1,0:T(8,128)(2,1)} %block_ref.1) | copy-start | bytes 3840004
  27.3 0.7 copy-start.2
  28.0 0.7 copy-start.5
  28.7 0.7 copy-start.7
  41.5 8.7 %collective-permute-start = (bf16[1024,128]{1,0:T(8,128)(2,1)S(1)}, bf16[1024,128]{1,0:T(8,128)(2,1)S(1)}, u32[]{:S(2)}, u32[]{:S(2)}) collective-permute-start(bf16[1024,128]{1,0:T(8,128)(2,1)S(1)} %bitcast.10), channel_id=1, source_target_pairs={{0,1},{1,0},{2,3},{3,2},{4,5},{5,4},{6,7},{7,6},{8,9},{9,8},{10,11... | collective-permute-start | bytes 786440 | tf_op jit(solution)/shard_map/ppermute | solution.py:118
  51.7 6.1 %collective-permute-start.2 = (f32[2048,128]{1,0:T(8,128)S(1)}, f32[2048,128]{1,0:T(8,128)S(1)}, u32[]{:S(2)}, u32[]{:S(2)}) collective-permute-start(f32[2048,128]{1,0:T(8,128)S(1)} %shard_map.77), channel_id=1, source_target_pairs={{0,4},{4,0},{1,5},{5,1},{2,6},{6,2},{3,7},{7,3},{8,12},{12,8},{9,1... | collective-permute-start | bytes 3145736 | tf_op jit(solution)/shard_map/ppermute | solution.py:131
  57.1 27.9 %copy-start.4 = (bf16[1,3200]{1,0:T(2,128)(2,1)S(1)}, bf16[1,3200]{1,0:T(2,128)(2,1)}, u32[]{:S(2)}) copy-start(bf16[1,3200]{1,0:T(2,128)(2,1)} %old_ref.1) | copy-start | bytes 19204
  58.8 26.1 %all-to-all-start.1 = ((f16[128,16,128]{2,1,0:T(8,128)(2,1)}), f16[128,16,128]{2,1,0:T(8,128)(2,1)S(1)}, u32[]{:S(2)}, u32[]{:S(2)}) async-start(f16[128,16,128]{2,1,0:T(8,128)(2,1)} %bitcast.6), calls=%async_computation.1 | async-start | bytes 1048576 | tf_op jit(solution)/shard_map/all_to_all | solution.py:134

commit v4 on v3

v4 whole, which is shorter than its diff:
```python
import functools

import jax
import jax.numpy as jnp
from jax import lax
from jax.experimental import pallas as pl
from jax.experimental.pallas import tpu as pltpu
from jax.sharding import Mesh
from jax.sharding import PartitionSpec as P

AXES = ("z", "y", "core", "x1", "x0")
BF16, F32, F16 = jnp.bfloat16, jnp.float32, jnp.float16
NV = 800
LANES = 128
TILES = 7
WIDE = TILES * LANES
SCALE = 64.0

VMEM = pl.BlockSpec(memory_space=pltpu.VMEM)
SMEM = pl.BlockSpec(memory_space=pltpu.SMEM)


def call(body, out, ins, flops, nbytes, scratch=()):
    return pl.pallas_call(
        body,
        out_shape=out,
        in_specs=[SMEM if kind == "s" else VMEM for kind in ins],
        out_specs=jax.tree.map(lambda _: VMEM, out),
        scratch_shapes=list(scratch),
        compiler_params=pltpu.CompilerParams(vmem_limit_bytes=16 * 1024 * 1024),
        cost_estimate=pl.CostEstimate(flops=flops, bytes_accessed=nbytes, transcendentals=0),
    )


def cut_body(steps, row_ref, out_ref, row, cut, in_sems, out_sems):
    filler = jnp.zeros((1, LANES), F32)
    lanes, slabs = row.shape[1] // steps, cut.shape[1] // steps

    def fetch(i):
        part = pl.ds(i * lanes, lanes)
        return pltpu.make_async_copy(row_ref.at[:, part], row.at[:, part], in_sems.at[i])

    def put(i):
        part = pl.ds(i * slabs, slabs)
        return pltpu.make_async_copy(cut.at[:, part], out_ref.at[:, part], out_sems.at[i])

    def four(q, carry):
        for r in range(4):
            at = [pl.multiple_of(q * 3200 + (6 * r + t) * LANES, LANES) for t in range(TILES)]
            tiles = [row[:, pl.ds(a, LANES)].astype(F32) for a in at]
            cut[r % 2, 2 * q + r // 2] = jnp.concatenate(tiles + [filler], axis=0).astype(BF16)
        return carry

    for i in range(steps):
        fetch(i).start()
    for i in range(steps):
        fetch(i).wait()
        lax.fori_loop(i * slabs // 2, (i + 1) * slabs // 2, four, 0, unroll=4)
        put(i).start()
    for i in range(steps):
        put(i).wait()


def kept_body(places_ref, slab_ref, upper_ref, virt_ref, block_ref, own_ref, mask_ref):
    x, slab = 2 * places_ref[2] + places_ref[1], slab_ref[places_ref[3]]
    label = lax.broadcasted_iota(jnp.int32, (16, NV), 0)
    virt = virt_ref[...].reshape(1, NV)
    rows = jnp.where(label == jnp.bitwise_xor(virt, slab), 1.0, 0.0).astype(BF16)

    def same(a):
        columns = jnp.where(label == jnp.bitwise_xor(virt, upper_ref[a]), 1.0, 0.0).astype(BF16)
        return lax.dot_general(rows, columns, (((0,), (0,)), ((), ())), preferred_element_type=F32)

    own_ref[...] = jnp.where(same(x) > 0.5, block_ref[...].astype(F32), 0.0).astype(BF16)
    mask_ref[...] = same(3 - x).astype(BF16)


def put_tiles(sums, count, out_ref, first, step):
    wide = jnp.concatenate([sums, jnp.zeros((count, WIDE - NV), F32)], axis=1)
    for t in range(TILES):
        out_ref[pl.ds(first + t, count, stride=step), :] = wide[:, t * LANES : (t + 1) * LANES]
    out_ref[pl.ds(first + TILES, count, stride=step), :] = jnp.zeros((count, LANES), F32)


def rows_body(zy, places_ref, mine_ref, other_ref, own_ref, lhs_ref, out_ref, wide):
    x0, r = places_ref[1], places_ref[3] % 4
    for block, source in ((0, mine_ref), (1, other_ref)):
        place = pl.multiple_of((x0 if block == 0 else 1 - x0) * zy, zy)
        out_ref[0 : zy * 8, :] = source[...].astype(F32)
        for t in range(TILES):
            wide[pl.ds(place, zy), t * LANES : (t + 1) * LANES] = out_ref[pl.ds(t, zy, stride=8), :]
    for shift in range(4):

        @pl.when(r == shift)
        def _():
            lhs_ref[...] = wide[:, 32 * shift : 32 * shift + NV].astype(BF16)

    sums = jnp.dot(lhs_ref[...], own_ref[...], preferred_element_type=F32)
    put_tiles(sums, 2 * zy, out_ref, 0, 8)


def ladder_body(zy, lhs_ref, own_sums_ref, partner_ref, mask_ref, out_ref):
    kept = partner_ref[...] * mask_ref[...]
    sums = jnp.dot(lhs_ref[...], kept, preferred_element_type=F32)
    put_tiles(sums, 2 * zy, out_ref, 8, 16)
    for t in range(8):
        out_ref[pl.ds(t, 2 * zy, stride=16), :] = own_sums_ref[pl.ds(t, 2 * zy, stride=8), :]


def finish_body(places_ref, pair_ref, upper_ref, sums_ref, virt_ref, old_ref, out_ref):
    swap = places_ref[2] == 1
    pair = pair_ref[0]
    order = ((0, 0), (1, 0), (1, 1), (0, 1))
    virt = virt_ref[...].reshape(1, NV)
    for a in range(4):
        s, h = order[a]
        s2, h2 = order[(a + 2) % 4]
        straight = sums_ref[s, 8 * h : 8 * h + 8, :]
        turned = sums_ref[s2, 8 * h2 : 8 * h2 + 8, :]
        tiles = jnp.where(swap, turned, straight) * (1.0 / SCALE)
        row = jnp.concatenate([tiles[t : t + 1, :] for t in range(TILES)], axis=1)[:, :NV]
        ab = jnp.bitwise_xor(virt, upper_ref[a])
        row = jnp.where(ab == pair, row, 0.0)
        old = old_ref[:, a * NV : (a + 1) * NV].astype(F32)
        out_ref[:, a * NV : (a + 1) * NV] = (old + row).astype(BF16)


def per_device(amplitudes, integrals, residual_in, pair_irrep, slab_irrep, upper_irrep, virt_irrep):
    core = lax.axis_index("core")
    x1 = lax.axis_index("x1")
    x0 = lax.axis_index("x0")
    slab = lax.axis_index(("z", "y", "core"))
    zy = lax.axis_size("z") * lax.axis_size("y")
    shape = jax.ShapeDtypeStruct
    places = jnp.stack([core, x0, x1, slab])

    partner = lax.ppermute(integrals, ("x1", "x0"), [(0, 3), (3, 0), (1, 2), (2, 1)])

    steps = 4
    cut = pl.pallas_call(
        functools.partial(cut_body, steps),
        in_specs=[pl.BlockSpec(memory_space=pl.ANY)],
        out_specs=pl.BlockSpec(memory_space=pl.ANY),
        out_shape=shape((2, zy, 8, LANES), BF16),
        scratch_shapes=[
            pltpu.VMEM(amplitudes.shape, BF16),
            pltpu.VMEM((2, zy, 8, LANES), BF16),
            pltpu.SemaphoreType.DMA((steps,)),
            pltpu.SemaphoreType.DMA((steps,)),
        ],
        cost_estimate=pl.CostEstimate(flops=0, bytes_accessed=700000, transcendentals=0),
    )(amplitudes)
    mine = lax.all_to_all(cut.reshape(2 * zy, 8, LANES), ("core", "z", "y"), 0, 0, tiled=True)
    mine = mine.reshape(2 * zy * 8, LANES)

    fill = call(kept_body, [shape((NV, NV), BF16)] * 2, "sssvv", 20000000, 3000000)
    own_v, mask = fill(places, slab_irrep, upper_irrep, virt_irrep, integrals)
    own_v, mask, mine = lax.optimization_barrier((own_v, mask, mine))
    half, tiles = shape((2 * zy, NV), BF16), shape((2 * zy * 8, LANES), F32)
    rows = call(
        functools.partial(rows_body, zy),
        [half, tiles],
        "svvv",
        2 * 128 * 800 * 800,
        3000000,
        [pltpu.VMEM((2 * zy, WIDE), F32)],
    )
    ladder = call(
        functools.partial(ladder_body, zy),
        shape((2 * zy * 16, LANES), F32),
        "vvvv",
        2 * 128 * 800 * 800,
        5000000,
    )

    def exchanged(of_core):
        here = lax.dynamic_slice_in_dim(mine, of_core * (zy * 8), zy * 8, 0)
        return here, lax.ppermute(here, "x0", [(0, 1), (1, 0)])

    send_rows, keep_rows = exchanged(1 - core), exchanged(core)
    send = ladder(*rows(places, *send_rows, own_v), partner, mask)
    send, keep_rows = lax.optimization_barrier((send, keep_rows))
    got = lax.ppermute(send, "core", [(0, 1), (1, 0)])
    keep = ladder(*rows(places, *keep_rows, own_v), partner, mask)
    part = ((keep + got) * SCALE).astype(F16).reshape(2 * zy, 16, LANES)
    back = lax.all_to_all(part, ("x0", "z", "y"), 0, 0, tiled=True)
    sums = jnp.sum(back.reshape(2, zy, 16, LANES).astype(F32), axis=1)
    finish = call(finish_body, shape((1, 4 * NV), BF16), "sssvvv", 0, 50000)
    return finish(places, pair_irrep, upper_irrep, sums, virt_irrep, residual_in)


def solution(mesh):
    fine = Mesh(mesh.devices.reshape(8, 8, 2, 2, 2), AXES)
    return jax.shard_map(
        per_device,
        mesh=fine,
        in_specs=(P(AXES, None), P(AXES[:3], AXES[3:]), P(AXES, None), P(AXES), P(), P(), P()),
        out_specs=P(AXES, None),
        check_vma=False,
    )
```

time: 86.9 us -> 85.8 us (0.987)
  waiting for transfers between devices: 36.5 us -> 31.1 us
  starting transfers between devices: 35.3 us -> 38.5 us
  Pallas kernels: 8.13 us -> 9.01 us
    ppermute x2 -> x3, waiting for transfers between devices: 6.24 us -> 2.25 us  [the longest x2 1.96 us: exchanged(): return (here, lax.ppermute(here, 'x0', [(0, 1), (1, 0)]))]
    ppermute x2 -> x3, starting transfers between devices: 5.73 us -> 8.83 us  [the longest x2 5.41 us: exchanged(): return (here, lax.ppermute(here, 'x0', [(0, 1), (1, 0)]))]
    all_to_all x1, waiting for transfers between devices: 10.9 us -> 9.53 us  [per_device(): lax.all_to_all(cut.reshape(2 * zy, 8, LANES), ('core', 'z', 'y'), 0, 0, t...]
    pallas_call x5 -> x6, Pallas kernels: 6.88 us -> 7.76 us  [the longest x1 2.35 us: per_device(): pl.pallas_call(functools.partial(cut_body, steps), in_specs=[pl.BlockSpec...]
  transfers between devices with their start and end apart: 5 -> 6, of which waited for: 4 -> 5; matrix products, arithmetic and copies ran while one was open for 0% -> 0% of each run, Pallas kernels for 6% -> 9%
where the time goes in v4:
time: 85.8 us; the launch traced here: 85.1 us
  starting transfers between devices  38.5 us (45%)
  waiting for transfers between devices  31.1 us (36%)
  Pallas kernels  9.01 us (11%)
  local copies, waits for them, and re-layouts  4.53 us (5%)
  other arithmetic  1.11 us (1%)
    all_to_all x1, waiting for transfers between devices, per_device(): back = lax.all_to_all(part, ('x0', 'z', 'y'), 0, 0, tiled=True)  19.3 us
    all_to_all x1, starting transfers between devices, per_device(): lax.all_to_all(cut.reshape(2 * zy, 8, LANES), ('core', 'z', 'y'), 0, 0, t...  18.2 us
    all_to_all x1, waiting for transfers between devices, per_device(): lax.all_to_all(cut.reshape(2 * zy, 8, LANES), ('core', 'z', 'y'), 0, 0, t...  9.53 us
    all_to_all x1, starting transfers between devices, per_device(): back = lax.all_to_all(part, ('x0', 'z', 'y'), 0, 0, tiled=True)  6.3 us
    ppermute x2, starting transfers between devices, exchanged(): return (here, lax.ppermute(here, 'x0', [(0, 1), (1, 0)]))  5.41 us
    ppermute x1, starting transfers between devices, per_device(): lax.ppermute(integrals, ('x1', 'x0'), [(0, 3), (3, 0), (1, 2), (2, 1)])  5.21 us
    unnamed x18, local copies, waits for them, and re-layouts  4.51 us
    ppermute x1, starting transfers between devices, per_device(): got = lax.ppermute(send, 'core', [(0, 1), (1, 0)])  3.42 us
  transfers between devices with their start and end apart: 6, of which 5 were waited for; matrix products, arithmetic and copies ran while one was open for 0% of the time, Pallas kernels for 9%

profile of v4, /device:TPU:1, one launch (start us, length us, event | category | flops | bytes accessed | tf_op | source)
XLA Modules:
  0.0 85.1 jit_solution(13961724619117381496)
XLA Ops:
  0.0 5.2 %collective-permute-start.1 = (bf16[800,800]{1,0:T(8,128)(2,1)}, bf16[800,800]{1,0:T(8,128)(2,1)S(1)}, u32[]{:S(2)}, u32[]{:S(2)}) collective-permute-start(bf16[800,800]{1,0:T(8,128)(2,1)} %block_ref.1), channel_id=1, source_target_pairs={{0,3},{3,0},{1,2},{2,1},{4,7},{7,4},{5,6},{6,5},{8,11},{11,8},{9,1... | collective-permute-start | bytes 3840008 | tf_op jit(solution)/shard_map/ppermute | solution.py:137
  5.2 2.4 %shard_map.74 = bf16[2,64,8,128]{3,2,1,0:T(8,128)(2,1)} custom-call(bf16[1,102400]{1,0:T(2,128)(2,1)} %row_ref.1), custom_call_target="tpu_custom_call" | custom-call | bytes 700000 | tf_op jit(solution)/shard_map/pallas_call | solution.py:140
  7.6 18.2 %all-to-all-start = ((bf16[128,8,128]{2,1,0:T(8,128)(2,1)}), bf16[128,8,128]{2,1,0:T(8,128)(2,1)S(1)}, u32[]{:S(2)}, u32[]{:S(2)}) async-start(bf16[128,8,128]{2,1,0:T(8,128)(2,1)} %bitcast.11), calls=%async_computation | async-start | bytes 524288 | tf_op jit(solution)/shard_map/all_to_all | solution.py:153
  25.8 0.1 pad_add_fusion.places_ref
  25.9 0.0 copy-start.2
  25.9 1.4 %copy-done.2 = bf16[800,800]{1,0:T(8,128)(2,1)S(1)} copy-done((bf16[800,800]{1,0:T(8,128)(2,1)S(1)}, bf16[800,800]{1,0:T(8,128)(2,1)}, u32[]{:S(2)}) %copy-start.2) | copy-done | bytes 1280024
  27.2 0.0 copy-start.3
  27.2 0.7 copy-done.3
  27.9 0.0 copy-start.6
  27.9 0.7 copy-done.6
  28.6 0.0 copy-start.8
  28.6 0.7 copy-done.8
  29.2 1.5 %shard_map.73 = (bf16[800,800]{1,0:T(8,128)(2,1)S(1)}, bf16[800,800]{1,0:T(8,128)(2,1)S(1)}) custom-call(s32[4]{0:T(128)S(1)} %pad_add_fusion.places_ref, s32[128]{0:T(128)S(1)} %copy-done.8, s32[4]{0:T(128)S(1)} %copy-done.6, s32[800]{0:T(1024)S(1)} %copy-done.3, bf16[800,800]{1,0:T(8,128)(2,1)S(1)} %copy-done.2), custom_call_target="tpu_custom_call" | custom-call | flops 20000000 | bytes 3000000 | tf_op jit(solution)/shard_map/pallas_call | solution.py:157
  30.7 0.0 copy-start
  30.7 1.1 %copy-done = bf16[800,800]{1,0:T(8,128)(2,1)} copy-done((bf16[800,800]{1,0:T(8,128)(2,1)}, bf16[800,800]{1,0:T(8,128)(2,1)S(1)}, u32[]{:S(2)}) %copy-start) | copy-done | bytes 1280024
  31.9 9.5 %all-to-all-done = bf16[128,8,128]{2,1,0:T(8,128)(2,1)S(1)} async-done(((bf16[128,8,128]{2,1,0:T(8,128)(2,1)}), bf16[128,8,128]{2,1,0:T(8,128)(2,1)S(1)}, u32[]{:S(2)}, u32[]{:S(2)}) %all-to-all-start) | async-done | bytes 262176 | tf_op jit(solution)/shard_map/all_to_all | solution.py:153
  41.4 0.0 copy-start.1
  41.4 2.1 %collective-permute-start = (bf16[512,128]{1,0:T(8,128)(2,1)S(1)}, bf16[512,128]{1,0:T(8,128)(2,1)S(1)}, u32[]{:S(2)}, u32[]{:S(2)}) collective-permute-start(bf16[512,128]{1,0:T(8,128)(2,1)S(1)} %get-tuple-element.30.mine_ref), channel_id=1, source_target_pairs={{0,1},{1,0},{2,3},{3,2},{4,5},{5,4},{6,7},{7,6},{8,9},{9,8},{10,11... | collective-permute-start | bytes 393224 | tf_op jit(solution)/shard_map/ppermute | solution.py:178
  43.5 3.4 %collective-permute-start.2 = (bf16[512,128]{1,0:T(8,128)(2,1)S(1)}, bf16[512,128]{1,0:T(8,128)(2,1)S(1)}, u32[]{:S(2)}, u32[]{:S(2)}) collective-permute-start(bf16[512,128]{1,0:T(8,128)(2,1)S(1)} %get-tuple-element.24.mine_ref), channel_id=1, source_target_pairs={{0,1},{1,0},{2,3},{3,2},{4,5},{5,4},{6,7},{7,6},{8,9},{9,8},{10,11... | collective-permute-start | bytes 393224 | tf_op jit(solution)/shard_map/ppermute | solution.py:178
  46.9 0.4 collective-permute-done.other_ref
  47.3 1.2 %shard_map.75 = (bf16[128,800]{1,0:T(8,128)(2,1)S(1)}, f32[1024,128]{1,0:T(8,128)S(1)}) custom-call(s32[4]{0:T(128)S(1)} %pad_add_fusion.places_ref, bf16[512,128]{1,0:T(8,128)(2,1)S(1)} %get-tuple-element.30.mine_ref, bf16[512,128]{1,0:T(8,128)(2,1)S(1)} %collective-permute-done.other_ref, bf16[800,800]{1,0:T(8,128)(2,1)S(1)} %get-tuple-element.20.own_ref), custom_call_target="tpu_custom_call" | custom-call | flops 163840000 | bytes 3000000 | tf_op jit(solution)/shard_map/pallas_call | solution.py:181
  48.5 0.0 collective-permute-done.1.partner_ref
  48.5 0.0 copy-done.1
  48.5 0.8 shard_map.76
  49.3 1.5 %collective-permute-done.2.other_ref = bf16[512,128]{1,0:T(8,128)(2,1)S(1)} collective-permute-done((bf16[512,128]{1,0:T(8,128)(2,1)S(1)}, bf16[512,128]{1,0:T(8,128)(2,1)S(1)}, u32[]{:S(2)}, u32[]{:S(2)}) %collective-permute-start.2) | collective-permute-done | bytes 131104 | tf_op jit(solution)/shard_map/ppermute | solution.py:178
  50.8 3.4 %collective-permute-start.3 = (f32[2048,128]{1,0:T(8,128)S(1)}, f32[2048,128]{1,0:T(8,128)S(1)}, u32[]{:S(2)}, u32[]{:S(2)}) collective-permute-start(f32[2048,128]{1,0:T(8,128)S(1)} %shard_map.76), channel_id=1, source_target_pairs={{0,4},{4,0},{1,5},{5,1},{2,6},{6,2},{3,7},{7,3},{8,12},{12,8},{9,1... | collective-permute-start | bytes 3145736 | tf_op jit(solution)/shard_map/ppermute | solution.py:183
  54.2 1.2 %shard_map.77 = (bf16[128,800]{1,0:T(8,128)(2,1)S(1)}, f32[1024,128]{1,0:T(8,128)S(1)}) custom-call(s32[4]{0:T(128)S(1)} %pad_add_fusion.places_ref, bf16[512,128]{1,0:T(8,128)(2,1)S(1)} %get-tuple-element.24.mine_ref, bf16[512,128]{1,0:T(8,128)(2,1)S(1)} %collective-permute-done.2.other_ref, bf16[800,800]{1,0:T(8,128)(2,1)S(1)} %get-tuple-element.20.own_ref), custom_call_target="tpu_custom_call" | custom-call | flops 163840000 | bytes 3000000 | tf_op jit(solution)/shard_map/pallas_call | solution.py:184
  55.5 0.8 shard_map.78
  56.2 0.3 collective-permute-done.3
  56.5 0.9 %multiply_convert_fusion = f16[2048,128]{1,0:T(8,128)(2,1)} fusion(f32[2048,128]{1,0:T(8,128)S(1)} %shard_map.78, f32[2048,128]{1,0:T(8,128)S(1)} %collective-permute-done.3), kind=kLoop, calls=%fused_computation.1 | loop fusion | flops 786432 | bytes 2621440 | tf_op jit(solution)/shard_map/convert_element_type | solution.py:185
  57.5 0.0 copy-start.4
  57.5 0.0 copy-start.5
  57.5 0.0 copy-start.7
  57.5 6.3 %all-to-all-start.1 = ((f16[128,16,128]{2,1,0:T(8,128)(2,1)}), f16[128,16,128]{2,1,0:T(8,128)(2,1)S(1)}, u32[]{:S(2)}, u32[]{:S(2)}) async-start(f16[128,16,128]{2,1,0:T(8,128)(2,1)} %bitcast.6), calls=%async_computation.1 | async-start | bytes 1048576 | tf_op jit(solution)/shard_map/all_to_all | solution.py:186
  64.4 19.3 %all-to-all-done.1 = f16[128,16,128]{2,1,0:T(8,128)(2,1)S(1)} async-done(((f16[128,16,128]{2,1,0:T(8,128)(2,1)}), f16[128,16,128]{2,1,0:T(8,128)(2,1)S(1)}, u32[]{:S(2)}, u32[]{:S(2)}) %all-to-all-start.1) | async-done | bytes 524320 | tf_op jit(solution)/shard_map/all_to_all | solution.py:186
  83.7 0.1 convert_reduce_fusion.sums_ref
  83.8 0.0 copy-done.4
  83.8 0.0 copy-done.5
  83.8 0.0 copy-done.7
  83.8 1.3 %shard_map.79 = bf16[1,3200]{1,0:T(2,128)(2,1)} custom-call(s32[4]{0:T(128)S(1)} %pad_add_fusion.places_ref, s32[1]{0:T(128)S(6)} %copy.8.pair_ref, s32[4]{0:T(128)S(1)} %copy-done.7, f32[2,16,128]{2,1,0:T(8,128)S(1)} %convert_reduce_fusion.sums_ref, s32[800]{0:T(1024)S(1)} %copy-done.4, bf16[1,3200]{1,0:T(2,128)(2,1)S(1)} %copy-done.5), custom_call_target="tpu_custom_call" | custom-call | bytes 50000 | tf_op jit(solution)/shard_map/pallas_call | solution.py:189
  (1 shorter events, 0.0 us)
Async XLA Ops:
  0.0 48.5 %collective-permute-start.1 = (bf16[800,800]{1,0:T(8,128)(2,1)}, bf16[800,800]{1,0:T(8,128)(2,1)S(1)}, u32[]{:S(2)}, u32[]{:S(2)}) collective-permute-start(bf16[800,800]{1,0:T(8,128)(2,1)} %block_ref.1), channel_id=1, source_target_pairs={{0,3},{3,0},{1,2},{2,1},{4,7},{7,4},{5,6},{6,5},{8,11},{11,8},{9,1... | collective-permute-start | bytes 3840008 | tf_op jit(solution)/shard_map/ppermute | solution.py:137
  7.6 33.8 %all-to-all-start = ((bf16[128,8,128]{2,1,0:T(8,128)(2,1)}), bf16[128,8,128]{2,1,0:T(8,128)(2,1)S(1)}, u32[]{:S(2)}, u32[]{:S(2)}) async-start(bf16[128,8,128]{2,1,0:T(8,128)(2,1)} %bitcast.11), calls=%async_computation | async-start | bytes 524288 | tf_op jit(solution)/shard_map/all_to_all | solution.py:153
  25.9 1.4 %copy-start.2 = (bf16[800,800]{1,0:T(8,128)(2,1)S(1)}, bf16[800,800]{1,0:T(8,128)(2,1)}, u32[]{:S(2)}) copy-start(bf16[800,800]{1,0:T(8,128)(2,1)} %block_ref.1) | copy-start | bytes 3840004
  27.2 0.7 copy-start.3
  27.9 0.7 copy-start.6
  28.6 0.7 copy-start.8
  30.7 1.1 %copy-start = (bf16[800,800]{1,0:T(8,128)(2,1)}, bf16[800,800]{1,0:T(8,128)(2,1)S(1)}, u32[]{:S(2)}) copy-start(bf16[800,800]{1,0:T(8,128)(2,1)S(1)} %get-tuple-element.23.mask_ref) | copy-start | bytes 3840004
  41.4 7.1 %copy-start.1 = (bf16[800,800]{1,0:T(8,128)(2,1)S(1)}, bf16[800,800]{1,0:T(8,128)(2,1)}, u32[]{:S(2)}) copy-start(bf16[800,800]{1,0:T(8,128)(2,1)} %copy-done) | copy-start | bytes 3840004
  41.4 5.8 %collective-permute-start = (bf16[512,128]{1,0:T(8,128)(2,1)S(1)}, bf16[512,128]{1,0:T(8,128)(2,1)S(1)}, u32[]{:S(2)}, u32[]{:S(2)}) collective-permute-start(bf16[512,128]{1,0:T(8,128)(2,1)S(1)} %get-tuple-element.30.mine_ref), channel_id=1, source_target_pairs={{0,1},{1,0},{2,3},{3,2},{4,5},{5,4},{6,7},{7,6},{8,9},{9,8},{10,11... | collective-permute-start | bytes 393224 | tf_op jit(solution)/shard_map/ppermute | solution.py:178
  43.5 7.3 %collective-permute-start.2 = (bf16[512,128]{1,0:T(8,128)(2,1)S(1)}, bf16[512,128]{1,0:T(8,128)(2,1)S(1)}, u32[]{:S(2)}, u32[]{:S(2)}) collective-permute-start(bf16[512,128]{1,0:T(8,128)(2,1)S(1)} %get-tuple-element.24.mine_ref), channel_id=1, source_target_pairs={{0,1},{1,0},{2,3},{3,2},{4,5},{5,4},{6,7},{7,6},{8,9},{9,8},{10,11... | collective-permute-start | bytes 393224 | tf_op jit(solution)/shard_map/ppermute | solution.py:178
  50.8 5.7 %collective-permute-start.3 = (f32[2048,128]{1,0:T(8,128)S(1)}, f32[2048,128]{1,0:T(8,128)S(1)}, u32[]{:S(2)}, u32[]{:S(2)}) collective-permute-start(f32[2048,128]{1,0:T(8,128)S(1)} %shard_map.76), channel_id=1, source_target_pairs={{0,4},{4,0},{1,5},{5,1},{2,6},{6,2},{3,7},{7,3},{8,12},{12,8},{9,1... | collective-permute-start | bytes 3145736 | tf_op jit(solution)/shard_map/ppermute | solution.py:183
  57.5 26.3 %copy-start.4 = (s32[800]{0:T(1024)S(1)}, s32[800]{0:T(1024)}, u32[]{:S(2)}) copy-start(s32[800]{0:T(1024)} %virt_ref.3) | copy-start | bytes 9604
  57.5 26.3 %copy-start.5 = (bf16[1,3200]{1,0:T(2,128)(2,1)S(1)}, bf16[1,3200]{1,0:T(2,128)(2,1)}, u32[]{:S(2)}) copy-start(bf16[1,3200]{1,0:T(2,128)(2,1)} %old_ref.1) | copy-start | bytes 19204
  57.5 26.3 %copy-start.7 = (s32[4]{0:T(128)S(1)}, s32[4]{0:T(128)}, u32[]{:S(2)}) copy-start(s32[4]{0:T(128)} %upper_ref.3) | copy-start | bytes 52
  57.5 26.2 %all-to-all-start.1 = ((f16[128,16,128]{2,1,0:T(8,128)(2,1)}), f16[128,16,128]{2,1,0:T(8,128)(2,1)S(1)}, u32[]{:S(2)}, u32[]{:S(2)}) async-start(f16[128,16,128]{2,1,0:T(8,128)(2,1)} %bitcast.6), calls=%async_computation.1 | async-start | bytes 1048576 | tf_op jit(solution)/shard_map/all_to_all | solution.py:186

commit v5 on v4

v5 whole, which is shorter than its diff:
```python
import functools

import jax
import jax.numpy as jnp
from jax import lax
from jax.experimental import pallas as pl
from jax.experimental.pallas import tpu as pltpu
from jax.sharding import Mesh
from jax.sharding import PartitionSpec as P

AXES = ("z", "y", "core", "x1", "x0")
BF16, F32, F16 = jnp.bfloat16, jnp.float32, jnp.float16
NV = 800
LANES = 128
TILES = 7
WIDE = TILES * LANES
SCALE = 64.0

VMEM = pl.BlockSpec(memory_space=pltpu.VMEM)
SMEM = pl.BlockSpec(memory_space=pltpu.SMEM)


def call(body, out, ins, flops, nbytes, scratch=()):
    return pl.pallas_call(
        body,
        out_shape=out,
        in_specs=[SMEM if kind == "s" else VMEM for kind in ins],
        out_specs=jax.tree.map(lambda _: VMEM, out),
        scratch_shapes=list(scratch),
        compiler_params=pltpu.CompilerParams(vmem_limit_bytes=16 * 1024 * 1024),
        cost_estimate=pl.CostEstimate(flops=flops, bytes_accessed=nbytes, transcendentals=0),
    )


def cut_body(steps, pair_ref, row_ref, out_ref, pair, row, cut, pair_sem, in_sems, out_sems):
    lanes, slabs = row.shape[1] // steps, cut.shape[0] // steps

    def fetch(i):
        part = pl.ds(i * lanes, lanes)
        return pltpu.make_async_copy(row_ref.at[:, part], row.at[:, part], in_sems.at[i])

    def put(i):
        part = pl.ds(i * slabs, slabs)
        return pltpu.make_async_copy(cut.at[part], out_ref.at[part], out_sems.at[i])

    label = pltpu.make_async_copy(pair_ref, pair, pair_sem)
    label.start()

    def four(q, carry):
        for r in range(4):
            at = [pl.multiple_of(q * 3200 + (6 * r + t) * LANES, LANES) for t in range(TILES)]
            tiles = [row[:, pl.ds(a, LANES)].astype(F32) for a in at]
            cut[4 * q + r] = jnp.concatenate(tiles + [filler], axis=0).astype(BF16)
        return carry

    for i in range(steps):
        fetch(i).start()
    label.wait()
    filler = jnp.full((1, LANES), pair[0].astype(F32))
    for i in range(steps):
        fetch(i).wait()
        lax.fori_loop(i * slabs // 4, (i + 1) * slabs // 4, four, 0, unroll=4)
        put(i).start()
    for i in range(steps):
        put(i).wait()


def put_tiles(sums, count, out_ref, first, step):
    wide = jnp.concatenate([sums, jnp.zeros((count, WIDE - NV), F32)], axis=1)
    for t in range(TILES):
        out_ref[pl.ds(first + t, count, stride=step), :] = wide[:, t * LANES : (t + 1) * LANES]
    out_ref[pl.ds(first + TILES, count, stride=step), :] = jnp.zeros((count, LANES), F32)


def kept_rows(flip, zy, places_ref, slab_ref, virt_ref, tiles_ref, flat, wide, lhs_ref, first):
    c = jnp.bitwise_xor(places_ref[3], flip)
    flat[...] = tiles_ref[:, jnp.bitwise_xor(places_ref[0], flip)].astype(F32).reshape(zy * 8, LANES)
    for t in range(TILES):
        wide[:, t * LANES : (t + 1) * LANES] = flat[pl.ds(t, zy, stride=8), :]
    pair = flat[pl.ds(TILES, zy, stride=8), :][:, 0:1]
    cd = jnp.bitwise_xor(virt_ref[...].reshape(1, NV), slab_ref[c]).astype(F32)
    for shift in range(4):

        @pl.when(c % 4 == shift)
        def _():
            row = wide[:, 32 * shift : 32 * shift + NV]
            lhs_ref[pl.ds(first, zy), :] = jnp.where(pair == cd, row, 0.0).astype(BF16)


def rows_body(zy, places_ref, slab_ref, virt_ref, tiles_ref, own_ref, lhs_ref, out_ref, flat, wide):
    kept_rows(0, zy, places_ref, slab_ref, virt_ref, tiles_ref, flat, wide, lhs_ref, 0)
    out_ref[...] = jnp.dot(lhs_ref[...], own_ref[...], preferred_element_type=F32)


def ordered(zy, places_ref, mine, there, rows):
    place = pl.multiple_of(places_ref[1] * zy, zy)
    rows[pl.ds(place, zy), :] = mine
    rows[pl.ds(pl.multiple_of(zy - place, zy), zy), :] = there


def other_body(zy, *refs):
    places_ref, slab_ref, virt_ref, mine_ref, there_ref, own_ref, sums_ref, sums2_ref = refs[:8]
    lhs_ref, out_ref, flat, wide, own_sums = refs[8:]
    place = pl.multiple_of(places_ref[1] * zy, zy)
    kept_rows(1, zy, places_ref, slab_ref, virt_ref, mine_ref, flat, wide, lhs_ref, place)
    there = pl.multiple_of(zy - place, zy)
    kept_rows(1, zy, places_ref, slab_ref, virt_ref, there_ref, flat, wide, lhs_ref, there)
    ordered(zy, places_ref, sums_ref[...], sums2_ref[...], own_sums)
    sums = own_sums[...] + jnp.dot(lhs_ref[...], own_ref[...], preferred_element_type=F32)
    put_tiles(sums, 2 * zy, out_ref, 0, 8)


def partner_body(zy, places_ref, mine_ref, there_ref, block_ref, out_ref, rows):
    ordered(zy, places_ref, mine_ref[...], there_ref[...], rows)
    out_ref[...] = jnp.dot(rows[...], block_ref[...], preferred_element_type=F32)


def ladder_body(zy, lhs_ref, block_ref, sums_ref, own_ref, out_ref):
    sums = sums_ref[...] + jnp.dot(lhs_ref[...], block_ref[...], preferred_element_type=F32)
    put_tiles(sums, 2 * zy, out_ref, 8, 16)
    for t in range(8):
        out_ref[pl.ds(t, 2 * zy, stride=16), :] = own_ref[pl.ds(t, 2 * zy, stride=8), :]


def finish_body(places_ref, pair_ref, upper_ref, sums_ref, virt_ref, old_ref, out_ref):
    swap = places_ref[2] == 1
    pair = pair_ref[0]
    order = ((0, 0), (1, 0), (1, 1), (0, 1))
    virt = virt_ref[...].reshape(1, NV)
    for a in range(4):
        s, h = order[a]
        s2, h2 = order[(a + 2) % 4]
        straight = sums_ref[s, 8 * h : 8 * h + 8, :]
        turned = sums_ref[s2, 8 * h2 : 8 * h2 + 8, :]
        tiles = jnp.where(swap, turned, straight) * (1.0 / SCALE)
        row = jnp.concatenate([tiles[t : t + 1, :] for t in range(TILES)], axis=1)[:, :NV]
        ab = jnp.bitwise_xor(virt, upper_ref[a])
        row = jnp.where(ab == pair, row, 0.0)
        old = old_ref[:, a * NV : (a + 1) * NV].astype(F32)
        out_ref[:, a * NV : (a + 1) * NV] = (old + row).astype(BF16)


def per_device(amplitudes, integrals, residual_in, pair_irrep, slab_irrep, upper_irrep, virt_irrep):
    core = lax.axis_index("core")
    x1 = lax.axis_index("x1")
    x0 = lax.axis_index("x0")
    slab = lax.axis_index(("z", "y", "core"))
    zy = lax.axis_size("z") * lax.axis_size("y")
    shape = jax.ShapeDtypeStruct
    places = jnp.stack([core, x0, x1, slab])

    other_core, other_x0 = [(0, 1), (1, 0)], [(0, 1), (1, 0)]

    partner = lax.ppermute(integrals, ("x1", "x0"), [(0, 3), (3, 0), (1, 2), (2, 1)])

    steps = 4
    cut = pl.pallas_call(
        functools.partial(cut_body, steps),
        in_specs=[pl.BlockSpec(memory_space=pl.ANY)] * 2,
        out_specs=pl.BlockSpec(memory_space=pl.ANY),
        out_shape=shape((2 * zy, 8, LANES), BF16),
        scratch_shapes=[
            pltpu.SMEM(pair_irrep.shape, jnp.int32),
            pltpu.VMEM(amplitudes.shape, BF16),
            pltpu.VMEM((2 * zy, 8, LANES), BF16),
            pltpu.SemaphoreType.DMA,
            pltpu.SemaphoreType.DMA((steps,)),
            pltpu.SemaphoreType.DMA((steps,)),
        ],
        cost_estimate=pl.CostEstimate(flops=0, bytes_accessed=700000, transcendentals=0),
    )(pair_irrep, amplitudes)
    cut, block = lax.optimization_barrier((cut, integrals))
    mine = lax.all_to_all(cut.reshape(zy, 16, LANES), ("z", "y"), 0, 0, tiled=True)
    mine = mine.reshape(zy, 2, 8, LANES)
    there = lax.ppermute(mine, "x0", other_x0)

    rows_f32, rows_bf16 = pltpu.VMEM((zy, WIDE), F32), shape((2 * zy, NV), BF16)
    flat, all_f32 = pltpu.VMEM((zy * 8, LANES), F32), shape((2 * zy, NV), F32)

    def rows(tiles, nbytes):
        out = [shape((zy, NV), BF16), shape((zy, NV), F32)]
        body = functools.partial(rows_body, zy)
        return call(body, out, "ssvvv", nbytes * 300, nbytes, [flat, rows_f32])(
            places, slab_irrep, virt_irrep, tiles, integrals
        )

    lhs_here, sums_here = rows(mine, 3000000)
    block2 = lax.ppermute(block, "core", other_core)
    partner, sums_here = lax.optimization_barrier((partner, sums_here))
    partner2 = lax.ppermute(partner, "core", other_core)
    lhs_there, sums_there = rows(there, 20000000)
    other = call(
        functools.partial(other_body, zy),
        [rows_bf16, shape((2 * zy * 8, LANES), F32)],
        "ssvvvvvv",
        1000,
        3000000,
        [flat, rows_f32, pltpu.VMEM((2 * zy, NV), F32)],
    )
    lhs2, own_sums = other(places, slab_irrep, virt_irrep, mine, there, block2, sums_here, sums_there)
    first = call(
        functools.partial(partner_body, zy), all_f32, "svvv", 6000000000, 20000000, [pltpu.VMEM((2 * zy, NV), BF16)]
    )
    ladder = call(
        functools.partial(ladder_body, zy), shape((2 * zy * 16, LANES), F32), "vvvv", 1000, 3000000
    )
    part = ladder(lhs2, partner2, first(places, lhs_here, lhs_there, partner), own_sums)
    part = (part * SCALE).astype(F16).reshape(2 * zy, 16, LANES)
    back = lax.all_to_all(part, ("x0", "z", "y"), 0, 0, tiled=True)
    sums = jnp.sum(back.reshape(2, zy, 16, LANES).astype(F32), axis=1)
    finish = call(finish_body, shape((1, 4 * NV), BF16), "sssvvv", 0, 50000)
    return finish(places, pair_irrep, upper_irrep, sums, virt_irrep, residual_in)


def solution(mesh):
    fine = Mesh(mesh.devices.reshape(8, 8, 2, 2, 2), AXES)
    return jax.shard_map(
        per_device,
        mesh=fine,
        in_specs=(P(AXES, None), P(AXES[:3], AXES[3:]), P(AXES, None), P(AXES), P(), P(), P()),
        out_specs=P(AXES, None),
        check_vma=False,
    )
```

time: 85.8 us -> 84.6 us (0.986)
  the two profiles are of different devices: /device:TPU:1 before, /device:TPU:4 now
where the time goes in v5:
time: 84.6 us; the launch traced here: 84.2 us
  blocking collectives  32.9 us (39%)
  starting transfers between devices  25.9 us (31%)
  waiting for transfers between devices  12.8 us (15%)
  Pallas kernels  8.78 us (10%)
  local copies, waits for them, and re-layouts  2.72 us (3%)
    all_to_all x1, blocking collectives, per_device(): back = lax.all_to_all(part, ('x0', 'z', 'y'), 0, 0, tiled=True)  32.9 us
    all_to_all x1, starting transfers between devices, per_device(): lax.all_to_all(cut.reshape(zy, 16, LANES), ('z', 'y'), 0, 0, tiled=True)  16.6 us
    all_to_all x1, waiting for transfers between devices, per_device(): lax.all_to_all(cut.reshape(zy, 16, LANES), ('z', 'y'), 0, 0, tiled=True)  12.8 us
    ppermute x1, starting transfers between devices, per_device(): there = lax.ppermute(mine, 'x0', other_x0)  3.04 us
    unnamed x14, local copies, waits for them, and re-layouts  2.72 us
    ppermute x1, starting transfers between devices, per_device(): lax.ppermute(integrals, ('x1', 'x0'), [(0, 3), (3, 0), (1, 2), (2, 1)])  2.43 us
    pallas_call x1, Pallas kernels, per_device(): pl.pallas_call(functools.partial(cut_body, steps), in_specs=[pl.BlockSpec...  2.34 us
    pallas_call x2, Pallas kernels, rows(): call(body, out, 'ssvvv', nbytes * 300, nbytes, [flat, rows_f32])  2.14 us
  transfers between devices with their start and end apart: 5, of which 1 were waited for; matrix products, arithmetic and copies ran while one was open for 0% of the time, Pallas kernels for 8%

profile of v5, /device:TPU:4, one launch (start us, length us, event | category | flops | bytes accessed | tf_op | source)
XLA Modules:
  0.0 84.2 jit_solution(12068022172169161482)
XLA Ops:
  0.0 2.4 %collective-permute-start.2 = (bf16[800,800]{1,0:T(8,128)(2,1)}, bf16[800,800]{1,0:T(8,128)(2,1)S(1)}, u32[]{:S(2)}, u32[]{:S(2)}) collective-permute-start(bf16[800,800]{1,0:T(8,128)(2,1)} %own_ref.3), channel_id=1, source_target_pairs={{0,3},{3,0},{1,2},{2,1},{4,7},{7,4},{5,6},{6,5},{8,11},{11,8},{9,1... | collective-permute-start | bytes 3840008 | tf_op jit(solution)/shard_map/ppermute | solution.py:154
  3.1 2.3 %shard_map.73 = bf16[128,8,128]{2,1,0:T(8,128)(2,1)} custom-call(s32[1]{0:T(128)S(6)} %copy.8.pair_ref, bf16[1,102400]{1,0:T(2,128)(2,1)} %row_ref.1), custom_call_target="tpu_custom_call" | custom-call | bytes 700000 | tf_op jit(solution)/shard_map/pallas_call | solution.py:157
  5.4 16.6 %all-to-all-start = ((bf16[64,16,128]{2,1,0:T(8,128)(2,1)}), bf16[64,16,128]{2,1,0:T(8,128)(2,1)S(1)}, u32[]{:S(2)}, u32[]{:S(2)}) async-start(bf16[64,16,128]{2,1,0:T(8,128)(2,1)} %bitcast.14), calls=%async_computation | async-start | bytes 524288 | tf_op jit(solution)/shard_map/all_to_all | solution.py:173
  22.0 1.9 %collective-permute-start.1 = (bf16[800,800]{1,0:T(8,128)(2,1)}, bf16[800,800]{1,0:T(8,128)(2,1)S(1)}, u32[]{:S(2)}, u32[]{:S(2)}) collective-permute-start(bf16[800,800]{1,0:T(8,128)(2,1)} %own_ref.3), channel_id=1, source_target_pairs={{0,4},{4,0},{1,5},{5,1},{2,6},{6,2},{3,7},{7,3},{8,12},{12,8},{9,1... | collective-permute-start | bytes 3840008 | tf_op jit(solution)/shard_map/ppermute | solution.py:188
  24.0 12.8 %all-to-all-done = bf16[64,16,128]{2,1,0:T(8,128)(2,1)S(1)} async-done(((bf16[64,16,128]{2,1,0:T(8,128)(2,1)}), bf16[64,16,128]{2,1,0:T(8,128)(2,1)S(1)}, u32[]{:S(2)}, u32[]{:S(2)}) %all-to-all-start) | async-done | bytes 262176 | tf_op jit(solution)/shard_map/all_to_all | solution.py:173
  36.7 3.0 %collective-permute-start = (bf16[64,2,8,128]{3,2,1,0:T(8,128)(2,1)S(1)}, bf16[64,2,8,128]{3,2,1,0:T(8,128)(2,1)S(1)}, u32[]{:S(2)}, u32[]{:S(2)}) collective-permute-start(bf16[64,2,8,128]{3,2,1,0:T(8,128)(2,1)S(1)} %bitcast.10), channel_id=1, source_target_pairs={{0,1},{1,0},{2,3},{3,2},{4,5},{5,4},{6,7},{7,6},{8,9},{9,8},{10,11... | collective-permute-start | bytes 786440 | tf_op jit(solution)/shard_map/ppermute | solution.py:175
  39.8 0.1 pad_add_fusion.places_ref.refs_0_
  39.9 0.0 copy-start
  39.9 0.7 copy-done
  40.6 0.0 copy-start.3
  40.6 0.7 copy-done.3
  41.2 0.0 copy-start.6
  41.2 1.4 %copy-done.6 = bf16[800,800]{1,0:T(8,128)(2,1)S(1)} copy-done((bf16[800,800]{1,0:T(8,128)(2,1)S(1)}, bf16[800,800]{1,0:T(8,128)(2,1)}, u32[]{:S(2)}) %copy-start.6) | copy-done | bytes 1280024
  42.6 0.0 copy-start.1
  42.6 0.0 copy-start.4
  42.6 1.1 %shard_map.74 = (bf16[64,800]{1,0:T(8,128)(2,1)S(1)}, f32[64,800]{1,0:T(8,128)S(1)}) custom-call(s32[4]{0:T(128)S(1)} %pad_add_fusion.places_ref.refs_0_, s32[128]{0:T(128)S(1)} %copy-done.3, s32[800]{0:T(1024)S(1)} %copy-done, bf16[64,2,8,128]{3,2,1,0:T(8,128)(2,1)S(1)} %bitcast.11, bf16[800,800]{1,0:T(8,128)(2,1)S(1)} %copy-done.6), custom_call_target="tpu_custom_call" | custom-call | flops 900000000 | bytes 3000000 | tf_op jit(solution)/shard_map/pallas_call | solution.py:183
  43.7 0.0 collective-permute-done.2.block_ref
  43.7 1.9 %collective-permute-start.3 = (bf16[800,800]{1,0:T(8,128)(2,1)S(1)}, bf16[800,800]{1,0:T(8,128)(2,1)S(1)}, u32[]{:S(2)}, u32[]{:S(2)}) collective-permute-start(bf16[800,800]{1,0:T(8,128)(2,1)S(1)} %collective-permute-done.2.block_ref), channel_id=1, source_target_pairs={{0,4},{4,0},{1,5},{5,1},{2,6},{6,2},{3,7},{7,3},{8,12},{12,8},{9,1... | collective-permute-start | bytes 3840008 | tf_op jit(solution)/shard_map/ppermute | solution.py:190
  45.6 0.0 collective-permute-done.tiles_ref.refs_4_
  45.6 0.0 copy-done.1
  45.6 0.0 copy-done.4
  45.6 1.1 %shard_map.75 = (bf16[64,800]{1,0:T(8,128)(2,1)S(1)}, f32[64,800]{1,0:T(8,128)S(1)}) custom-call(s32[4]{0:T(128)S(1)} %pad_add_fusion.places_ref.refs_0_, s32[128]{0:T(128)S(1)} %copy-done.4, s32[800]{0:T(1024)S(1)} %copy-done.1, bf16[64,2,8,128]{3,2,1,0:T(8,128)(2,1)S(1)} %collective-permute-done.tiles_ref.refs_4_, bf16[800,800]{1,0:T(8,128)(2,1)S(1)} %copy-done.6), custom_call_target="tpu_custom_call" | custom-call | flops 6000000000 | bytes 20000000 | tf_op jit(solution)/shard_map/pallas_call | solution.py:183
  46.7 0.0 collective-permute-done.1.refs_5_
  46.7 1.4 %shard_map.76 = (bf16[128,800]{1,0:T(8,128)(2,1)S(1)}, f32[1024,128]{1,0:T(8,128)S(1)}) custom-call(s32[4]{0:T(128)S(1)} %pad_add_fusion.places_ref.refs_0_, s32[128]{0:T(128)S(1)} %copy-done.4, s32[800]{0:T(1024)S(1)} %copy-done.1, bf16[64,2,8,128]{3,2,1,0:T(8,128)(2,1)S(1)} %bitcast.12, bf16[64,2,8,128]{3,2,1,0:T(8,128)(2,1)S(1)} %collective-permute-done.tiles_ref.refs_4_, ...), custom_call_target="tpu_custom_call" | custom-call | flops 1000 | bytes 3000000 | tf_op jit(solution)/shard_map/pallas_call | solution.py:200
  48.1 1.0 %shard_map.77.sums_ref = f32[128,800]{1,0:T(8,128)S(1)} custom-call(s32[4]{0:T(128)S(1)} %pad_add_fusion.places_ref.refs_0_, bf16[64,800]{1,0:T(8,128)(2,1)S(1)} %get-tuple-element.22.mine_ref, bf16[64,800]{1,0:T(8,128)(2,1)S(1)} %get-tuple-element.23.there_ref, bf16[800,800]{1,0:T(8,128)(2,1)S(1)} %collective-permute-done.2.block_ref), custom_call_target="tpu_custom_call" | custom-call | flops 6000000000 | bytes 20000000 | tf_op jit(solution)/shard_map/pallas_call | solution.py:207
  49.1 0.0 collective-permute-done.3.block_ref
  49.1 0.7 shard_map.78
  49.8 0.0 copy-start.2
  49.8 0.0 copy-start.5
  49.8 0.1 multiply_convert_fusion
  49.9 32.9 %all_to_all.10 = f16[128,16,128]{2,1,0:T(8,128)(2,1)S(1)} all-to-all(f16[128,16,128]{2,1,0:T(8,128)(2,1)S(1)} %bitcast.13), channel_id=1, replica_groups=mesh['z'=8,'y'=8,'core'=2,'x1'=2,'x0'=2] {'x0','z','y'}, dimensions={0} | all-to-all | bytes 1048576 | tf_op jit(solution)/shard_map/all_to_all | solution.py:209
  82.8 0.1 convert_reduce_fusion.sums_ref
  82.9 0.0 copy-done.2
  82.9 0.0 copy-done.5
  82.9 1.3 %shard_map.79 = bf16[1,3200]{1,0:T(2,128)(2,1)} custom-call(s32[4]{0:T(128)S(1)} %pad_add_fusion.places_ref.refs_0_, s32[1]{0:T(128)S(6)} %copy.8.pair_ref, s32[4]{0:T(128)S(1)} %copy-done.5, f32[2,16,128]{2,1,0:T(8,128)S(1)} %convert_reduce_fusion.sums_ref, s32[800]{0:T(1024)S(1)} %copy-done.1, bf16[1,3200]{1,0:T(2,128)(2,1)S(1)} %copy-done.2), custom_call_target="tpu_custom_call" | custom-call | bytes 50000 | tf_op jit(solution)/shard_map/pallas_call | solution.py:212
Async XLA Ops:
  0.0 43.7 %collective-permute-start.2 = (bf16[800,800]{1,0:T(8,128)(2,1)}, bf16[800,800]{1,0:T(8,128)(2,1)S(1)}, u32[]{:S(2)}, u32[]{:S(2)}) collective-permute-start(bf16[800,800]{1,0:T(8,128)(2,1)} %own_ref.3), channel_id=1, source_target_pairs={{0,3},{3,0},{1,2},{2,1},{4,7},{7,4},{5,6},{6,5},{8,11},{11,8},{9,1... | collective-permute-start | bytes 3840008 | tf_op jit(solution)/shard_map/ppermute | solution.py:154
  5.4 31.3 %all-to-all-start = ((bf16[64,16,128]{2,1,0:T(8,128)(2,1)}), bf16[64,16,128]{2,1,0:T(8,128)(2,1)S(1)}, u32[]{:S(2)}, u32[]{:S(2)}) async-start(bf16[64,16,128]{2,1,0:T(8,128)(2,1)} %bitcast.14), calls=%async_computation | async-start | bytes 524288 | tf_op jit(solution)/shard_map/all_to_all | solution.py:173
  22.0 24.7 %collective-permute-start.1 = (bf16[800,800]{1,0:T(8,128)(2,1)}, bf16[800,800]{1,0:T(8,128)(2,1)S(1)}, u32[]{:S(2)}, u32[]{:S(2)}) collective-permute-start(bf16[800,800]{1,0:T(8,128)(2,1)} %own_ref.3), channel_id=1, source_target_pairs={{0,4},{4,0},{1,5},{5,1},{2,6},{6,2},{3,7},{7,3},{8,12},{12,8},{9,1... | collective-permute-start | bytes 3840008 | tf_op jit(solution)/shard_map/ppermute | solution.py:188
  36.7 8.9 %collective-permute-start = (bf16[64,2,8,128]{3,2,1,0:T(8,128)(2,1)S(1)}, bf16[64,2,8,128]{3,2,1,0:T(8,128)(2,1)S(1)}, u32[]{:S(2)}, u32[]{:S(2)}) collective-permute-start(bf16[64,2,8,128]{3,2,1,0:T(8,128)(2,1)S(1)} %bitcast.10), channel_id=1, source_target_pairs={{0,1},{1,0},{2,3},{3,2},{4,5},{5,4},{6,7},{7,6},{8,9},{9,8},{10,11... | collective-permute-start | bytes 786440 | tf_op jit(solution)/shard_map/ppermute | solution.py:175
  39.9 0.7 copy-start
  40.6 0.7 copy-start.3
  41.2 1.4 %copy-start.6 = (bf16[800,800]{1,0:T(8,128)(2,1)S(1)}, bf16[800,800]{1,0:T(8,128)(2,1)}, u32[]{:S(2)}) copy-start(bf16[800,800]{1,0:T(8,128)(2,1)} %own_ref.3) | copy-start | bytes 3840004
  42.6 3.0 %copy-start.1 = (s32[800]{0:T(1024)S(1)}, s32[800]{0:T(1024)}, u32[]{:S(2)}) copy-start(s32[800]{0:T(1024)} %virt_ref.5) | copy-start | bytes 9604
  42.6 3.0 %copy-start.4 = (s32[128]{0:T(128)S(1)}, s32[128]{0:T(128)}, u32[]{:S(2)}) copy-start(s32[128]{0:T(128)} %refs_1_.1) | copy-start | bytes 1540
  43.7 5.4 %collective-permute-start.3 = (bf16[800,800]{1,0:T(8,128)(2,1)S(1)}, bf16[800,800]{1,0:T(8,128)(2,1)S(1)}, u32[]{:S(2)}, u32[]{:S(2)}) collective-permute-start(bf16[800,800]{1,0:T(8,128)(2,1)S(1)} %collective-permute-done.2.block_ref), channel_id=1, source_target_pairs={{0,4},{4,0},{1,5},{5,1},{2,6},{6,2},{3,7},{7,3},{8,12},{12,8},{9,1... | collective-permute-start | bytes 3840008 | tf_op jit(solution)/shard_map/ppermute | solution.py:190
  49.8 33.1 %copy-start.2 = (bf16[1,3200]{1,0:T(2,128)(2,1)S(1)}, bf16[1,3200]{1,0:T(2,128)(2,1)}, u32[]{:S(2)}) copy-start(bf16[1,3200]{1,0:T(2,128)(2,1)} %old_ref.1) | copy-start | bytes 19204
  49.8 33.1 %copy-start.5 = (s32[4]{0:T(128)S(1)}, s32[4]{0:T(128)}, u32[]{:S(2)}) copy-start(s32[4]{0:T(128)} %upper_ref.1) | copy-start | bytes 52

commit v6 on v5

--- a/solution.py
+++ b/solution.py
@@ -87,31 +87,27 @@
             lhs_ref[pl.ds(first, zy), :] = jnp.where(pair == cd, row, 0.0).astype(BF16)
 
 
-def rows_body(zy, places_ref, slab_ref, virt_ref, tiles_ref, own_ref, lhs_ref, out_ref, flat, wide):
+def rows_body(zy, places_ref, slab_ref, virt_ref, tiles_ref, own_ref, lhs_ref, lhs2_ref, out_ref, flat, wide):
     kept_rows(0, zy, places_ref, slab_ref, virt_ref, tiles_ref, flat, wide, lhs_ref, 0)
     out_ref[...] = jnp.dot(lhs_ref[...], own_ref[...], preferred_element_type=F32)
-
-
-def ordered(zy, places_ref, mine, there, rows):
-    place = pl.multiple_of(places_ref[1] * zy, zy)
-    rows[pl.ds(place, zy), :] = mine
-    rows[pl.ds(pl.multiple_of(zy - place, zy), zy), :] = there
-
-
-def other_body(zy, *refs):
-    places_ref, slab_ref, virt_ref, mine_ref, there_ref, own_ref, sums_ref, sums2_ref = refs[:8]
-    lhs_ref, out_ref, flat, wide, own_sums = refs[8:]
-    place = pl.multiple_of(places_ref[1] * zy, zy)
-    kept_rows(1, zy, places_ref, slab_ref, virt_ref, mine_ref, flat, wide, lhs_ref, place)
-    there = pl.multiple_of(zy - place, zy)
-    kept_rows(1, zy, places_ref, slab_ref, virt_ref, there_ref, flat, wide, lhs_ref, there)
-    ordered(zy, places_ref, sums_ref[...], sums2_ref[...], own_sums)
-    sums = own_sums[...] + jnp.dot(lhs_ref[...], own_ref[...], preferred_element_type=F32)
-    put_tiles(sums, 2 * zy, out_ref, 0, 8)
-
-
-def partner_body(zy, places_ref, mine_ref, there_ref, block_ref, out_ref, rows):
-    ordered(zy, places_ref, mine_ref[...], there_ref[...], rows)
+    kept_rows(1, zy, places_ref, slab_ref, virt_ref, tiles_ref, flat, wide, lhs2_ref, 0)
+
+
+def there_body(zy, *refs):
+    places_ref, slab_ref, virt_ref, tiles_ref, lhs_ref, lhs2_ref, sums_ref = refs[:7]
+    own_ref, own2_ref, block_ref = refs[7:10]
+    rows2_ref, own_sums_ref, out_ref, flat, wide, rows, sums = refs[10:]
+    here = pl.multiple_of(places_ref[1] * zy, zy)
+    there = pl.multiple_of(zy - here, zy)
+    rows[pl.ds(here, zy), :] = lhs_ref[...]
+    rows2_ref[pl.ds(here, zy), :] = lhs2_ref[...]
+    sums[pl.ds(here, zy), :] = sums_ref[...]
+    kept_rows(0, zy, places_ref, slab_ref, virt_ref, tiles_ref, flat, wide, rows, there)
+    kept_rows(1, zy, places_ref, slab_ref, virt_ref, tiles_ref, flat, wide, rows2_ref, there)
+    own = jnp.dot(rows[pl.ds(there, zy), :], own_ref[...], preferred_element_type=F32)
+    sums[pl.ds(there, zy), :] = own
+    own = sums[...] + jnp.dot(rows2_ref[...], own2_ref[...], preferred_element_type=F32)
+    put_tiles(own, 2 * zy, own_sums_ref, 0, 8)
     out_ref[...] = jnp.dot(rows[...], block_ref[...], preferred_element_type=F32)
 
 
@@ -122,11 +118,9 @@
         out_ref[pl.ds(t, 2 * zy, stride=16), :] = own_ref[pl.ds(t, 2 * zy, stride=8), :]
 
 
-def finish_body(places_ref, pair_ref, upper_ref, sums_ref, virt_ref, old_ref, out_ref):
+def finish_body(places_ref, sums_ref, kept_ref, old_ref, out_ref):
     swap = places_ref[2] == 1
-    pair = pair_ref[0]
     order = ((0, 0), (1, 0), (1, 1), (0, 1))
-    virt = virt_ref[...].reshape(1, NV)
     for a in range(4):
         s, h = order[a]
         s2, h2 = order[(a + 2) % 4]
@@ -134,8 +128,7 @@
         turned = sums_ref[s2, 8 * h2 : 8 * h2 + 8, :]
         tiles = jnp.where(swap, turned, straight) * (1.0 / SCALE)
         row = jnp.concatenate([tiles[t : t + 1, :] for t in range(TILES)], axis=1)[:, :NV]
-        ab = jnp.bitwise_xor(virt, upper_ref[a])
-        row = jnp.where(ab == pair, row, 0.0)
+        row = jnp.where(kept_ref[a : a + 1, :] > 0.5, row, 0.0)
         old = old_ref[:, a * NV : (a + 1) * NV].astype(F32)
         out_ref[:, a * NV : (a + 1) * NV] = (old + row).astype(BF16)
 
@@ -156,8 +149,8 @@
     steps = 4
     cut = pl.pallas_call(
         functools.partial(cut_body, steps),
-        in_specs=[pl.BlockSpec(memory_space=pl.ANY)] * 2,
-        out_specs=pl.BlockSpec(memory_space=pl.ANY),
+        in_specs=[pl.BlockSpec(memory_space=pltpu.HBM)] * 2,
+        out_specs=pl.BlockSpec(memory_space=pltpu.HBM),
         out_shape=shape((2 * zy, 8, LANES), BF16),
         scratch_shapes=[
             pltpu.SMEM(pair_irrep.shape, jnp.int32),
@@ -174,42 +167,43 @@
     mine = mine.reshape(zy, 2, 8, LANES)
     there = lax.ppermute(mine, "x0", other_x0)
 
-    rows_f32, rows_bf16 = pltpu.VMEM((zy, WIDE), F32), shape((2 * zy, NV), BF16)
-    flat, all_f32 = pltpu.VMEM((zy * 8, LANES), F32), shape((2 * zy, NV), F32)
-
-    def rows(tiles, nbytes):
-        out = [shape((zy, NV), BF16), shape((zy, NV), F32)]
-        body = functools.partial(rows_body, zy)
-        return call(body, out, "ssvvv", nbytes * 300, nbytes, [flat, rows_f32])(
-            places, slab_irrep, virt_irrep, tiles, integrals
-        )
-
-    lhs_here, sums_here = rows(mine, 3000000)
+    flat, wide = pltpu.VMEM((zy * 8, LANES), F32), pltpu.VMEM((zy, WIDE), F32)
+    half, whole = shape((zy, NV), BF16), shape((2 * zy, NV), BF16)
+    rows = call(
+        functools.partial(rows_body, zy),
+        [half, half, shape((zy, NV), F32)],
+        "ssvvv",
+        24000000 * 300,
+        24000000,
+        [flat, wide],
+    )
+    lhs, lhs2, sums = rows(places, slab_irrep, virt_irrep, mine, integrals)
     block2 = lax.ppermute(block, "core", other_core)
-    partner, sums_here = lax.optimization_barrier((partner, sums_here))
+    partner, sums = lax.optimization_barrier((partner, sums))
     partner2 = lax.ppermute(partner, "core", other_core)
-    lhs_there, sums_there = rows(there, 20000000)
-    other = call(
-        functools.partial(other_body, zy),
-        [rows_bf16, shape((2 * zy * 8, LANES), F32)],
-        "ssvvvvvv",
-        1000,
-        3000000,
-        [flat, rows_f32, pltpu.VMEM((2 * zy, NV), F32)],
-    )
-    lhs2, own_sums = other(places, slab_irrep, virt_irrep, mine, there, block2, sums_here, sums_there)
-    first = call(
-        functools.partial(partner_body, zy), all_f32, "svvv", 6000000000, 20000000, [pltpu.VMEM((2 * zy, NV), BF16)]
+    after = call(
+        functools.partial(there_body, zy),
+        [whole, shape((2 * zy * 8, LANES), F32), shape((2 * zy, NV), F32)],
+        "ssvvvvvvvv",
+        40000000 * 300,
+        40000000,
+        [flat, wide, pltpu.VMEM((2 * zy, NV), BF16), pltpu.VMEM((2 * zy, NV), F32)],
+    )
+    rows2, own_sums, sums = after(
+        places, slab_irrep, virt_irrep, there, lhs, lhs2, sums, integrals, block2, partner
     )
     ladder = call(
         functools.partial(ladder_body, zy), shape((2 * zy * 16, LANES), F32), "vvvv", 1000, 3000000
     )
-    part = ladder(lhs2, partner2, first(places, lhs_here, lhs_there, partner), own_sums)
+    part = ladder(rows2, partner2, sums, own_sums)
     part = (part * SCALE).astype(F16).reshape(2 * zy, 16, LANES)
+    part, upper = lax.optimization_barrier((part, upper_irrep))
     back = lax.all_to_all(part, ("x0", "z", "y"), 0, 0, tiled=True)
+    ab_irrep = jnp.bitwise_xor(upper[:, None], virt_irrep[None, :])
+    kept = (ab_irrep == cut[0, TILES, 0].astype(jnp.int32)).astype(F32)
     sums = jnp.sum(back.reshape(2, zy, 16, LANES).astype(F32), axis=1)
-    finish = call(finish_body, shape((1, 4 * NV), BF16), "sssvvv", 0, 50000)
-    return finish(places, pair_irrep, upper_irrep, sums, virt_irrep, residual_in)
+    finish = call(finish_body, shape((1, 4 * NV), BF16), "svvv", 0, 50000)
+    return finish(places, sums, kept, residual_in)
 
 
 def solution(mesh):

time: 84.6 us -> 84.9 us (level)
  blocking collectives: 32.9 us -> 0 us
  waiting for transfers between devices: 12.8 us -> 33.4 us
  starting transfers between devices: 25.9 us -> 37.1 us
  Pallas kernels: 8.78 us -> 7.46 us
  local copies, waits for them, and re-layouts: 2.72 us -> 3.89 us
  other arithmetic: 0.27 us -> 1.14 us
    all_to_all x1 -> x0, blocking collectives: 32.9 us -> none  [per_device(): back = lax.all_to_all(part, ('x0', 'z', 'y'), 0, 0, tiled=True)]
    all_to_all x0 -> x1, waiting for transfers between devices: none -> 19.5 us  [per_device(): back = lax.all_to_all(part, ('x0', 'z', 'y'), 0, 0, tiled=True)]
    all_to_all x0 -> x1, starting transfers between devices: none -> 11.2 us  [per_device(): back = lax.all_to_all(part, ('x0', 'z', 'y'), 0, 0, tiled=True)]
    pallas_call x6 -> x4, Pallas kernels: 6.45 us -> 5.11 us  [the longest x1 1.93 us: per_device(): after(places, slab_irrep, virt_irrep, there, lhs, lhs2, sums, integrals,...]
    ppermute x1, waiting for transfers between devices: 0.01 us -> 1.21 us  [per_device(): partner2 = lax.ppermute(partner, 'core', other_core)]
    slice x0 -> x1, local copies, waits for them, and re-layouts: none -> 1.18 us  [per_device(): kept = (ab_irrep == cut[0, TILES, 0].astype(jnp.int32)).astype(F32)]
    unnamed x14 -> x12, local copies, waits for them, and re-layouts: 2.72 us -> 2.71 us
  transfers between devices with their start and end apart: 5 -> 6, of which waited for: 1 -> 3; matrix products, arithmetic and copies ran while one was open for 0% -> 2% of each run, Pallas kernels for 8% -> 6%
where the time goes in v6:
time: 84.9 us; the launch traced here: 84.5 us
  starting transfers between devices  37.1 us (44%)
  waiting for transfers between devices  33.4 us (39%)
  Pallas kernels  7.46 us (9%)
  local copies, waits for them, and re-layouts  3.89 us (5%)
  between operations  1.48 us (2%)
  other arithmetic  1.14 us (1%)
    all_to_all x1, waiting for transfers between devices, per_device(): back = lax.all_to_all(part, ('x0', 'z', 'y'), 0, 0, tiled=True)  19.5 us
    all_to_all x1, starting transfers between devices, per_device(): lax.all_to_all(cut.reshape(zy, 16, LANES), ('z', 'y'), 0, 0, tiled=True)  16.6 us
    all_to_all x1, waiting for transfers between devices, per_device(): lax.all_to_all(cut.reshape(zy, 16, LANES), ('z', 'y'), 0, 0, tiled=True)  12.7 us
    all_to_all x1, starting transfers between devices, per_device(): back = lax.all_to_all(part, ('x0', 'z', 'y'), 0, 0, tiled=True)  11.2 us
    ppermute x1, starting transfers between devices, per_device(): there = lax.ppermute(mine, 'x0', other_x0)  3.04 us
    unnamed x12, local copies, waits for them, and re-layouts  2.71 us
    ppermute x1, starting transfers between devices, per_device(): lax.ppermute(integrals, ('x1', 'x0'), [(0, 3), (3, 0), (1, 2), (2, 1)])  2.43 us
    pallas_call x1, Pallas kernels, per_device(): pl.pallas_call(functools.partial(cut_body, steps), in_specs=[pl.BlockSpec...  2.36 us
  transfers between devices with their start and end apart: 6, of which 3 were waited for; matrix products, arithmetic and copies ran while one was open for 2% of the time, Pallas kernels for 6%

profile of v6, /device:TPU:4, one launch (start us, length us, event | category | flops | bytes accessed | tf_op | source)
XLA Modules:
  0.0 84.5 jit_solution(16107223437222119102)
XLA Ops:
  0.0 2.4 %collective-permute-start.1 = (bf16[800,800]{1,0:T(8,128)(2,1)}, bf16[800,800]{1,0:T(8,128)(2,1)S(1)}, u32[]{:S(2)}, u32[]{:S(2)}) collective-permute-start(bf16[800,800]{1,0:T(8,128)(2,1)} %refs_7_.1), channel_id=1, source_target_pairs={{0,3},{3,0},{1,2},{2,1},{4,7},{7,4},{5,6},{6,5},{8,11},{11,8},{9,1... | collective-permute-start | bytes 3840008 | tf_op jit(solution)/shard_map/ppermute | solution.py:147
  3.1 2.4 %shard_map.73 = bf16[128,8,128]{2,1,0:T(8,128)(2,1)} custom-call(s32[1]{0:T(128)S(6)} %copy.8.pair_ref, bf16[1,102400]{1,0:T(2,128)(2,1)} %row_ref.1), custom_call_target="tpu_custom_call" | custom-call | bytes 700000 | tf_op jit(solution)/shard_map/pallas_call | solution.py:150
  5.4 16.6 %all-to-all-start = ((bf16[64,16,128]{2,1,0:T(8,128)(2,1)}), bf16[64,16,128]{2,1,0:T(8,128)(2,1)S(1)}, u32[]{:S(2)}, u32[]{:S(2)}) async-start(bf16[64,16,128]{2,1,0:T(8,128)(2,1)} %bitcast.14), calls=%async_computation | async-start | bytes 524288 | tf_op jit(solution)/shard_map/all_to_all | solution.py:166
  22.1 1.9 %collective-permute-start.2 = (bf16[800,800]{1,0:T(8,128)(2,1)}, bf16[800,800]{1,0:T(8,128)(2,1)S(1)}, u32[]{:S(2)}, u32[]{:S(2)}) collective-permute-start(bf16[800,800]{1,0:T(8,128)(2,1)} %refs_7_.1), channel_id=1, source_target_pairs={{0,4},{4,0},{1,5},{5,1},{2,6},{6,2},{3,7},{7,3},{8,12},{12,8},{9,1... | collective-permute-start | bytes 3840008 | tf_op jit(solution)/shard_map/ppermute | solution.py:181
  24.0 0.1 pad_add_fusion.places_ref.refs_0_
  24.1 12.7 %all-to-all-done = bf16[64,16,128]{2,1,0:T(8,128)(2,1)S(1)} async-done(((bf16[64,16,128]{2,1,0:T(8,128)(2,1)}), bf16[64,16,128]{2,1,0:T(8,128)(2,1)S(1)}, u32[]{:S(2)}, u32[]{:S(2)}) %all-to-all-start) | async-done | bytes 262176 | tf_op jit(solution)/shard_map/all_to_all | solution.py:166
  36.8 3.0 %collective-permute-start = (bf16[64,2,8,128]{3,2,1,0:T(8,128)(2,1)S(1)}, bf16[64,2,8,128]{3,2,1,0:T(8,128)(2,1)S(1)}, u32[]{:S(2)}, u32[]{:S(2)}) collective-permute-start(bf16[64,2,8,128]{3,2,1,0:T(8,128)(2,1)S(1)} %bitcast.12), channel_id=1, source_target_pairs={{0,1},{1,0},{2,3},{3,2},{4,5},{5,4},{6,7},{7,6},{8,9},{9,8},{10,11... | collective-permute-start | bytes 786440 | tf_op jit(solution)/shard_map/ppermute | solution.py:168
  39.8 0.0 copy-start.1
  39.8 0.7 copy-done.1
  40.5 0.0 copy-start.3
  40.5 1.4 %copy-done.3 = bf16[800,800]{1,0:T(8,128)(2,1)S(1)} copy-done((bf16[800,800]{1,0:T(8,128)(2,1)S(1)}, bf16[800,800]{1,0:T(8,128)(2,1)}, u32[]{:S(2)}) %copy-start.3) | copy-done | bytes 1280024
  41.9 0.0 copy-start.4
  41.9 0.7 copy-done.4
  42.5 1.2 %shard_map.74 = (bf16[64,800]{1,0:T(8,128)(2,1)S(1)}, bf16[64,800]{1,0:T(8,128)(2,1)S(1)}, f32[64,800]{1,0:T(8,128)S(1)}) custom-call(s32[4]{0:T(128)S(1)} %pad_add_fusion.places_ref.refs_0_, s32[128]{0:T(128)S(1)} %copy-done.4, s32[800]{0:T(1024)S(1)} %copy-done.1, bf16[64,2,8,128]{3,2,1,0:T(8,128)(2,1)S(1)} %bitcast.13, bf16[800,800]{1,0:T(8,128)(2,1)S(1)} %copy-done.3), custom_call_target="tpu_custom_call" | custom-call | flops 7200000000 | bytes 24000000 | tf_op jit(solution)/shard_map/pallas_call | solution.py:180
  43.7 0.0 collective-permute-done.1.refs_9_
  43.7 1.9 %collective-permute-start.3 = (bf16[800,800]{1,0:T(8,128)(2,1)S(1)}, bf16[800,800]{1,0:T(8,128)(2,1)S(1)}, u32[]{:S(2)}, u32[]{:S(2)}) collective-permute-start(bf16[800,800]{1,0:T(8,128)(2,1)S(1)} %collective-permute-done.1.refs_9_), channel_id=1, source_target_pairs={{0,4},{4,0},{1,5},{5,1},{2,6},{6,2},{3,7},{7,3},{8,12},{12,8},{9,1... | collective-permute-start | bytes 3840008 | tf_op jit(solution)/shard_map/ppermute | solution.py:183
  45.7 0.0 collective-permute-done.refs_3_
  45.7 0.0 collective-permute-done.2.refs_8_
  45.7 1.9 %shard_map.75 = (bf16[128,800]{1,0:T(8,128)(2,1)S(1)}, f32[1024,128]{1,0:T(8,128)S(1)}, f32[128,800]{1,0:T(8,128)S(1)}) custom-call(s32[4]{0:T(128)S(1)} %pad_add_fusion.places_ref.refs_0_, s32[128]{0:T(128)S(1)} %copy-done.4, s32[800]{0:T(1024)S(1)} %copy-done.1, bf16[64,2,8,128]{3,2,1,0:T(8,128)(2,1)S(1)} %collective-permute-done.refs_3_, ...), custom_call_target="tpu_custom_call" | custom-call | flops 12000000000 | bytes 40000000 | tf_op jit(solution)/shard_map/pallas_call | solution.py:192
  47.6 1.2 %collective-permute-done.3.block_ref = bf16[800,800]{1,0:T(8,128)(2,1)S(1)} collective-permute-done((bf16[800,800]{1,0:T(8,128)(2,1)S(1)}, bf16[800,800]{1,0:T(8,128)(2,1)S(1)}, u32[]{:S(2)}, u32[]{:S(2)}) %collective-permute-start.3) | collective-permute-done | bytes 1280032 | tf_op jit(solution)/shard_map/ppermute | solution.py:183
  48.8 0.7 shard_map.76
  49.6 0.0 copy-start.2
  49.6 0.0 copy-start.5
  49.6 0.0 copy-start
  49.6 0.9 %multiply_convert_fusion = f16[2048,128]{1,0:T(8,128)(2,1)} fusion(f32[2048,128]{1,0:T(8,128)S(1)} %shard_map.76), kind=kLoop, calls=%fused_computation.1 | loop fusion | flops 524288 | bytes 1572864 | tf_op jit(solution)/shard_map/convert_element_type | solution.py:199
  50.5 11.2 %all-to-all-start.1 = ((f16[128,16,128]{2,1,0:T(8,128)(2,1)}), f16[128,16,128]{2,1,0:T(8,128)(2,1)S(1)}, u32[]{:S(2)}, u32[]{:S(2)}) async-start(f16[128,16,128]{2,1,0:T(8,128)(2,1)} %bitcast.6), calls=%async_computation.1 | async-start | bytes 1048576 | tf_op jit(solution)/shard_map/all_to_all | solution.py:201
  61.7 1.2 %slice.3 = bf16[1,1,1]{2,1,0:T(2,128)(2,1)} slice(bf16[128,8,128]{2,1,0:T(8,128)(2,1)} %shard_map.73), slice={[0:1], [7:8], [0:1]} | slice | bytes 4 | tf_op jit(solution)/shard_map/slice | solution.py:203
  63.5 0.0 copy-done.2
  63.5 0.0 copy-done.5
  63.5 0.1 fusion.kept_ref
  63.6 19.5 %all-to-all-done.1 = f16[128,16,128]{2,1,0:T(8,128)(2,1)S(1)} async-done(((f16[128,16,128]{2,1,0:T(8,128)(2,1)}), f16[128,16,128]{2,1,0:T(8,128)(2,1)S(1)}, u32[]{:S(2)}, u32[]{:S(2)}) %all-to-all-start.1) | async-done | bytes 524320 | tf_op jit(solution)/shard_map/all_to_all | solution.py:201
  83.1 0.1 convert_reduce_fusion.sums_ref
  83.2 0.0 copy-done
  83.2 1.3 %shard_map.77 = bf16[1,3200]{1,0:T(2,128)(2,1)} custom-call(s32[4]{0:T(128)S(1)} %pad_add_fusion.places_ref.refs_0_, f32[2,16,128]{2,1,0:T(8,128)S(1)} %convert_reduce_fusion.sums_ref, f32[4,800]{1,0:T(4,128)S(1)} %fusion.kept_ref, bf16[1,3200]{1,0:T(2,128)(2,1)S(1)} %copy-done), custom_call_target="tpu_custom_call" | custom-call | bytes 50000 | tf_op jit(solution)/shard_map/pallas_call | solution.py:206
Async XLA Ops:
  0.0 43.7 %collective-permute-start.1 = (bf16[800,800]{1,0:T(8,128)(2,1)}, bf16[800,800]{1,0:T(8,128)(2,1)S(1)}, u32[]{:S(2)}, u32[]{:S(2)}) collective-permute-start(bf16[800,800]{1,0:T(8,128)(2,1)} %refs_7_.1), channel_id=1, source_target_pairs={{0,3},{3,0},{1,2},{2,1},{4,7},{7,4},{5,6},{6,5},{8,11},{11,8},{9,1... | collective-permute-start | bytes 3840008 | tf_op jit(solution)/shard_map/ppermute | solution.py:147
  5.4 31.3 %all-to-all-start = ((bf16[64,16,128]{2,1,0:T(8,128)(2,1)}), bf16[64,16,128]{2,1,0:T(8,128)(2,1)S(1)}, u32[]{:S(2)}, u32[]{:S(2)}) async-start(bf16[64,16,128]{2,1,0:T(8,128)(2,1)} %bitcast.14), calls=%async_computation | async-start | bytes 524288 | tf_op jit(solution)/shard_map/all_to_all | solution.py:166
  22.1 23.6 %collective-permute-start.2 = (bf16[800,800]{1,0:T(8,128)(2,1)}, bf16[800,800]{1,0:T(8,128)(2,1)S(1)}, u32[]{:S(2)}, u32[]{:S(2)}) collective-permute-start(bf16[800,800]{1,0:T(8,128)(2,1)} %refs_7_.1), channel_id=1, source_target_pairs={{0,4},{4,0},{1,5},{5,1},{2,6},{6,2},{3,7},{7,3},{8,12},{12,8},{9,1... | collective-permute-start | bytes 3840008 | tf_op jit(solution)/shard_map/ppermute | solution.py:181
  36.8 8.9 %collective-permute-start = (bf16[64,2,8,128]{3,2,1,0:T(8,128)(2,1)S(1)}, bf16[64,2,8,128]{3,2,1,0:T(8,128)(2,1)S(1)}, u32[]{:S(2)}, u32[]{:S(2)}) collective-permute-start(bf16[64,2,8,128]{3,2,1,0:T(8,128)(2,1)S(1)} %bitcast.12), channel_id=1, source_target_pairs={{0,1},{1,0},{2,3},{3,2},{4,5},{5,4},{6,7},{7,6},{8,9},{9,8},{10,11... | collective-permute-start | bytes 786440 | tf_op jit(solution)/shard_map/ppermute | solution.py:168
  39.8 0.7 copy-start.1
  40.5 1.4 %copy-start.3 = (bf16[800,800]{1,0:T(8,128)(2,1)S(1)}, bf16[800,800]{1,0:T(8,128)(2,1)}, u32[]{:S(2)}) copy-start(bf16[800,800]{1,0:T(8,128)(2,1)} %refs_7_.1) | copy-start | bytes 3840004
  41.9 0.7 copy-start.4
  43.7 5.1 %collective-permute-start.3 = (bf16[800,800]{1,0:T(8,128)(2,1)S(1)}, bf16[800,800]{1,0:T(8,128)(2,1)S(1)}, u32[]{:S(2)}, u32[]{:S(2)}) collective-permute-start(bf16[800,800]{1,0:T(8,128)(2,1)S(1)} %collective-permute-done.1.refs_9_), channel_id=1, source_target_pairs={{0,4},{4,0},{1,5},{5,1},{2,6},{6,2},{3,7},{7,3},{8,12},{12,8},{9,1... | collective-permute-start | bytes 3840008 | tf_op jit(solution)/shard_map/ppermute | solution.py:183
  49.6 13.9 %copy-start.2 = (s32[800]{0:T(1024)S(1)}, s32[800]{0:T(1024)}, u32[]{:S(2)}) copy-start(s32[800]{0:T(1024)} %refs_2_.1) | copy-start | bytes 9604
  49.6 13.9 %copy-start.5 = (s32[4]{0:T(128)S(1)}, s32[4]{0:T(128)}, u32[]{:S(2)}) copy-start(s32[4]{0:T(128)} %param.12) | copy-start | bytes 52
  49.6 33.6 %copy-start = (bf16[1,3200]{1,0:T(2,128)(2,1)S(1)}, bf16[1,3200]{1,0:T(2,128)(2,1)}, u32[]{:S(2)}) copy-start(bf16[1,3200]{1,0:T(2,128)(2,1)} %old_ref.1) | copy-start | bytes 19204
  50.5 32.6 %all-to-all-start.1 = ((f16[128,16,128]{2,1,0:T(8,128)(2,1)}), f16[128,16,128]{2,1,0:T(8,128)(2,1)S(1)}, u32[]{:S(2)}, u32[]{:S(2)}) async-start(f16[128,16,128]{2,1,0:T(8,128)(2,1)} %bitcast.6), calls=%async_computation.1 | async-start | bytes 1048576 | tf_op jit(solution)/shard_map/all_to_all | solution.py:201

commit v7 on v6

--- a/solution.py
+++ b/solution.py
@@ -196,12 +196,15 @@
         functools.partial(ladder_body, zy), shape((2 * zy * 16, LANES), F32), "vvvv", 1000, 3000000
     )
     part = ladder(rows2, partner2, sums, own_sums)
-    part = (part * SCALE).astype(F16).reshape(2 * zy, 16, LANES)
-    part, upper = lax.optimization_barrier((part, upper_irrep))
-    back = lax.all_to_all(part, ("x0", "z", "y"), 0, 0, tiled=True)
-    ab_irrep = jnp.bitwise_xor(upper[:, None], virt_irrep[None, :])
+    num_z, num_y = lax.axis_size("z"), lax.axis_size("y")
+    part = (part * SCALE).astype(F16).reshape(2, num_z, num_y, 16, LANES)
+    part = jnp.transpose(part, (2, 0, 1, 3, 4)).reshape(num_y, 2 * num_z * 16, LANES)
+    back = lax.all_to_all(part, "y", 0, 0, tiled=True)
+    sums = jnp.sum(back.astype(F32), axis=0).reshape(2 * num_z, 16, LANES)
+    sums = lax.all_to_all(sums, ("x0", "z"), 0, 0, tiled=True)
+    sums = jnp.sum(sums.reshape(2, num_z, 16, LANES), axis=1)
+    ab_irrep = jnp.bitwise_xor(upper_irrep[:, None], virt_irrep[None, :])
     kept = (ab_irrep == cut[0, TILES, 0].astype(jnp.int32)).astype(F32)
-    sums = jnp.sum(back.reshape(2, zy, 16, LANES).astype(F32), axis=1)
     finish = call(finish_body, shape((1, 4 * NV), BF16), "svvv", 0, 50000)
     return finish(places, sums, kept, residual_in)
 

time: 84.9 us -> 89.6 us (1.055)
  blocking collectives: 0 us -> 20.5 us
  waiting for transfers between devices: 33.4 us -> 20.7 us
  starting transfers between devices: 37.1 us -> 33.9 us
    all_to_all x0 -> x1, blocking collectives: none -> 20.5 us  [per_device(): back = lax.all_to_all(part, 'y', 0, 0, tiled=True)]
    all_to_all x1, waiting for transfers between devices: 19.5 us -> 6.8 us  [per_device(): sums = lax.all_to_all(sums, ('x0', 'z'), 0, 0, tiled=True)]
    all_to_all x1, starting transfers between devices: 11.2 us -> 8 us  [per_device(): sums = lax.all_to_all(sums, ('x0', 'z'), 0, 0, tiled=True)]
  transfers between devices with their start and end apart: 6 -> 6, of which waited for: 3 -> 3; matrix products, arithmetic and copies ran while one was open for 2% -> 1% of each run, Pallas kernels for 6% -> 6%
where the time goes in v7:
time: 89.6 us; the launch traced here: 89.1 us
  starting transfers between devices  33.9 us (38%)
  waiting for transfers between devices  20.7 us (23%)
  blocking collectives  20.5 us (23%)
  Pallas kernels  7.45 us (8%)
  local copies, waits for them, and re-layouts  4.02 us (4%)
  between operations  1.5 us (2%)
  other arithmetic  0.99 us (1%)
    all_to_all x1, blocking collectives, per_device(): back = lax.all_to_all(part, 'y', 0, 0, tiled=True)  20.5 us
    all_to_all x1, starting transfers between devices, per_device(): lax.all_to_all(cut.reshape(zy, 16, LANES), ('z', 'y'), 0, 0, tiled=True)  16.6 us
    all_to_all x1, waiting for transfers between devices, per_device(): lax.all_to_all(cut.reshape(zy, 16, LANES), ('z', 'y'), 0, 0, tiled=True)  12.7 us
    all_to_all x1, starting transfers between devices, per_device(): sums = lax.all_to_all(sums, ('x0', 'z'), 0, 0, tiled=True)  8 us
    all_to_all x1, waiting for transfers between devices, per_device(): sums = lax.all_to_all(sums, ('x0', 'z'), 0, 0, tiled=True)  6.8 us
    ppermute x1, starting transfers between devices, per_device(): there = lax.ppermute(mine, 'x0', other_x0)  3.04 us
    unnamed x12, local copies, waits for them, and re-layouts  2.71 us
    ppermute x1, starting transfers between devices, per_device(): lax.ppermute(integrals, ('x1', 'x0'), [(0, 3), (3, 0), (1, 2), (2, 1)])  2.43 us
  transfers between devices with their start and end apart: 6, of which 3 were waited for; matrix products, arithmetic and copies ran while one was open for 1% of the time, Pallas kernels for 6%

profile of v7, /device:TPU:4, one launch (start us, length us, event | category | flops | bytes accessed | tf_op | source)
XLA Modules:
  0.0 89.1 jit_solution(3341588801789713905)
XLA Ops:
  0.0 2.4 %collective-permute-start.1 = (bf16[800,800]{1,0:T(8,128)(2,1)}, bf16[800,800]{1,0:T(8,128)(2,1)S(1)}, u32[]{:S(2)}, u32[]{:S(2)}) collective-permute-start(bf16[800,800]{1,0:T(8,128)(2,1)} %refs_7_.1), channel_id=1, source_target_pairs={{0,3},{3,0},{1,2},{2,1},{4,7},{7,4},{5,6},{6,5},{8,11},{11,8},{9,1... | collective-permute-start | bytes 3840008 | tf_op jit(solution)/shard_map/ppermute | solution.py:147
  3.1 2.3 %shard_map.73 = bf16[128,8,128]{2,1,0:T(8,128)(2,1)} custom-call(s32[1]{0:T(128)S(6)} %copy.10.pair_ref, bf16[1,102400]{1,0:T(2,128)(2,1)} %row_ref.1), custom_call_target="tpu_custom_call" | custom-call | bytes 700000 | tf_op jit(solution)/shard_map/pallas_call | solution.py:150
  5.4 16.6 %all-to-all-start = ((bf16[64,16,128]{2,1,0:T(8,128)(2,1)}), bf16[64,16,128]{2,1,0:T(8,128)(2,1)S(1)}, u32[]{:S(2)}, u32[]{:S(2)}) async-start(bf16[64,16,128]{2,1,0:T(8,128)(2,1)} %bitcast.19), calls=%async_computation | async-start | bytes 524288 | tf_op jit(solution)/shard_map/all_to_all | solution.py:166
  22.0 1.9 %collective-permute-start.2 = (bf16[800,800]{1,0:T(8,128)(2,1)}, bf16[800,800]{1,0:T(8,128)(2,1)S(1)}, u32[]{:S(2)}, u32[]{:S(2)}) collective-permute-start(bf16[800,800]{1,0:T(8,128)(2,1)} %refs_7_.1), channel_id=1, source_target_pairs={{0,4},{4,0},{1,5},{5,1},{2,6},{6,2},{3,7},{7,3},{8,12},{12,8},{9,1... | collective-permute-start | bytes 3840008 | tf_op jit(solution)/shard_map/ppermute | solution.py:181
  24.0 0.1 pad_add_fusion.places_ref.refs_0_
  24.1 12.7 %all-to-all-done = bf16[64,16,128]{2,1,0:T(8,128)(2,1)S(1)} async-done(((bf16[64,16,128]{2,1,0:T(8,128)(2,1)}), bf16[64,16,128]{2,1,0:T(8,128)(2,1)S(1)}, u32[]{:S(2)}, u32[]{:S(2)}) %all-to-all-start) | async-done | bytes 262176 | tf_op jit(solution)/shard_map/all_to_all | solution.py:166
  36.8 3.0 %collective-permute-start = (bf16[64,2,8,128]{3,2,1,0:T(8,128)(2,1)S(1)}, bf16[64,2,8,128]{3,2,1,0:T(8,128)(2,1)S(1)}, u32[]{:S(2)}, u32[]{:S(2)}) collective-permute-start(bf16[64,2,8,128]{3,2,1,0:T(8,128)(2,1)S(1)} %bitcast.15), channel_id=1, source_target_pairs={{0,1},{1,0},{2,3},{3,2},{4,5},{5,4},{6,7},{7,6},{8,9},{9,8},{10,11... | collective-permute-start | bytes 786440 | tf_op jit(solution)/shard_map/ppermute | solution.py:168
  39.8 0.0 copy-start.1
  39.8 0.7 copy-done.1
  40.5 0.0 copy-start.3
  40.5 1.4 %copy-done.3 = bf16[800,800]{1,0:T(8,128)(2,1)S(1)} copy-done((bf16[800,800]{1,0:T(8,128)(2,1)S(1)}, bf16[800,800]{1,0:T(8,128)(2,1)}, u32[]{:S(2)}) %copy-start.3) | copy-done | bytes 1280024
  41.8 0.0 copy-start.4
  41.9 0.7 copy-done.4
  42.5 1.2 %shard_map.74 = (bf16[64,800]{1,0:T(8,128)(2,1)S(1)}, bf16[64,800]{1,0:T(8,128)(2,1)S(1)}, f32[64,800]{1,0:T(8,128)S(1)}) custom-call(s32[4]{0:T(128)S(1)} %pad_add_fusion.places_ref.refs_0_, s32[128]{0:T(128)S(1)} %copy-done.4, s32[800]{0:T(1024)S(1)} %copy-done.1, bf16[64,2,8,128]{3,2,1,0:T(8,128)(2,1)S(1)} %bitcast.16, bf16[800,800]{1,0:T(8,128)(2,1)S(1)} %copy-done.3), custom_call_target="tpu_custom_call" | custom-call | flops 7200000000 | bytes 24000000 | tf_op jit(solution)/shard_map/pallas_call | solution.py:180
  43.7 0.0 collective-permute-done.1.refs_9_
  43.7 1.9 %collective-permute-start.3 = (bf16[800,800]{1,0:T(8,128)(2,1)S(1)}, bf16[800,800]{1,0:T(8,128)(2,1)S(1)}, u32[]{:S(2)}, u32[]{:S(2)}) collective-permute-start(bf16[800,800]{1,0:T(8,128)(2,1)S(1)} %collective-permute-done.1.refs_9_), channel_id=1, source_target_pairs={{0,4},{4,0},{1,5},{5,1},{2,6},{6,2},{3,7},{7,3},{8,12},{12,8},{9,1... | collective-permute-start | bytes 3840008 | tf_op jit(solution)/shard_map/ppermute | solution.py:183
  45.6 0.0 collective-permute-done.refs_3_
  45.7 0.0 collective-permute-done.2.refs_8_
  45.7 1.9 %shard_map.75 = (bf16[128,800]{1,0:T(8,128)(2,1)S(1)}, f32[1024,128]{1,0:T(8,128)S(1)}, f32[128,800]{1,0:T(8,128)S(1)}) custom-call(s32[4]{0:T(128)S(1)} %pad_add_fusion.places_ref.refs_0_, s32[128]{0:T(128)S(1)} %copy-done.4, s32[800]{0:T(1024)S(1)} %copy-done.1, bf16[64,2,8,128]{3,2,1,0:T(8,128)(2,1)S(1)} %collective-permute-done.refs_3_, ...), custom_call_target="tpu_custom_call" | custom-call | flops 12000000000 | bytes 40000000 | tf_op jit(solution)/shard_map/pallas_call | solution.py:192
  47.6 1.2 %collective-permute-done.3.block_ref = bf16[800,800]{1,0:T(8,128)(2,1)S(1)} collective-permute-done((bf16[800,800]{1,0:T(8,128)(2,1)S(1)}, bf16[800,800]{1,0:T(8,128)(2,1)S(1)}, u32[]{:S(2)}, u32[]{:S(2)}) %collective-permute-start.3) | collective-permute-done | bytes 1280032 | tf_op jit(solution)/shard_map/ppermute | solution.py:183
  48.8 0.7 shard_map.76
  49.6 0.1 multiply_convert_fusion
  49.7 0.0 copy-start.2
  49.7 0.0 copy-start.5
  49.7 0.0 copy-start
  49.7 0.1 copy.9
  49.8 20.5 %all_to_all.15 = f16[8,256,128]{2,1,0:T(8,128)(2,1)S(1)} all-to-all(f16[8,256,128]{2,1,0:T(8,128)(2,1)S(1)} %bitcast.18), channel_id=1, replica_groups=mesh['z'=8,'y'=8,'core'=2,'x1'=2,'x0'=2] {'y'}, dimensions={0} | all-to-all | bytes 1048576 | tf_op jit(solution)/shard_map/all_to_all | solution.py:202
  70.3 0.7 convert_reduce_fusion
  71.0 8.0 %all-to-all-start.2 = ((f32[16,16,128]{2,1,0:T(8,128)}), f32[16,16,128]{2,1,0:T(8,128)S(1)}, u32[]{:S(2)}, u32[]{:S(2)}) async-start(f32[16,16,128]{2,1,0:T(8,128)} %bitcast.9), calls=%async_computation.2 | async-start | bytes 262144 | tf_op jit(solution)/shard_map/all_to_all | solution.py:204
  79.0 1.2 %slice.3 = bf16[1,1,1]{2,1,0:T(2,128)(2,1)} slice(bf16[128,8,128]{2,1,0:T(8,128)(2,1)} %shard_map.73), slice={[0:1], [7:8], [0:1]} | slice | bytes 4 | tf_op jit(solution)/shard_map/slice | solution.py:207
  80.9 0.0 copy-done.2
  80.9 0.0 copy-done.5
  80.9 0.1 fusion.kept_ref
  81.0 6.8 %all-to-all-done.2 = f32[16,16,128]{2,1,0:T(8,128)S(1)} async-done(((f32[16,16,128]{2,1,0:T(8,128)}), f32[16,16,128]{2,1,0:T(8,128)S(1)}, u32[]{:S(2)}, u32[]{:S(2)}) %all-to-all-start.2) | async-done | bytes 131104 | tf_op jit(solution)/shard_map/all_to_all | solution.py:204
  87.8 0.0 copy-done
  87.8 1.3 %shard_map.77 = bf16[1,3200]{1,0:T(2,128)(2,1)} custom-call(s32[4]{0:T(128)S(1)} %pad_add_fusion.places_ref.refs_0_, f32[2,16,128]{2,1,0:T(8,128)S(1)} %bitcast_reduce_fusion.sums_ref, f32[4,800]{1,0:T(4,128)S(1)} %fusion.kept_ref, bf16[1,3200]{1,0:T(2,128)(2,1)S(1)} %copy-done), custom_call_target="tpu_custom_call" | custom-call | bytes 50000 | tf_op jit(solution)/shard_map/pallas_call | solution.py:209
  (1 shorter events, 0.0 us)
Async XLA Ops:
  0.0 43.7 %collective-permute-start.1 = (bf16[800,800]{1,0:T(8,128)(2,1)}, bf16[800,800]{1,0:T(8,128)(2,1)S(1)}, u32[]{:S(2)}, u32[]{:S(2)}) collective-permute-start(bf16[800,800]{1,0:T(8,128)(2,1)} %refs_7_.1), channel_id=1, source_target_pairs={{0,3},{3,0},{1,2},{2,1},{4,7},{7,4},{5,6},{6,5},{8,11},{11,8},{9,1... | collective-permute-start | bytes 3840008 | tf_op jit(solution)/shard_map/ppermute | solution.py:147
  5.4 31.3 %all-to-all-start = ((bf16[64,16,128]{2,1,0:T(8,128)(2,1)}), bf16[64,16,128]{2,1,0:T(8,128)(2,1)S(1)}, u32[]{:S(2)}, u32[]{:S(2)}) async-start(bf16[64,16,128]{2,1,0:T(8,128)(2,1)} %bitcast.19), calls=%async_computation | async-start | bytes 524288 | tf_op jit(solution)/shard_map/all_to_all | solution.py:166
  22.0 23.6 %collective-permute-start.2 = (bf16[800,800]{1,0:T(8,128)(2,1)}, bf16[800,800]{1,0:T(8,128)(2,1)S(1)}, u32[]{:S(2)}, u32[]{:S(2)}) collective-permute-start(bf16[800,800]{1,0:T(8,128)(2,1)} %refs_7_.1), channel_id=1, source_target_pairs={{0,4},{4,0},{1,5},{5,1},{2,6},{6,2},{3,7},{7,3},{8,12},{12,8},{9,1... | collective-permute-start | bytes 3840008 | tf_op jit(solution)/shard_map/ppermute | solution.py:181
  36.8 8.9 %collective-permute-start = (bf16[64,2,8,128]{3,2,1,0:T(8,128)(2,1)S(1)}, bf16[64,2,8,128]{3,2,1,0:T(8,128)(2,1)S(1)}, u32[]{:S(2)}, u32[]{:S(2)}) collective-permute-start(bf16[64,2,8,128]{3,2,1,0:T(8,128)(2,1)S(1)} %bitcast.15), channel_id=1, source_target_pairs={{0,1},{1,0},{2,3},{3,2},{4,5},{5,4},{6,7},{7,6},{8,9},{9,8},{10,11... | collective-permute-start | bytes 786440 | tf_op jit(solution)/shard_map/ppermute | solution.py:168
  39.8 0.7 copy-start.1
  40.5 1.4 %copy-start.3 = (bf16[800,800]{1,0:T(8,128)(2,1)S(1)}, bf16[800,800]{1,0:T(8,128)(2,1)}, u32[]{:S(2)}) copy-start(bf16[800,800]{1,0:T(8,128)(2,1)} %refs_7_.1) | copy-start | bytes 3840004
  41.8 0.7 copy-start.4
  43.7 5.1 %collective-permute-start.3 = (bf16[800,800]{1,0:T(8,128)(2,1)S(1)}, bf16[800,800]{1,0:T(8,128)(2,1)S(1)}, u32[]{:S(2)}, u32[]{:S(2)}) collective-permute-start(bf16[800,800]{1,0:T(8,128)(2,1)S(1)} %collective-permute-done.1.refs_9_), channel_id=1, source_target_pairs={{0,4},{4,0},{1,5},{5,1},{2,6},{6,2},{3,7},{7,3},{8,12},{12,8},{9,1... | collective-permute-start | bytes 3840008 | tf_op jit(solution)/shard_map/ppermute | solution.py:183
  49.7 31.2 %copy-start.2 = (s32[800]{0:T(1024)S(1)}, s32[800]{0:T(1024)}, u32[]{:S(2)}) copy-start(s32[800]{0:T(1024)} %refs_2_.1) | copy-start | bytes 9604
  49.7 31.2 %copy-start.5 = (s32[4]{0:T(128)S(1)}, s32[4]{0:T(128)}, u32[]{:S(2)}) copy-start(s32[4]{0:T(128)} %param.12) | copy-start | bytes 52
  49.7 38.1 %copy-start = (bf16[1,3200]{1,0:T(2,128)(2,1)S(1)}, bf16[1,3200]{1,0:T(2,128)(2,1)}, u32[]{:S(2)}) copy-start(bf16[1,3200]{1,0:T(2,128)(2,1)} %old_ref.1) | copy-start | bytes 19204
  71.0 16.7 %all-to-all-start.2 = ((f32[16,16,128]{2,1,0:T(8,128)}), f32[16,16,128]{2,1,0:T(8,128)S(1)}, u32[]{:S(2)}, u32[]{:S(2)}) async-start(f32[16,16,128]{2,1,0:T(8,128)} %bitcast.9), calls=%async_computation.2 | async-start | bytes 262144 | tf_op jit(solution)/shard_map/all_to_all | solution.py:204

commit v8 on v6

--- a/solution.py
+++ b/solution.py
@@ -14,6 +14,7 @@
 LANES = 128
 TILES = 7
 WIDE = TILES * LANES
+ROLLED = [(z + 4) % 8 * 8 + (y + 4) % 8 for z in range(8) for y in range(8)]
 SCALE = 64.0
 
 VMEM = pl.BlockSpec(memory_space=pltpu.VMEM)
@@ -50,7 +51,9 @@
         for r in range(4):
             at = [pl.multiple_of(q * 3200 + (6 * r + t) * LANES, LANES) for t in range(TILES)]
             tiles = [row[:, pl.ds(a, LANES)].astype(F32) for a in at]
-            cut[4 * q + r] = jnp.concatenate(tiles + [filler], axis=0).astype(BF16)
+            chip = 2 * q + r // 2
+            place = (chip // 8 + 4) % 8 * 8 + (chip + 4) % 8
+            cut[2 * place + r % 2] = jnp.concatenate(tiles + [filler], axis=0).astype(BF16)
         return carry
 
     for i in range(steps):
@@ -60,7 +63,7 @@
     for i in range(steps):
         fetch(i).wait()
         lax.fori_loop(i * slabs // 4, (i + 1) * slabs // 4, four, 0, unroll=4)
-        put(i).start()
+        put((i + 2) % 4).start()
     for i in range(steps):
         put(i).wait()
 
@@ -163,7 +166,9 @@
         cost_estimate=pl.CostEstimate(flops=0, bytes_accessed=700000, transcendentals=0),
     )(pair_irrep, amplitudes)
     cut, block = lax.optimization_barrier((cut, integrals))
-    mine = lax.all_to_all(cut.reshape(zy, 16, LANES), ("z", "y"), 0, 0, tiled=True)
+    mine = lax.all_to_all(
+        cut.reshape(zy, 16, LANES), ("z", "y"), 0, 0, axis_index_groups=[ROLLED], tiled=True
+    )
     mine = mine.reshape(zy, 2, 8, LANES)
     there = lax.ppermute(mine, "x0", other_x0)
 
@@ -198,7 +203,9 @@
     part = ladder(rows2, partner2, sums, own_sums)
     part = (part * SCALE).astype(F16).reshape(2 * zy, 16, LANES)
     part, upper = lax.optimization_barrier((part, upper_irrep))
-    back = lax.all_to_all(part, ("x0", "z", "y"), 0, 0, tiled=True)
+    back = lax.all_to_all(
+        part, ("x0", "z", "y"), 0, 0, axis_index_groups=[ROLLED + [64 + i for i in ROLLED]], tiled=True
+    )
     ab_irrep = jnp.bitwise_xor(upper[:, None], virt_irrep[None, :])
     kept = (ab_irrep == cut[0, TILES, 0].astype(jnp.int32)).astype(F32)
     sums = jnp.sum(back.reshape(2, zy, 16, LANES).astype(F32), axis=1)

time: 84.9 us -> 79.4 us (0.935)
  the two profiles are of different devices: /device:TPU:4 before, /device:TPU:1 now
where the time goes in v8:
time: 79.4 us; the launch traced here: 79 us
  starting transfers between devices  50.2 us (63%)
  waiting for transfers between devices  14.2 us (18%)
  Pallas kernels  8.07 us (10%)
  local copies, waits for them, and re-layouts  3.89 us (5%)
  between operations  1.48 us (2%)
  other arithmetic  1.14 us (1%)
    all_to_all x1, starting transfers between devices, per_device(): lax.all_to_all(cut.reshape(zy, 16, LANES), ('z', 'y'), 0, 0, axis_index_g...  19.3 us
    all_to_all x1, starting transfers between devices, per_device(): lax.all_to_all(part, ('x0', 'z', 'y'), 0, 0, axis_index_groups=[ROLLED +...  16.4 us
    all_to_all x1, waiting for transfers between devices, per_device(): lax.all_to_all(part, ('x0', 'z', 'y'), 0, 0, axis_index_groups=[ROLLED +...  11.2 us
    ppermute x1, starting transfers between devices, per_device(): lax.ppermute(integrals, ('x1', 'x0'), [(0, 3), (3, 0), (1, 2), (2, 1)])  5.21 us
    ppermute x1, starting transfers between devices, per_device(): partner2 = lax.ppermute(partner, 'core', other_core)  3.94 us
    ppermute x1, starting transfers between devices, per_device(): block2 = lax.ppermute(block, 'core', other_core)  3.43 us
    pallas_call x1, Pallas kernels, per_device(): pl.pallas_call(functools.partial(cut_body, steps), in_specs=[pl.BlockSpec...  2.94 us
    unnamed x12, local copies, waits for them, and re-layouts  2.71 us
  transfers between devices with their start and end apart: 6, of which 3 were waited for; matrix products, arithmetic and copies ran while one was open for 2% of the time, Pallas kernels for 8%

profile of v8, /device:TPU:1, one launch (start us, length us, event | category | flops | bytes accessed | tf_op | source)
XLA Modules:
  0.0 79.0 jit_solution(922433092450734160)
XLA Ops:
  0.0 5.2 %collective-permute-start.1 = (bf16[800,800]{1,0:T(8,128)(2,1)}, bf16[800,800]{1,0:T(8,128)(2,1)S(1)}, u32[]{:S(2)}, u32[]{:S(2)}) collective-permute-start(bf16[800,800]{1,0:T(8,128)(2,1)} %refs_7_.1), channel_id=1, source_target_pairs={{0,3},{3,0},{1,2},{2,1},{4,7},{7,4},{5,6},{6,5},{8,11},{11,8},{9,1... | collective-permute-start | bytes 3840008 | tf_op jit(solution)/shard_map/ppermute | solution.py:150
  5.9 2.9 %shard_map.73 = bf16[128,8,128]{2,1,0:T(8,128)(2,1)} custom-call(s32[1]{0:T(128)S(6)} %copy.8.pair_ref, bf16[1,102400]{1,0:T(2,128)(2,1)} %row_ref.1), custom_call_target="tpu_custom_call" | custom-call | bytes 700000 | tf_op jit(solution)/shard_map/pallas_call | solution.py:153
  8.8 19.3 %all-to-all-start = ((bf16[64,16,128]{2,1,0:T(8,128)(2,1)}), bf16[64,16,128]{2,1,0:T(8,128)(2,1)S(1)}, u32[]{:S(2)}, u32[]{:S(2)}) async-start(bf16[64,16,128]{2,1,0:T(8,128)(2,1)} %bitcast.14), calls=%async_computation | async-start | bytes 524288 | tf_op jit(solution)/shard_map/all_to_all | solution.py:169
  28.1 3.4 %collective-permute-start.2 = (bf16[800,800]{1,0:T(8,128)(2,1)}, bf16[800,800]{1,0:T(8,128)(2,1)S(1)}, u32[]{:S(2)}, u32[]{:S(2)}) collective-permute-start(bf16[800,800]{1,0:T(8,128)(2,1)} %refs_7_.1), channel_id=1, source_target_pairs={{0,4},{4,0},{1,5},{5,1},{2,6},{6,2},{3,7},{7,3},{8,12},{12,8},{9,1... | collective-permute-start | bytes 3840008 | tf_op jit(solution)/shard_map/ppermute | solution.py:186
  31.6 0.1 pad_add_fusion.places_ref.refs_0_
  31.6 2.1 %all-to-all-done = bf16[64,16,128]{2,1,0:T(8,128)(2,1)S(1)} async-done(((bf16[64,16,128]{2,1,0:T(8,128)(2,1)}), bf16[64,16,128]{2,1,0:T(8,128)(2,1)S(1)}, u32[]{:S(2)}, u32[]{:S(2)}) %all-to-all-start) | async-done | bytes 262176 | tf_op jit(solution)/shard_map/all_to_all | solution.py:169
  33.7 1.9 %collective-permute-start = (bf16[64,2,8,128]{3,2,1,0:T(8,128)(2,1)S(1)}, bf16[64,2,8,128]{3,2,1,0:T(8,128)(2,1)S(1)}, u32[]{:S(2)}, u32[]{:S(2)}) collective-permute-start(bf16[64,2,8,128]{3,2,1,0:T(8,128)(2,1)S(1)} %bitcast.12), channel_id=1, source_target_pairs={{0,1},{1,0},{2,3},{3,2},{4,5},{5,4},{6,7},{7,6},{8,9},{9,8},{10,11... | collective-permute-start | bytes 786440 | tf_op jit(solution)/shard_map/ppermute | solution.py:173
  35.6 0.0 copy-start.1
  35.7 0.7 copy-done.1
  36.3 0.0 copy-start.3
  36.3 1.4 %copy-done.3 = bf16[800,800]{1,0:T(8,128)(2,1)S(1)} copy-done((bf16[800,800]{1,0:T(8,128)(2,1)S(1)}, bf16[800,800]{1,0:T(8,128)(2,1)}, u32[]{:S(2)}) %copy-start.3) | copy-done | bytes 1280024
  37.7 0.0 copy-start.4
  37.7 0.7 copy-done.4
  38.3 1.2 %shard_map.74 = (bf16[64,800]{1,0:T(8,128)(2,1)S(1)}, bf16[64,800]{1,0:T(8,128)(2,1)S(1)}, f32[64,800]{1,0:T(8,128)S(1)}) custom-call(s32[4]{0:T(128)S(1)} %pad_add_fusion.places_ref.refs_0_, s32[128]{0:T(128)S(1)} %copy-done.4, s32[800]{0:T(1024)S(1)} %copy-done.1, bf16[64,2,8,128]{3,2,1,0:T(8,128)(2,1)S(1)} %bitcast.13, bf16[800,800]{1,0:T(8,128)(2,1)S(1)} %copy-done.3), custom_call_target="tpu_custom_call" | custom-call | flops 7200000000 | bytes 24000000 | tf_op jit(solution)/shard_map/pallas_call | solution.py:185
  39.6 0.0 collective-permute-done.1.refs_9_
  39.6 3.9 %collective-permute-start.3 = (bf16[800,800]{1,0:T(8,128)(2,1)S(1)}, bf16[800,800]{1,0:T(8,128)(2,1)S(1)}, u32[]{:S(2)}, u32[]{:S(2)}) collective-permute-start(bf16[800,800]{1,0:T(8,128)(2,1)S(1)} %collective-permute-done.1.refs_9_), channel_id=1, source_target_pairs={{0,4},{4,0},{1,5},{5,1},{2,6},{6,2},{3,7},{7,3},{8,12},{12,8},{9,1... | collective-permute-start | bytes 3840008 | tf_op jit(solution)/shard_map/ppermute | solution.py:188
  43.5 0.0 collective-permute-done.refs_3_
  43.5 0.0 collective-permute-done.2.refs_8_
  43.5 1.9 %shard_map.75 = (bf16[128,800]{1,0:T(8,128)(2,1)S(1)}, f32[1024,128]{1,0:T(8,128)S(1)}, f32[128,800]{1,0:T(8,128)S(1)}) custom-call(s32[4]{0:T(128)S(1)} %pad_add_fusion.places_ref.refs_0_, s32[128]{0:T(128)S(1)} %copy-done.4, s32[800]{0:T(1024)S(1)} %copy-done.1, bf16[64,2,8,128]{3,2,1,0:T(8,128)(2,1)S(1)} %collective-permute-done.refs_3_, ...), custom_call_target="tpu_custom_call" | custom-call | flops 12000000000 | bytes 40000000 | tf_op jit(solution)/shard_map/pallas_call | solution.py:197
  45.5 0.8 %collective-permute-done.3.block_ref = bf16[800,800]{1,0:T(8,128)(2,1)S(1)} collective-permute-done((bf16[800,800]{1,0:T(8,128)(2,1)S(1)}, bf16[800,800]{1,0:T(8,128)(2,1)S(1)}, u32[]{:S(2)}, u32[]{:S(2)}) %collective-permute-start.3) | collective-permute-done | bytes 1280032 | tf_op jit(solution)/shard_map/ppermute | solution.py:188
  46.3 0.7 shard_map.76
  47.1 0.0 copy-start.2
  47.1 0.0 copy-start.5
  47.1 0.0 copy-start
  47.1 0.9 %multiply_convert_fusion = f16[2048,128]{1,0:T(8,128)(2,1)} fusion(f32[2048,128]{1,0:T(8,128)S(1)} %shard_map.76), kind=kLoop, calls=%fused_computation.1 | loop fusion | flops 524288 | bytes 1572864 | tf_op jit(solution)/shard_map/convert_element_type | solution.py:204
  48.0 16.4 %all-to-all-start.1 = ((f16[128,16,128]{2,1,0:T(8,128)(2,1)}), f16[128,16,128]{2,1,0:T(8,128)(2,1)S(1)}, u32[]{:S(2)}, u32[]{:S(2)}) async-start(f16[128,16,128]{2,1,0:T(8,128)(2,1)} %bitcast.6), calls=%async_computation.1 | async-start | bytes 1048576 | tf_op jit(solution)/shard_map/all_to_all | solution.py:206
  64.4 1.2 %slice.3 = bf16[1,1,1]{2,1,0:T(2,128)(2,1)} slice(bf16[128,8,128]{2,1,0:T(8,128)(2,1)} %shard_map.73), slice={[0:1], [7:8], [0:1]} | slice | bytes 4 | tf_op jit(solution)/shard_map/slice | solution.py:210
  66.3 0.0 copy-done.2
  66.3 0.0 copy-done.5
  66.3 0.1 fusion.kept_ref
  66.4 11.2 %all-to-all-done.1 = f16[128,16,128]{2,1,0:T(8,128)(2,1)S(1)} async-done(((f16[128,16,128]{2,1,0:T(8,128)(2,1)}), f16[128,16,128]{2,1,0:T(8,128)(2,1)S(1)}, u32[]{:S(2)}, u32[]{:S(2)}) %all-to-all-start.1) | async-done | bytes 524320 | tf_op jit(solution)/shard_map/all_to_all | solution.py:206
  77.6 0.1 convert_reduce_fusion.sums_ref
  77.7 0.0 copy-done
  77.7 1.3 %shard_map.77 = bf16[1,3200]{1,0:T(2,128)(2,1)} custom-call(s32[4]{0:T(128)S(1)} %pad_add_fusion.places_ref.refs_0_, f32[2,16,128]{2,1,0:T(8,128)S(1)} %convert_reduce_fusion.sums_ref, f32[4,800]{1,0:T(4,128)S(1)} %fusion.kept_ref, bf16[1,3200]{1,0:T(2,128)(2,1)S(1)} %copy-done), custom_call_target="tpu_custom_call" | custom-call | bytes 50000 | tf_op jit(solution)/shard_map/pallas_call | solution.py:213
Async XLA Ops:
  0.0 39.6 %collective-permute-start.1 = (bf16[800,800]{1,0:T(8,128)(2,1)}, bf16[800,800]{1,0:T(8,128)(2,1)S(1)}, u32[]{:S(2)}, u32[]{:S(2)}) collective-permute-start(bf16[800,800]{1,0:T(8,128)(2,1)} %refs_7_.1), channel_id=1, source_target_pairs={{0,3},{3,0},{1,2},{2,1},{4,7},{7,4},{5,6},{6,5},{8,11},{11,8},{9,1... | collective-permute-start | bytes 3840008 | tf_op jit(solution)/shard_map/ppermute | solution.py:150
  8.8 24.9 %all-to-all-start = ((bf16[64,16,128]{2,1,0:T(8,128)(2,1)}), bf16[64,16,128]{2,1,0:T(8,128)(2,1)S(1)}, u32[]{:S(2)}, u32[]{:S(2)}) async-start(bf16[64,16,128]{2,1,0:T(8,128)(2,1)} %bitcast.14), calls=%async_computation | async-start | bytes 524288 | tf_op jit(solution)/shard_map/all_to_all | solution.py:169
  28.1 15.4 %collective-permute-start.2 = (bf16[800,800]{1,0:T(8,128)(2,1)}, bf16[800,800]{1,0:T(8,128)(2,1)S(1)}, u32[]{:S(2)}, u32[]{:S(2)}) collective-permute-start(bf16[800,800]{1,0:T(8,128)(2,1)} %refs_7_.1), channel_id=1, source_target_pairs={{0,4},{4,0},{1,5},{5,1},{2,6},{6,2},{3,7},{7,3},{8,12},{12,8},{9,1... | collective-permute-start | bytes 3840008 | tf_op jit(solution)/shard_map/ppermute | solution.py:186
  33.7 9.8 %collective-permute-start = (bf16[64,2,8,128]{3,2,1,0:T(8,128)(2,1)S(1)}, bf16[64,2,8,128]{3,2,1,0:T(8,128)(2,1)S(1)}, u32[]{:S(2)}, u32[]{:S(2)}) collective-permute-start(bf16[64,2,8,128]{3,2,1,0:T(8,128)(2,1)S(1)} %bitcast.12), channel_id=1, source_target_pairs={{0,1},{1,0},{2,3},{3,2},{4,5},{5,4},{6,7},{7,6},{8,9},{9,8},{10,11... | collective-permute-start | bytes 786440 | tf_op jit(solution)/shard_map/ppermute | solution.py:173
  35.6 0.7 copy-start.1
  36.3 1.4 %copy-start.3 = (bf16[800,800]{1,0:T(8,128)(2,1)S(1)}, bf16[800,800]{1,0:T(8,128)(2,1)}, u32[]{:S(2)}) copy-start(bf16[800,800]{1,0:T(8,128)(2,1)} %refs_7_.1) | copy-start | bytes 3840004
  37.7 0.7 copy-start.4
  39.6 6.8 %collective-permute-start.3 = (bf16[800,800]{1,0:T(8,128)(2,1)S(1)}, bf16[800,800]{1,0:T(8,128)(2,1)S(1)}, u32[]{:S(2)}, u32[]{:S(2)}) collective-permute-start(bf16[800,800]{1,0:T(8,128)(2,1)S(1)} %collective-permute-done.1.refs_9_), channel_id=1, source_target_pairs={{0,4},{4,0},{1,5},{5,1},{2,6},{6,2},{3,7},{7,3},{8,12},{12,8},{9,1... | collective-permute-start | bytes 3840008 | tf_op jit(solution)/shard_map/ppermute | solution.py:188
  47.1 19.2 %copy-start.2 = (s32[800]{0:T(1024)S(1)}, s32[800]{0:T(1024)}, u32[]{:S(2)}) copy-start(s32[800]{0:T(1024)} %refs_2_.1) | copy-start | bytes 9604
  47.1 19.2 %copy-start.5 = (s32[4]{0:T(128)S(1)}, s32[4]{0:T(128)}, u32[]{:S(2)}) copy-start(s32[4]{0:T(128)} %param.12) | copy-start | bytes 52
  47.1 30.6 %copy-start = (bf16[1,3200]{1,0:T(2,128)(2,1)S(1)}, bf16[1,3200]{1,0:T(2,128)(2,1)}, u32[]{:S(2)}) copy-start(bf16[1,3200]{1,0:T(2,128)(2,1)} %old_ref.1) | copy-start | bytes 19204
  48.0 29.6 %all-to-all-start.1 = ((f16[128,16,128]{2,1,0:T(8,128)(2,1)}), f16[128,16,128]{2,1,0:T(8,128)(2,1)S(1)}, u32[]{:S(2)}, u32[]{:S(2)}) async-start(f16[128,16,128]{2,1,0:T(8,128)(2,1)} %bitcast.6), calls=%async_computation.1 | async-start | bytes 1048576 | tf_op jit(solution)/shard_map/all_to_all | solution.py:206

commit v9 on v8

--- a/solution.py
+++ b/solution.py
@@ -169,6 +169,9 @@
     mine = lax.all_to_all(
         cut.reshape(zy, 16, LANES), ("z", "y"), 0, 0, axis_index_groups=[ROLLED], tiled=True
     )
+    ab_irrep = jnp.bitwise_xor(upper_irrep[:, None], virt_irrep[None, :])
+    kept = (ab_irrep == cut[0, TILES, 0].astype(jnp.int32)).astype(F32)
+    mine, kept = lax.optimization_barrier((mine, kept))
     mine = mine.reshape(zy, 2, 8, LANES)
     there = lax.ppermute(mine, "x0", other_x0)
 
@@ -202,12 +205,9 @@
     )
     part = ladder(rows2, partner2, sums, own_sums)
     part = (part * SCALE).astype(F16).reshape(2 * zy, 16, LANES)
-    part, upper = lax.optimization_barrier((part, upper_irrep))
     back = lax.all_to_all(
         part, ("x0", "z", "y"), 0, 0, axis_index_groups=[ROLLED + [64 + i for i in ROLLED]], tiled=True
     )
-    ab_irrep = jnp.bitwise_xor(upper[:, None], virt_irrep[None, :])
-    kept = (ab_irrep == cut[0, TILES, 0].astype(jnp.int32)).astype(F32)
     sums = jnp.sum(back.reshape(2, zy, 16, LANES).astype(F32), axis=1)
     finish = call(finish_body, shape((1, 4 * NV), BF16), "svvv", 0, 50000)
     return finish(places, sums, kept, residual_in)

time: 79.4 us -> 78.4 us (0.987)
  blocking collectives: 0 us -> 29.4 us
  starting transfers between devices: 50.2 us -> 33.2 us
  waiting for transfers between devices: 14.2 us -> 0.86 us
    all_to_all x0 -> x1, blocking collectives: none -> 29.4 us  [per_device(): lax.all_to_all(part, ('x0', 'z', 'y'), 0, 0, axis_index_groups=[ROLLED +...]
    all_to_all x1 -> x0, starting transfers between devices: 16.4 us -> none  [per_device(): lax.all_to_all(part, ('x0', 'z', 'y'), 0, 0, axis_index_groups=[ROLLED +...]
    all_to_all x1 -> x0, waiting for transfers between devices: 11.2 us -> none  [per_device(): lax.all_to_all(part, ('x0', 'z', 'y'), 0, 0, axis_index_groups=[ROLLED +...]
    all_to_all x1, waiting for transfers between devices: 2.07 us -> 0.01 us  [per_device(): lax.all_to_all(cut.reshape(zy, 16, LANES), ('z', 'y'), 0, 0, axis_index_g...]
    convert_element_type x1, other arithmetic: 0.9 us -> 0.11 us  [per_device(): part = (part * SCALE).astype(F16).reshape(2 * zy, 16, LANES)]
    unnamed x12 -> x8, local copies, waits for them, and re-layouts: 2.71 us -> 2.7 us
  transfers between devices with their start and end apart: 6 -> 5, of which waited for: 3 -> 1; matrix products, arithmetic and copies ran while one was open for 2% -> 3% of each run, Pallas kernels for 8% -> 8%
where the time goes in v9:
time: 78.4 us; the launch traced here: 77.9 us
  starting transfers between devices  33.2 us (42%)
  blocking collectives  29.4 us (38%)
  Pallas kernels  8.05 us (10%)
  local copies, waits for them, and re-layouts  3.93 us (5%)
  between operations  1.47 us (2%)
  other arithmetic  1.04 us (1%)
  waiting for transfers between devices  0.86 us (1%)
    all_to_all x1, blocking collectives, per_device(): lax.all_to_all(part, ('x0', 'z', 'y'), 0, 0, axis_index_groups=[ROLLED +...  29.4 us
    all_to_all x1, starting transfers between devices, per_device(): lax.all_to_all(cut.reshape(zy, 16, LANES), ('z', 'y'), 0, 0, axis_index_g...  19.3 us
    ppermute x1, starting transfers between devices, per_device(): lax.ppermute(integrals, ('x1', 'x0'), [(0, 3), (3, 0), (1, 2), (2, 1)])  5.21 us
    ppermute x1, starting transfers between devices, per_device(): block2 = lax.ppermute(block, 'core', other_core)  3.43 us
    ppermute x1, starting transfers between devices, per_device(): partner2 = lax.ppermute(partner, 'core', other_core)  3.34 us
    pallas_call x1, Pallas kernels, per_device(): pl.pallas_call(functools.partial(cut_body, steps), in_specs=[pl.BlockSpec...  2.95 us
    unnamed x8, local copies, waits for them, and re-layouts  2.7 us
    pallas_call x1, Pallas kernels, per_device(): after(places, slab_irrep, virt_irrep, there, lhs, lhs2, sums, integrals,...  1.93 us
  transfers between devices with their start and end apart: 5, of which 1 were waited for; matrix products, arithmetic and copies ran while one was open for 3% of the time, Pallas kernels for 8%

profile of v9, /device:TPU:1, one launch (start us, length us, event | category | flops | bytes accessed | tf_op | source)
XLA Modules:
  0.0 77.9 jit_solution(10482845301794620971)
XLA Ops:
  0.0 5.2 %collective-permute-start.1 = (bf16[800,800]{1,0:T(8,128)(2,1)}, bf16[800,800]{1,0:T(8,128)(2,1)S(1)}, u32[]{:S(2)}, u32[]{:S(2)}) collective-permute-start(bf16[800,800]{1,0:T(8,128)(2,1)} %refs_7_.1), channel_id=1, source_target_pairs={{0,3},{3,0},{1,2},{2,1},{4,7},{7,4},{5,6},{6,5},{8,11},{11,8},{9,1... | collective-permute-start | bytes 3840008 | tf_op jit(solution)/shard_map/ppermute | solution.py:150
  5.9 2.9 %shard_map.73 = bf16[128,8,128]{2,1,0:T(8,128)(2,1)} custom-call(s32[1]{0:T(128)S(6)} %copy.8.pair_ref, bf16[1,102400]{1,0:T(2,128)(2,1)} %row_ref.1), custom_call_target="tpu_custom_call" | custom-call | bytes 700000 | tf_op jit(solution)/shard_map/pallas_call | solution.py:153
  8.8 19.3 %all-to-all-start = ((bf16[64,16,128]{2,1,0:T(8,128)(2,1)}), bf16[64,16,128]{2,1,0:T(8,128)(2,1)S(1)}, u32[]{:S(2)}, u32[]{:S(2)}) async-start(bf16[64,16,128]{2,1,0:T(8,128)(2,1)} %bitcast.15), calls=%async_computation | async-start | bytes 524288 | tf_op jit(solution)/shard_map/all_to_all | solution.py:169
  28.1 3.4 %collective-permute-start.2 = (bf16[800,800]{1,0:T(8,128)(2,1)}, bf16[800,800]{1,0:T(8,128)(2,1)S(1)}, u32[]{:S(2)}, u32[]{:S(2)}) collective-permute-start(bf16[800,800]{1,0:T(8,128)(2,1)} %refs_7_.1), channel_id=1, source_target_pairs={{0,4},{4,0},{1,5},{5,1},{2,6},{6,2},{3,7},{7,3},{8,12},{12,8},{9,1... | collective-permute-start | bytes 3840008 | tf_op jit(solution)/shard_map/ppermute | solution.py:189
  31.6 1.2 %slice.3 = bf16[1,1,1]{2,1,0:T(2,128)(2,1)} slice(bf16[128,8,128]{2,1,0:T(8,128)(2,1)} %shard_map.73), slice={[0:1], [7:8], [0:1]} | slice | bytes 4 | tf_op jit(solution)/shard_map/slice | solution.py:173
  33.5 0.1 pad_add_fusion.places_ref.refs_0_
  33.6 0.8 fusion.kept_ref
  34.3 0.0 all-to-all-done
  34.3 1.9 %collective-permute-start = (bf16[64,2,8,128]{3,2,1,0:T(8,128)(2,1)S(1)}, bf16[64,2,8,128]{3,2,1,0:T(8,128)(2,1)S(1)}, u32[]{:S(2)}, u32[]{:S(2)}) collective-permute-start(bf16[64,2,8,128]{3,2,1,0:T(8,128)(2,1)S(1)} %bitcast.12), channel_id=1, source_target_pairs={{0,1},{1,0},{2,3},{3,2},{4,5},{5,4},{6,7},{7,6},{8,9},{9,8},{10,11... | collective-permute-start | bytes 786440 | tf_op jit(solution)/shard_map/ppermute | solution.py:176
  36.3 0.0 copy-start.1
  36.3 0.7 copy-done.1
  36.9 0.0 copy-start.2
  36.9 1.4 %copy-done.2 = bf16[800,800]{1,0:T(8,128)(2,1)S(1)} copy-done((bf16[800,800]{1,0:T(8,128)(2,1)S(1)}, bf16[800,800]{1,0:T(8,128)(2,1)}, u32[]{:S(2)}) %copy-start.2) | copy-done | bytes 1280024
  38.3 0.0 copy-start.3
  38.3 0.7 copy-done.3
  39.0 1.2 %shard_map.74 = (bf16[64,800]{1,0:T(8,128)(2,1)S(1)}, bf16[64,800]{1,0:T(8,128)(2,1)S(1)}, f32[64,800]{1,0:T(8,128)S(1)}) custom-call(s32[4]{0:T(128)S(1)} %pad_add_fusion.places_ref.refs_0_, s32[128]{0:T(128)S(1)} %copy-done.3, s32[800]{0:T(1024)S(1)} %copy-done.1, bf16[64,2,8,128]{3,2,1,0:T(8,128)(2,1)S(1)} %bitcast.13, bf16[800,800]{1,0:T(8,128)(2,1)S(1)} %copy-done.2), custom_call_target="tpu_custom_call" | custom-call | flops 7200000000 | bytes 24000000 | tf_op jit(solution)/shard_map/pallas_call | solution.py:188
  40.2 0.0 collective-permute-done.1.refs_9_
  40.2 3.3 %collective-permute-start.3 = (bf16[800,800]{1,0:T(8,128)(2,1)S(1)}, bf16[800,800]{1,0:T(8,128)(2,1)S(1)}, u32[]{:S(2)}, u32[]{:S(2)}) collective-permute-start(bf16[800,800]{1,0:T(8,128)(2,1)S(1)} %collective-permute-done.1.refs_9_), channel_id=1, source_target_pairs={{0,4},{4,0},{1,5},{5,1},{2,6},{6,2},{3,7},{7,3},{8,12},{12,8},{9,1... | collective-permute-start | bytes 3840008 | tf_op jit(solution)/shard_map/ppermute | solution.py:191
  43.5 0.0 collective-permute-done.refs_3_
  43.5 0.0 collective-permute-done.2.refs_8_
  43.5 1.9 %shard_map.75 = (bf16[128,800]{1,0:T(8,128)(2,1)S(1)}, f32[1024,128]{1,0:T(8,128)S(1)}, f32[128,800]{1,0:T(8,128)S(1)}) custom-call(s32[4]{0:T(128)S(1)} %pad_add_fusion.places_ref.refs_0_, s32[128]{0:T(128)S(1)} %copy-done.3, s32[800]{0:T(1024)S(1)} %copy-done.1, bf16[64,2,8,128]{3,2,1,0:T(8,128)(2,1)S(1)} %collective-permute-done.refs_3_, ...), custom_call_target="tpu_custom_call" | custom-call | flops 12000000000 | bytes 40000000 | tf_op jit(solution)/shard_map/pallas_call | solution.py:200
  45.5 0.9 %collective-permute-done.3.block_ref = bf16[800,800]{1,0:T(8,128)(2,1)S(1)} collective-permute-done((bf16[800,800]{1,0:T(8,128)(2,1)S(1)}, bf16[800,800]{1,0:T(8,128)(2,1)S(1)}, u32[]{:S(2)}, u32[]{:S(2)}) %collective-permute-start.3) | collective-permute-done | bytes 1280032 | tf_op jit(solution)/shard_map/ppermute | solution.py:191
  46.3 0.7 shard_map.76
  47.1 0.0 copy-start
  47.1 0.1 multiply_convert_fusion
  47.2 29.4 %all_to_all.10 = f16[128,16,128]{2,1,0:T(8,128)(2,1)S(1)} all-to-all(f16[128,16,128]{2,1,0:T(8,128)(2,1)S(1)} %bitcast.14), channel_id=1, replica_groups={{288,296,304,312,256,264,272,280,352,360,368,376,320,328,336,344,416,42..., dimensions={0} | all-to-all | bytes 1048576 | tf_op jit(solution)/shard_map/all_to_all | solution.py:208
  76.6 0.1 convert_reduce_fusion.sums_ref
  76.7 0.0 copy-done
  76.7 1.3 %shard_map.77 = bf16[1,3200]{1,0:T(2,128)(2,1)} custom-call(s32[4]{0:T(128)S(1)} %pad_add_fusion.places_ref.refs_0_, f32[2,16,128]{2,1,0:T(8,128)S(1)} %convert_reduce_fusion.sums_ref, f32[4,800]{1,0:T(4,128)S(1)} %fusion.kept_ref, bf16[1,3200]{1,0:T(2,128)(2,1)S(1)} %copy-done), custom_call_target="tpu_custom_call" | custom-call | bytes 50000 | tf_op jit(solution)/shard_map/pallas_call | solution.py:213
Async XLA Ops:
  0.0 40.2 %collective-permute-start.1 = (bf16[800,800]{1,0:T(8,128)(2,1)}, bf16[800,800]{1,0:T(8,128)(2,1)S(1)}, u32[]{:S(2)}, u32[]{:S(2)}) collective-permute-start(bf16[800,800]{1,0:T(8,128)(2,1)} %refs_7_.1), channel_id=1, source_target_pairs={{0,3},{3,0},{1,2},{2,1},{4,7},{7,4},{5,6},{6,5},{8,11},{11,8},{9,1... | collective-permute-start | bytes 3840008 | tf_op jit(solution)/shard_map/ppermute | solution.py:150
  8.8 25.5 %all-to-all-start = ((bf16[64,16,128]{2,1,0:T(8,128)(2,1)}), bf16[64,16,128]{2,1,0:T(8,128)(2,1)S(1)}, u32[]{:S(2)}, u32[]{:S(2)}) async-start(bf16[64,16,128]{2,1,0:T(8,128)(2,1)} %bitcast.15), calls=%async_computation | async-start | bytes 524288 | tf_op jit(solution)/shard_map/all_to_all | solution.py:169
  28.1 15.4 %collective-permute-start.2 = (bf16[800,800]{1,0:T(8,128)(2,1)}, bf16[800,800]{1,0:T(8,128)(2,1)S(1)}, u32[]{:S(2)}, u32[]{:S(2)}) collective-permute-start(bf16[800,800]{1,0:T(8,128)(2,1)} %refs_7_.1), channel_id=1, source_target_pairs={{0,4},{4,0},{1,5},{5,1},{2,6},{6,2},{3,7},{7,3},{8,12},{12,8},{9,1... | collective-permute-start | bytes 3840008 | tf_op jit(solution)/shard_map/ppermute | solution.py:189
  34.3 9.2 %collective-permute-start = (bf16[64,2,8,128]{3,2,1,0:T(8,128)(2,1)S(1)}, bf16[64,2,8,128]{3,2,1,0:T(8,128)(2,1)S(1)}, u32[]{:S(2)}, u32[]{:S(2)}) collective-permute-start(bf16[64,2,8,128]{3,2,1,0:T(8,128)(2,1)S(1)} %bitcast.12), channel_id=1, source_target_pairs={{0,1},{1,0},{2,3},{3,2},{4,5},{5,4},{6,7},{7,6},{8,9},{9,8},{10,11... | collective-permute-start | bytes 786440 | tf_op jit(solution)/shard_map/ppermute | solution.py:176
  36.3 0.7 copy-start.1
  36.9 1.4 %copy-start.2 = (bf16[800,800]{1,0:T(8,128)(2,1)S(1)}, bf16[800,800]{1,0:T(8,128)(2,1)}, u32[]{:S(2)}) copy-start(bf16[800,800]{1,0:T(8,128)(2,1)} %refs_7_.1) | copy-start | bytes 3840004
  38.3 0.7 copy-start.3
  40.2 6.2 %collective-permute-start.3 = (bf16[800,800]{1,0:T(8,128)(2,1)S(1)}, bf16[800,800]{1,0:T(8,128)(2,1)S(1)}, u32[]{:S(2)}, u32[]{:S(2)}) collective-permute-start(bf16[800,800]{1,0:T(8,128)(2,1)S(1)} %collective-permute-done.1.refs_9_), channel_id=1, source_target_pairs={{0,4},{4,0},{1,5},{5,1},{2,6},{6,2},{3,7},{7,3},{8,12},{12,8},{9,1... | collective-permute-start | bytes 3840008 | tf_op jit(solution)/shard_map/ppermute | solution.py:191
  47.1 29.6 %copy-start = (bf16[1,3200]{1,0:T(2,128)(2,1)S(1)}, bf16[1,3200]{1,0:T(2,128)(2,1)}, u32[]{:S(2)}) copy-start(bf16[1,3200]{1,0:T(2,128)(2,1)} %old_ref.1) | copy-start | bytes 19204

commit v10 on v9

--- a/solution.py
+++ b/solution.py
@@ -72,7 +72,6 @@
     wide = jnp.concatenate([sums, jnp.zeros((count, WIDE - NV), F32)], axis=1)
     for t in range(TILES):
         out_ref[pl.ds(first + t, count, stride=step), :] = wide[:, t * LANES : (t + 1) * LANES]
-    out_ref[pl.ds(first + TILES, count, stride=step), :] = jnp.zeros((count, LANES), F32)
 
 
 def kept_rows(flip, zy, places_ref, slab_ref, virt_ref, tiles_ref, flat, wide, lhs_ref, first):
@@ -110,27 +109,27 @@
     own = jnp.dot(rows[pl.ds(there, zy), :], own_ref[...], preferred_element_type=F32)
     sums[pl.ds(there, zy), :] = own
     own = sums[...] + jnp.dot(rows2_ref[...], own2_ref[...], preferred_element_type=F32)
-    put_tiles(own, 2 * zy, own_sums_ref, 0, 8)
+    put_tiles(own, 2 * zy, own_sums_ref, 0, TILES)
     out_ref[...] = jnp.dot(rows[...], block_ref[...], preferred_element_type=F32)
 
 
 def ladder_body(zy, lhs_ref, block_ref, sums_ref, own_ref, out_ref):
     sums = sums_ref[...] + jnp.dot(lhs_ref[...], block_ref[...], preferred_element_type=F32)
-    put_tiles(sums, 2 * zy, out_ref, 8, 16)
-    for t in range(8):
-        out_ref[pl.ds(t, 2 * zy, stride=16), :] = own_ref[pl.ds(t, 2 * zy, stride=8), :]
+    put_tiles(sums, 2 * zy, out_ref, TILES, 2 * TILES)
+    for t in range(TILES):
+        out_ref[pl.ds(t, 2 * zy, stride=2 * TILES), :] = own_ref[pl.ds(t, 2 * zy, stride=TILES), :]
 
 
 def finish_body(places_ref, sums_ref, kept_ref, old_ref, out_ref):
     swap = places_ref[2] == 1
     order = ((0, 0), (1, 0), (1, 1), (0, 1))
     for a in range(4):
-        s, h = order[a]
-        s2, h2 = order[(a + 2) % 4]
-        straight = sums_ref[s, 8 * h : 8 * h + 8, :]
-        turned = sums_ref[s2, 8 * h2 : 8 * h2 + 8, :]
-        tiles = jnp.where(swap, turned, straight) * (1.0 / SCALE)
-        row = jnp.concatenate([tiles[t : t + 1, :] for t in range(TILES)], axis=1)[:, :NV]
+        (s, h), (s2, h2) = order[a], order[(a + 2) % 4]
+        tiles = []
+        for t in range(TILES):
+            (p, q), (p2, q2) = divmod(TILES * h + t, 2), divmod(TILES * h2 + t, 2)
+            tiles.append(jnp.where(swap, sums_ref[s2, p2, q2 : q2 + 1, :], sums_ref[s, p, q : q + 1, :]))
+        row = jnp.concatenate(tiles, axis=1)[:, :NV] * (1.0 / SCALE)
         row = jnp.where(kept_ref[a : a + 1, :] > 0.5, row, 0.0)
         old = old_ref[:, a * NV : (a + 1) * NV].astype(F32)
         out_ref[:, a * NV : (a + 1) * NV] = (old + row).astype(BF16)
@@ -191,7 +190,7 @@
     partner2 = lax.ppermute(partner, "core", other_core)
     after = call(
         functools.partial(there_body, zy),
-        [whole, shape((2 * zy * 8, LANES), F32), shape((2 * zy, NV), F32)],
+        [whole, shape((2 * zy * TILES, LANES), F32), shape((2 * zy, NV), F32)],
         "ssvvvvvvvv",
         40000000 * 300,
         40000000,
@@ -201,14 +200,14 @@
         places, slab_irrep, virt_irrep, there, lhs, lhs2, sums, integrals, block2, partner
     )
     ladder = call(
-        functools.partial(ladder_body, zy), shape((2 * zy * 16, LANES), F32), "vvvv", 1000, 3000000
+        functools.partial(ladder_body, zy), shape((2 * zy * 2 * TILES, LANES), F32), "vvvv", 1000, 3000000
     )
     part = ladder(rows2, partner2, sums, own_sums)
-    part = (part * SCALE).astype(F16).reshape(2 * zy, 16, LANES)
+    part = (part * SCALE).astype(F16).reshape(2 * zy, TILES, 2, LANES)
     back = lax.all_to_all(
         part, ("x0", "z", "y"), 0, 0, axis_index_groups=[ROLLED + [64 + i for i in ROLLED]], tiled=True
     )
-    sums = jnp.sum(back.reshape(2, zy, 16, LANES).astype(F32), axis=1)
+    sums = jnp.sum(back.reshape(2, zy, TILES, 2, LANES).astype(F32), axis=1)
     finish = call(finish_body, shape((1, 4 * NV), BF16), "svvv", 0, 50000)
     return finish(places, sums, kept, residual_in)
 

time: 78.4 us -> 77 us (0.982)
  blocking collectives: 29.4 us -> 28 us
    all_to_all x1, blocking collectives: 29.4 us -> 28 us  [per_device(): lax.all_to_all(part, ('x0', 'z', 'y'), 0, 0, axis_index_groups=[ROLLED +...]
where the time goes in v10:
time: 77 us; the launch traced here: 76.5 us
  starting transfers between devices  33.2 us (43%)
  blocking collectives  28 us (36%)
  Pallas kernels  7.72 us (10%)
  local copies, waits for them, and re-layouts  3.93 us (5%)
  between operations  1.46 us (2%)
  other arithmetic  1.31 us (2%)
  waiting for transfers between devices  0.9 us (1%)
    all_to_all x1, blocking collectives, per_device(): lax.all_to_all(part, ('x0', 'z', 'y'), 0, 0, axis_index_groups=[ROLLED +...  28 us
    all_to_all x1, starting transfers between devices, per_device(): lax.all_to_all(cut.reshape(zy, 16, LANES), ('z', 'y'), 0, 0, axis_index_g...  19.3 us
    ppermute x1, starting transfers between devices, per_device(): lax.ppermute(integrals, ('x1', 'x0'), [(0, 3), (3, 0), (1, 2), (2, 1)])  5.21 us
    ppermute x1, starting transfers between devices, per_device(): block2 = lax.ppermute(block, 'core', other_core)  3.43 us
    ppermute x1, starting transfers between devices, per_device(): partner2 = lax.ppermute(partner, 'core', other_core)  3.34 us
    pallas_call x1, Pallas kernels, per_device(): pl.pallas_call(functools.partial(cut_body, steps), in_specs=[pl.BlockSpec...  2.95 us
    unnamed x8, local copies, waits for them, and re-layouts  2.7 us
    ppermute x1, starting transfers between devices, per_device(): there = lax.ppermute(mine, 'x0', other_x0)  1.91 us
  transfers between devices with their start and end apart: 5, of which 1 were waited for; matrix products, arithmetic and copies ran while one was open for 3% of the time, Pallas kernels for 8%

profile of v10, /device:TPU:1, one launch (start us, length us, event | category | flops | bytes accessed | tf_op | source)
XLA Modules:
  0.0 76.5 jit_solution(6418370886631589686)
XLA Ops:
  0.0 5.2 %collective-permute-start.1 = (bf16[800,800]{1,0:T(8,128)(2,1)}, bf16[800,800]{1,0:T(8,128)(2,1)S(1)}, u32[]{:S(2)}, u32[]{:S(2)}) collective-permute-start(bf16[800,800]{1,0:T(8,128)(2,1)} %refs_7_.1), channel_id=1, source_target_pairs={{0,3},{3,0},{1,2},{2,1},{4,7},{7,4},{5,6},{6,5},{8,11},{11,8},{9,1... | collective-permute-start | bytes 3840008 | tf_op jit(solution)/shard_map/ppermute | solution.py:149
  5.9 2.9 %shard_map.73 = bf16[128,8,128]{2,1,0:T(8,128)(2,1)} custom-call(s32[1]{0:T(128)S(6)} %copy.8.pair_ref, bf16[1,102400]{1,0:T(2,128)(2,1)} %row_ref.1), custom_call_target="tpu_custom_call" | custom-call | bytes 700000 | tf_op jit(solution)/shard_map/pallas_call | solution.py:152
  8.8 19.3 %all-to-all-start = ((bf16[64,16,128]{2,1,0:T(8,128)(2,1)}), bf16[64,16,128]{2,1,0:T(8,128)(2,1)S(1)}, u32[]{:S(2)}, u32[]{:S(2)}) async-start(bf16[64,16,128]{2,1,0:T(8,128)(2,1)} %bitcast.15), calls=%async_computation | async-start | bytes 524288 | tf_op jit(solution)/shard_map/all_to_all | solution.py:168
  28.1 3.4 %collective-permute-start.2 = (bf16[800,800]{1,0:T(8,128)(2,1)}, bf16[800,800]{1,0:T(8,128)(2,1)S(1)}, u32[]{:S(2)}, u32[]{:S(2)}) collective-permute-start(bf16[800,800]{1,0:T(8,128)(2,1)} %refs_7_.1), channel_id=1, source_target_pairs={{0,4},{4,0},{1,5},{5,1},{2,6},{6,2},{3,7},{7,3},{8,12},{12,8},{9,1... | collective-permute-start | bytes 3840008 | tf_op jit(solution)/shard_map/ppermute | solution.py:188
  31.6 1.2 %slice.3 = bf16[1,1,1]{2,1,0:T(2,128)(2,1)} slice(bf16[128,8,128]{2,1,0:T(8,128)(2,1)} %shard_map.73), slice={[0:1], [7:8], [0:1]} | slice | bytes 4 | tf_op jit(solution)/shard_map/slice | solution.py:172
  33.5 0.1 pad_add_fusion.places_ref.refs_0_
  33.6 0.8 fusion.kept_ref
  34.3 0.0 all-to-all-done
  34.3 1.9 %collective-permute-start = (bf16[64,2,8,128]{3,2,1,0:T(8,128)(2,1)S(1)}, bf16[64,2,8,128]{3,2,1,0:T(8,128)(2,1)S(1)}, u32[]{:S(2)}, u32[]{:S(2)}) collective-permute-start(bf16[64,2,8,128]{3,2,1,0:T(8,128)(2,1)S(1)} %bitcast.12), channel_id=1, source_target_pairs={{0,1},{1,0},{2,3},{3,2},{4,5},{5,4},{6,7},{7,6},{8,9},{9,8},{10,11... | collective-permute-start | bytes 786440 | tf_op jit(solution)/shard_map/ppermute | solution.py:175
  36.3 0.0 copy-start.1
  36.3 0.7 copy-done.1
  36.9 0.0 copy-start.2
  36.9 1.4 %copy-done.2 = bf16[800,800]{1,0:T(8,128)(2,1)S(1)} copy-done((bf16[800,800]{1,0:T(8,128)(2,1)S(1)}, bf16[800,800]{1,0:T(8,128)(2,1)}, u32[]{:S(2)}) %copy-start.2) | copy-done | bytes 1280024
  38.3 0.0 copy-start.3
  38.3 0.7 copy-done.3
  39.0 1.2 %shard_map.74 = (bf16[64,800]{1,0:T(8,128)(2,1)S(1)}, bf16[64,800]{1,0:T(8,128)(2,1)S(1)}, f32[64,800]{1,0:T(8,128)S(1)}) custom-call(s32[4]{0:T(128)S(1)} %pad_add_fusion.places_ref.refs_0_, s32[128]{0:T(128)S(1)} %copy-done.3, s32[800]{0:T(1024)S(1)} %copy-done.1, bf16[64,2,8,128]{3,2,1,0:T(8,128)(2,1)S(1)} %bitcast.13, bf16[800,800]{1,0:T(8,128)(2,1)S(1)} %copy-done.2), custom_call_target="tpu_custom_call" | custom-call | flops 7200000000 | bytes 24000000 | tf_op jit(solution)/shard_map/pallas_call | solution.py:187
  40.2 0.0 collective-permute-done.1.refs_9_
  40.2 3.3 %collective-permute-start.3 = (bf16[800,800]{1,0:T(8,128)(2,1)S(1)}, bf16[800,800]{1,0:T(8,128)(2,1)S(1)}, u32[]{:S(2)}, u32[]{:S(2)}) collective-permute-start(bf16[800,800]{1,0:T(8,128)(2,1)S(1)} %collective-permute-done.1.refs_9_), channel_id=1, source_target_pairs={{0,4},{4,0},{1,5},{5,1},{2,6},{6,2},{3,7},{7,3},{8,12},{12,8},{9,1... | collective-permute-start | bytes 3840008 | tf_op jit(solution)/shard_map/ppermute | solution.py:190
  43.5 0.0 collective-permute-done.refs_3_
  43.5 0.0 collective-permute-done.2.refs_8_
  43.5 1.9 %shard_map.75 = (bf16[128,800]{1,0:T(8,128)(2,1)S(1)}, f32[896,128]{1,0:T(8,128)S(1)}, f32[128,800]{1,0:T(8,128)S(1)}) custom-call(s32[4]{0:T(128)S(1)} %pad_add_fusion.places_ref.refs_0_, s32[128]{0:T(128)S(1)} %copy-done.3, s32[800]{0:T(1024)S(1)} %copy-done.1, bf16[64,2,8,128]{3,2,1,0:T(8,128)(2,1)S(1)} %collective-permute-done.refs_3_, ...), custom_call_target="tpu_custom_call" | custom-call | flops 12000000000 | bytes 40000000 | tf_op jit(solution)/shard_map/pallas_call | solution.py:199
  45.5 0.9 %collective-permute-done.3.block_ref = bf16[800,800]{1,0:T(8,128)(2,1)S(1)} collective-permute-done((bf16[800,800]{1,0:T(8,128)(2,1)S(1)}, bf16[800,800]{1,0:T(8,128)(2,1)S(1)}, u32[]{:S(2)}, u32[]{:S(2)}) %collective-permute-start.3) | collective-permute-done | bytes 1280032 | tf_op jit(solution)/shard_map/ppermute | solution.py:190
  46.3 0.4 shard_map.76
  46.8 0.0 copy-start
  46.8 0.1 multiply_convert_fusion
  46.9 28.0 %all_to_all.10 = f16[128,7,2,128]{3,2,1,0:T(2,128)(2,1)S(1)} all-to-all(f16[128,7,2,128]{3,2,1,0:T(2,128)(2,1)S(1)} %bitcast.14), channel_id=1, replica_groups={{288,296,304,312,256,264,272,280,352,360,368,376,320,328,336,344,416,42..., dimensions={0} | all-to-all | bytes 917504 | tf_op jit(solution)/shard_map/all_to_all | solution.py:207
  74.9 0.4 convert_reduce_fusion.sums_ref
  75.3 0.0 copy-done
  75.3 1.3 %shard_map.77 = bf16[1,3200]{1,0:T(2,128)(2,1)} custom-call(s32[4]{0:T(128)S(1)} %pad_add_fusion.places_ref.refs_0_, f32[2,7,2,128]{3,2,1,0:T(2,128)S(1)} %convert_reduce_fusion.sums_ref, f32[4,800]{1,0:T(4,128)S(1)} %fusion.kept_ref, bf16[1,3200]{1,0:T(2,128)(2,1)S(1)} %copy-done), custom_call_target="tpu_custom_call" | custom-call | bytes 50000 | tf_op jit(solution)/shard_map/pallas_call | solution.py:212
Async XLA Ops:
  0.0 40.2 %collective-permute-start.1 = (bf16[800,800]{1,0:T(8,128)(2,1)}, bf16[800,800]{1,0:T(8,128)(2,1)S(1)}, u32[]{:S(2)}, u32[]{:S(2)}) collective-permute-start(bf16[800,800]{1,0:T(8,128)(2,1)} %refs_7_.1), channel_id=1, source_target_pairs={{0,3},{3,0},{1,2},{2,1},{4,7},{7,4},{5,6},{6,5},{8,11},{11,8},{9,1... | collective-permute-start | bytes 3840008 | tf_op jit(solution)/shard_map/ppermute | solution.py:149
  8.8 25.5 %all-to-all-start = ((bf16[64,16,128]{2,1,0:T(8,128)(2,1)}), bf16[64,16,128]{2,1,0:T(8,128)(2,1)S(1)}, u32[]{:S(2)}, u32[]{:S(2)}) async-start(bf16[64,16,128]{2,1,0:T(8,128)(2,1)} %bitcast.15), calls=%async_computation | async-start | bytes 524288 | tf_op jit(solution)/shard_map/all_to_all | solution.py:168
  28.1 15.4 %collective-permute-start.2 = (bf16[800,800]{1,0:T(8,128)(2,1)}, bf16[800,800]{1,0:T(8,128)(2,1)S(1)}, u32[]{:S(2)}, u32[]{:S(2)}) collective-permute-start(bf16[800,800]{1,0:T(8,128)(2,1)} %refs_7_.1), channel_id=1, source_target_pairs={{0,4},{4,0},{1,5},{5,1},{2,6},{6,2},{3,7},{7,3},{8,12},{12,8},{9,1... | collective-permute-start | bytes 3840008 | tf_op jit(solution)/shard_map/ppermute | solution.py:188
  34.3 9.2 %collective-permute-start = (bf16[64,2,8,128]{3,2,1,0:T(8,128)(2,1)S(1)}, bf16[64,2,8,128]{3,2,1,0:T(8,128)(2,1)S(1)}, u32[]{:S(2)}, u32[]{:S(2)}) collective-permute-start(bf16[64,2,8,128]{3,2,1,0:T(8,128)(2,1)S(1)} %bitcast.12), channel_id=1, source_target_pairs={{0,1},{1,0},{2,3},{3,2},{4,5},{5,4},{6,7},{7,6},{8,9},{9,8},{10,11... | collective-permute-start | bytes 786440 | tf_op jit(solution)/shard_map/ppermute | solution.py:175
  36.3 0.7 copy-start.1
  36.9 1.4 %copy-start.2 = (bf16[800,800]{1,0:T(8,128)(2,1)S(1)}, bf16[800,800]{1,0:T(8,128)(2,1)}, u32[]{:S(2)}) copy-start(bf16[800,800]{1,0:T(8,128)(2,1)} %refs_7_.1) | copy-start | bytes 3840004
  38.3 0.7 copy-start.3
  40.2 6.2 %collective-permute-start.3 = (bf16[800,800]{1,0:T(8,128)(2,1)S(1)}, bf16[800,800]{1,0:T(8,128)(2,1)S(1)}, u32[]{:S(2)}, u32[]{:S(2)}) collective-permute-start(bf16[800,800]{1,0:T(8,128)(2,1)S(1)} %collective-permute-done.1.refs_9_), channel_id=1, source_target_pairs={{0,4},{4,0},{1,5},{5,1},{2,6},{6,2},{3,7},{7,3},{8,12},{12,8},{9,1... | collective-permute-start | bytes 3840008 | tf_op jit(solution)/shard_map/ppermute | solution.py:190
  46.8 28.5 %copy-start = (bf16[1,3200]{1,0:T(2,128)(2,1)S(1)}, bf16[1,3200]{1,0:T(2,128)(2,1)}, u32[]{:S(2)}) copy-start(bf16[1,3200]{1,0:T(2,128)(2,1)} %old_ref.1) | copy-start | bytes 19204

commit v11 on v10

--- a/solution.py
+++ b/solution.py
@@ -14,7 +14,8 @@
 LANES = 128
 TILES = 7
 WIDE = TILES * LANES
-ROLLED = [(z + 4) % 8 * 8 + (y + 4) % 8 for z in range(8) for y in range(8)]
+FIRST_Z = 7
+ROLLED = [(z + FIRST_Z) % 8 * 8 + (y + 4) % 8 for z in range(8) for y in range(8)]
 SCALE = 64.0
 
 VMEM = pl.BlockSpec(memory_space=pltpu.VMEM)
@@ -35,14 +36,15 @@
 
 def cut_body(steps, pair_ref, row_ref, out_ref, pair, row, cut, pair_sem, in_sems, out_sems):
     lanes, slabs = row.shape[1] // steps, cut.shape[0] // steps
+    rows = slabs // 2
 
     def fetch(i):
         part = pl.ds(i * lanes, lanes)
         return pltpu.make_async_copy(row_ref.at[:, part], row.at[:, part], in_sems.at[i])
 
-    def put(i):
-        part = pl.ds(i * slabs, slabs)
-        return pltpu.make_async_copy(cut.at[part], out_ref.at[part], out_sems.at[i])
+    def put(z):
+        part = cut.at[pl.ds(z * rows, rows)]
+        return pltpu.make_async_copy(part, out_ref.at[pl.ds((z - FIRST_Z) % 8 * rows, rows)], out_sems.at[z])
 
     label = pltpu.make_async_copy(pair_ref, pair, pair_sem)
     label.start()
@@ -51,9 +53,7 @@
         for r in range(4):
             at = [pl.multiple_of(q * 3200 + (6 * r + t) * LANES, LANES) for t in range(TILES)]
             tiles = [row[:, pl.ds(a, LANES)].astype(F32) for a in at]
-            chip = 2 * q + r // 2
-            place = (chip // 8 + 4) % 8 * 8 + (chip + 4) % 8
-            cut[2 * place + r % 2] = jnp.concatenate(tiles + [filler], axis=0).astype(BF16)
+            cut[4 * jnp.bitwise_xor(q, 2) + r] = jnp.concatenate(tiles + [filler], axis=0).astype(BF16)
         return carry
 
     for i in range(steps):
@@ -63,9 +63,10 @@
     for i in range(steps):
         fetch(i).wait()
         lax.fori_loop(i * slabs // 4, (i + 1) * slabs // 4, four, 0, unroll=4)
-        put((i + 2) % 4).start()
-    for i in range(steps):
-        put(i).wait()
+        put(2 * i).start()
+        put(2 * i + 1).start()
+    for z in range(2 * steps):
+        put(z).wait()
 
 
 def put_tiles(sums, count, out_ref, first, step):
@@ -160,7 +161,7 @@
             pltpu.VMEM((2 * zy, 8, LANES), BF16),
             pltpu.SemaphoreType.DMA,
             pltpu.SemaphoreType.DMA((steps,)),
-            pltpu.SemaphoreType.DMA((steps,)),
+            pltpu.SemaphoreType.DMA((2 * steps,)),
         ],
         cost_estimate=pl.CostEstimate(flops=0, bytes_accessed=700000, transcendentals=0),
     )(pair_irrep, amplitudes)

time: 77 us -> 78.4 us (1.018)
  waiting for transfers between devices: 0.9 us -> 3.37 us
    all_to_all x1, waiting for transfers between devices: 0.01 us -> 2.48 us  [per_device(): lax.all_to_all(cut.reshape(zy, 16, LANES), ('z', 'y'), 0, 0, axis_index_g...]
    all_to_all x1, starting transfers between devices: 19.3 us -> 18.1 us  [per_device(): lax.all_to_all(cut.reshape(zy, 16, LANES), ('z', 'y'), 0, 0, axis_index_g...]
    ppermute x1, starting transfers between devices: 3.34 us -> 4.18 us  [per_device(): partner2 = lax.ppermute(partner, 'core', other_core)]
  transfers between devices with their start and end apart: 5 -> 5, of which waited for: 1 -> 2; matrix products, arithmetic and copies ran while one was open for 3% -> 3% of each run, Pallas kernels for 8% -> 7%
where the time goes in v11:
time: 78.4 us; the launch traced here: 77.9 us
  starting transfers between devices  32.6 us (42%)
  blocking collectives  28.1 us (36%)
  Pallas kernels  7.16 us (9%)
  local copies, waits for them, and re-layouts  3.93 us (5%)
  waiting for transfers between devices  3.37 us (4%)
  between operations  1.46 us (2%)
  other arithmetic  1.31 us (2%)
    all_to_all x1, blocking collectives, per_device(): lax.all_to_all(part, ('x0', 'z', 'y'), 0, 0, axis_index_groups=[ROLLED +...  28.1 us
    all_to_all x1, starting transfers between devices, per_device(): lax.all_to_all(cut.reshape(zy, 16, LANES), ('z', 'y'), 0, 0, axis_index_g...  18.1 us
    ppermute x1, starting transfers between devices, per_device(): lax.ppermute(integrals, ('x1', 'x0'), [(0, 3), (3, 0), (1, 2), (2, 1)])  5.21 us
    ppermute x1, starting transfers between devices, per_device(): partner2 = lax.ppermute(partner, 'core', other_core)  4.18 us
    ppermute x1, starting transfers between devices, per_device(): block2 = lax.ppermute(block, 'core', other_core)  3.15 us
    unnamed x8, local copies, waits for them, and re-layouts  2.7 us
    all_to_all x1, waiting for transfers between devices, per_device(): lax.all_to_all(cut.reshape(zy, 16, LANES), ('z', 'y'), 0, 0, axis_index_g...  2.48 us
    pallas_call x1, Pallas kernels, per_device(): pl.pallas_call(functools.partial(cut_body, steps), in_specs=[pl.BlockSpec...  2.39 us
  transfers between devices with their start and end apart: 5, of which 2 were waited for; matrix products, arithmetic and copies ran while one was open for 3% of the time, Pallas kernels for 7%

profile of v11, /device:TPU:1, one launch (start us, length us, event | category | flops | bytes accessed | tf_op | source)
XLA Modules:
  0.0 77.9 jit_solution(14033639578131153093)
XLA Ops:
  0.0 5.2 %collective-permute-start.1 = (bf16[800,800]{1,0:T(8,128)(2,1)}, bf16[800,800]{1,0:T(8,128)(2,1)S(1)}, u32[]{:S(2)}, u32[]{:S(2)}) collective-permute-start(bf16[800,800]{1,0:T(8,128)(2,1)} %refs_7_.1), channel_id=1, source_target_pairs={{0,3},{3,0},{1,2},{2,1},{4,7},{7,4},{5,6},{6,5},{8,11},{11,8},{9,1... | collective-permute-start | bytes 3840008 | tf_op jit(solution)/shard_map/ppermute | solution.py:150
  5.9 2.4 %shard_map.73 = bf16[128,8,128]{2,1,0:T(8,128)(2,1)} custom-call(s32[1]{0:T(128)S(6)} %copy.8.pair_ref, bf16[1,102400]{1,0:T(2,128)(2,1)} %row_ref.1), custom_call_target="tpu_custom_call" | custom-call | bytes 700000 | tf_op jit(solution)/shard_map/pallas_call | solution.py:153
  8.3 18.1 %all-to-all-start = ((bf16[64,16,128]{2,1,0:T(8,128)(2,1)}), bf16[64,16,128]{2,1,0:T(8,128)(2,1)S(1)}, u32[]{:S(2)}, u32[]{:S(2)}) async-start(bf16[64,16,128]{2,1,0:T(8,128)(2,1)} %bitcast.15), calls=%async_computation | async-start | bytes 524288 | tf_op jit(solution)/shard_map/all_to_all | solution.py:169
  26.4 3.1 %collective-permute-start.2 = (bf16[800,800]{1,0:T(8,128)(2,1)}, bf16[800,800]{1,0:T(8,128)(2,1)S(1)}, u32[]{:S(2)}, u32[]{:S(2)}) collective-permute-start(bf16[800,800]{1,0:T(8,128)(2,1)} %refs_7_.1), channel_id=1, source_target_pairs={{0,4},{4,0},{1,5},{5,1},{2,6},{6,2},{3,7},{7,3},{8,12},{12,8},{9,1... | collective-permute-start | bytes 3840008 | tf_op jit(solution)/shard_map/ppermute | solution.py:189
  29.6 1.2 %slice.3 = bf16[1,1,1]{2,1,0:T(2,128)(2,1)} slice(bf16[128,8,128]{2,1,0:T(8,128)(2,1)} %shard_map.73), slice={[0:1], [7:8], [0:1]} | slice | bytes 4 | tf_op jit(solution)/shard_map/slice | solution.py:173
  31.5 0.1 pad_add_fusion.places_ref.refs_0_
  31.6 0.8 fusion.kept_ref
  32.3 2.5 %all-to-all-done = bf16[64,16,128]{2,1,0:T(8,128)(2,1)S(1)} async-done(((bf16[64,16,128]{2,1,0:T(8,128)(2,1)}), bf16[64,16,128]{2,1,0:T(8,128)(2,1)S(1)}, u32[]{:S(2)}, u32[]{:S(2)}) %all-to-all-start) | async-done | bytes 262176 | tf_op jit(solution)/shard_map/all_to_all | solution.py:169
  34.8 1.9 %collective-permute-start = (bf16[64,2,8,128]{3,2,1,0:T(8,128)(2,1)S(1)}, bf16[64,2,8,128]{3,2,1,0:T(8,128)(2,1)S(1)}, u32[]{:S(2)}, u32[]{:S(2)}) collective-permute-start(bf16[64,2,8,128]{3,2,1,0:T(8,128)(2,1)S(1)} %bitcast.12), channel_id=1, source_target_pairs={{0,1},{1,0},{2,3},{3,2},{4,5},{5,4},{6,7},{7,6},{8,9},{9,8},{10,11... | collective-permute-start | bytes 786440 | tf_op jit(solution)/shard_map/ppermute | solution.py:176
  36.7 0.0 copy-start.1
  36.7 0.7 copy-done.1
  37.4 0.0 copy-start.2
  37.4 1.4 %copy-done.2 = bf16[800,800]{1,0:T(8,128)(2,1)S(1)} copy-done((bf16[800,800]{1,0:T(8,128)(2,1)S(1)}, bf16[800,800]{1,0:T(8,128)(2,1)}, u32[]{:S(2)}) %copy-start.2) | copy-done | bytes 1280024
  38.8 0.0 copy-start.3
  38.8 0.7 copy-done.3
  39.4 1.2 %shard_map.74 = (bf16[64,800]{1,0:T(8,128)(2,1)S(1)}, bf16[64,800]{1,0:T(8,128)(2,1)S(1)}, f32[64,800]{1,0:T(8,128)S(1)}) custom-call(s32[4]{0:T(128)S(1)} %pad_add_fusion.places_ref.refs_0_, s32[128]{0:T(128)S(1)} %copy-done.3, s32[800]{0:T(1024)S(1)} %copy-done.1, bf16[64,2,8,128]{3,2,1,0:T(8,128)(2,1)S(1)} %bitcast.13, bf16[800,800]{1,0:T(8,128)(2,1)S(1)} %copy-done.2), custom_call_target="tpu_custom_call" | custom-call | flops 7200000000 | bytes 24000000 | tf_op jit(solution)/shard_map/pallas_call | solution.py:188
  40.6 0.0 collective-permute-done.1.refs_9_
  40.6 4.2 %collective-permute-start.3 = (bf16[800,800]{1,0:T(8,128)(2,1)S(1)}, bf16[800,800]{1,0:T(8,128)(2,1)S(1)}, u32[]{:S(2)}, u32[]{:S(2)}) collective-permute-start(bf16[800,800]{1,0:T(8,128)(2,1)S(1)} %collective-permute-done.1.refs_9_), channel_id=1, source_target_pairs={{0,4},{4,0},{1,5},{5,1},{2,6},{6,2},{3,7},{7,3},{8,12},{12,8},{9,1... | collective-permute-start | bytes 3840008 | tf_op jit(solution)/shard_map/ppermute | solution.py:191
  44.8 0.0 collective-permute-done.refs_3_
  44.8 0.0 collective-permute-done.2.refs_8_
  44.9 1.9 %shard_map.75 = (bf16[128,800]{1,0:T(8,128)(2,1)S(1)}, f32[896,128]{1,0:T(8,128)S(1)}, f32[128,800]{1,0:T(8,128)S(1)}) custom-call(s32[4]{0:T(128)S(1)} %pad_add_fusion.places_ref.refs_0_, s32[128]{0:T(128)S(1)} %copy-done.3, s32[800]{0:T(1024)S(1)} %copy-done.1, bf16[64,2,8,128]{3,2,1,0:T(8,128)(2,1)S(1)} %collective-permute-done.refs_3_, ...), custom_call_target="tpu_custom_call" | custom-call | flops 12000000000 | bytes 40000000 | tf_op jit(solution)/shard_map/pallas_call | solution.py:200
  46.8 0.9 %collective-permute-done.3.block_ref = bf16[800,800]{1,0:T(8,128)(2,1)S(1)} collective-permute-done((bf16[800,800]{1,0:T(8,128)(2,1)S(1)}, bf16[800,800]{1,0:T(8,128)(2,1)S(1)}, u32[]{:S(2)}, u32[]{:S(2)}) %collective-permute-start.3) | collective-permute-done | bytes 1280032 | tf_op jit(solution)/shard_map/ppermute | solution.py:191
  47.7 0.4 shard_map.76
  48.1 0.0 copy-start
  48.1 0.1 multiply_convert_fusion
  48.2 28.1 %all_to_all.10 = f16[128,7,2,128]{3,2,1,0:T(2,128)(2,1)S(1)} all-to-all(f16[128,7,2,128]{3,2,1,0:T(2,128)(2,1)S(1)} %bitcast.14), channel_id=1, replica_groups={{480,488,496,504,448,456,464,472,32,40,48,56,0,8,16,24,96,104,112,120,6..., dimensions={0} | all-to-all | bytes 917504 | tf_op jit(solution)/shard_map/all_to_all | solution.py:208
  76.3 0.4 convert_reduce_fusion.sums_ref
  76.7 0.0 copy-done
  76.7 1.3 %shard_map.77 = bf16[1,3200]{1,0:T(2,128)(2,1)} custom-call(s32[4]{0:T(128)S(1)} %pad_add_fusion.places_ref.refs_0_, f32[2,7,2,128]{3,2,1,0:T(2,128)S(1)} %convert_reduce_fusion.sums_ref, f32[4,800]{1,0:T(4,128)S(1)} %fusion.kept_ref, bf16[1,3200]{1,0:T(2,128)(2,1)S(1)} %copy-done), custom_call_target="tpu_custom_call" | custom-call | bytes 50000 | tf_op jit(solution)/shard_map/pallas_call | solution.py:213
Async XLA Ops:
  0.0 40.6 %collective-permute-start.1 = (bf16[800,800]{1,0:T(8,128)(2,1)}, bf16[800,800]{1,0:T(8,128)(2,1)S(1)}, u32[]{:S(2)}, u32[]{:S(2)}) collective-permute-start(bf16[800,800]{1,0:T(8,128)(2,1)} %refs_7_.1), channel_id=1, source_target_pairs={{0,3},{3,0},{1,2},{2,1},{4,7},{7,4},{5,6},{6,5},{8,11},{11,8},{9,1... | collective-permute-start | bytes 3840008 | tf_op jit(solution)/shard_map/ppermute | solution.py:150
  8.3 26.5 %all-to-all-start = ((bf16[64,16,128]{2,1,0:T(8,128)(2,1)}), bf16[64,16,128]{2,1,0:T(8,128)(2,1)S(1)}, u32[]{:S(2)}, u32[]{:S(2)}) async-start(bf16[64,16,128]{2,1,0:T(8,128)(2,1)} %bitcast.15), calls=%async_computation | async-start | bytes 524288 | tf_op jit(solution)/shard_map/all_to_all | solution.py:169
  26.4 18.4 %collective-permute-start.2 = (bf16[800,800]{1,0:T(8,128)(2,1)}, bf16[800,800]{1,0:T(8,128)(2,1)S(1)}, u32[]{:S(2)}, u32[]{:S(2)}) collective-permute-start(bf16[800,800]{1,0:T(8,128)(2,1)} %refs_7_.1), channel_id=1, source_target_pairs={{0,4},{4,0},{1,5},{5,1},{2,6},{6,2},{3,7},{7,3},{8,12},{12,8},{9,1... | collective-permute-start | bytes 3840008 | tf_op jit(solution)/shard_map/ppermute | solution.py:189
  34.8 10.0 %collective-permute-start = (bf16[64,2,8,128]{3,2,1,0:T(8,128)(2,1)S(1)}, bf16[64,2,8,128]{3,2,1,0:T(8,128)(2,1)S(1)}, u32[]{:S(2)}, u32[]{:S(2)}) collective-permute-start(bf16[64,2,8,128]{3,2,1,0:T(8,128)(2,1)S(1)} %bitcast.12), channel_id=1, source_target_pairs={{0,1},{1,0},{2,3},{3,2},{4,5},{5,4},{6,7},{7,6},{8,9},{9,8},{10,11... | collective-permute-start | bytes 786440 | tf_op jit(solution)/shard_map/ppermute | solution.py:176
  36.7 0.7 copy-start.1
  37.4 1.4 %copy-start.2 = (bf16[800,800]{1,0:T(8,128)(2,1)S(1)}, bf16[800,800]{1,0:T(8,128)(2,1)}, u32[]{:S(2)}) copy-start(bf16[800,800]{1,0:T(8,128)(2,1)} %refs_7_.1) | copy-start | bytes 3840004
  38.8 0.7 copy-start.3
  40.6 7.0 %collective-permute-start.3 = (bf16[800,800]{1,0:T(8,128)(2,1)S(1)}, bf16[800,800]{1,0:T(8,128)(2,1)S(1)}, u32[]{:S(2)}, u32[]{:S(2)}) collective-permute-start(bf16[800,800]{1,0:T(8,128)(2,1)S(1)} %collective-permute-done.1.refs_9_), channel_id=1, source_target_pairs={{0,4},{4,0},{1,5},{5,1},{2,6},{6,2},{3,7},{7,3},{8,12},{12,8},{9,1... | collective-permute-start | bytes 3840008 | tf_op jit(solution)/shard_map/ppermute | solution.py:191
  48.1 28.6 %copy-start = (bf16[1,3200]{1,0:T(2,128)(2,1)S(1)}, bf16[1,3200]{1,0:T(2,128)(2,1)}, u32[]{:S(2)}) copy-start(bf16[1,3200]{1,0:T(2,128)(2,1)} %old_ref.1) | copy-start | bytes 19204

commit v12 on v11

--- a/solution.py
+++ b/solution.py
@@ -14,7 +14,7 @@
 LANES = 128
 TILES = 7
 WIDE = TILES * LANES
-FIRST_Z = 7
+FIRST_Z = 4
 ROLLED = [(z + FIRST_Z) % 8 * 8 + (y + 4) % 8 for z in range(8) for y in range(8)]
 SCALE = 64.0
 

time: 78.4 us -> 77 us (0.982)
  waiting for transfers between devices: 3.37 us -> 0.9 us
    all_to_all x1, waiting for transfers between devices: 2.48 us -> 0.01 us  [per_device(): lax.all_to_all(cut.reshape(zy, 16, LANES), ('z', 'y'), 0, 0, axis_index_g...]
    all_to_all x1, starting transfers between devices: 18.1 us -> 19.3 us  [per_device(): lax.all_to_all(cut.reshape(zy, 16, LANES), ('z', 'y'), 0, 0, axis_index_g...]
    ppermute x1, starting transfers between devices: 4.18 us -> 3.33 us  [per_device(): partner2 = lax.ppermute(partner, 'core', other_core)]
  transfers between devices with their start and end apart: 5 -> 5, of which waited for: 2 -> 1; matrix products, arithmetic and copies ran while one was open for 3% -> 3% of each run, Pallas kernels for 7% -> 7%
where the time goes in v12:
time: 77 us; the launch traced here: 76.5 us
  starting transfers between devices  33.2 us (43%)
  blocking collectives  28.6 us (37%)
  Pallas kernels  7.16 us (9%)
  local copies, waits for them, and re-layouts  3.93 us (5%)
  between operations  1.46 us (2%)
  other arithmetic  1.31 us (2%)
  waiting for transfers between devices  0.9 us (1%)
    all_to_all x1, blocking collectives, per_device(): lax.all_to_all(part, ('x0', 'z', 'y'), 0, 0, axis_index_groups=[ROLLED +...  28.6 us
    all_to_all x1, starting transfers between devices, per_device(): lax.all_to_all(cut.reshape(zy, 16, LANES), ('z', 'y'), 0, 0, axis_index_g...  19.3 us
    ppermute x1, starting transfers between devices, per_device(): lax.ppermute(integrals, ('x1', 'x0'), [(0, 3), (3, 0), (1, 2), (2, 1)])  5.21 us
    ppermute x1, starting transfers between devices, per_device(): block2 = lax.ppermute(block, 'core', other_core)  3.43 us
    ppermute x1, starting transfers between devices, per_device(): partner2 = lax.ppermute(partner, 'core', other_core)  3.33 us
    unnamed x8, local copies, waits for them, and re-layouts  2.7 us
    pallas_call x1, Pallas kernels, per_device(): pl.pallas_call(functools.partial(cut_body, steps), in_specs=[pl.BlockSpec...  2.39 us
    ppermute x1, starting transfers between devices, per_device(): there = lax.ppermute(mine, 'x0', other_x0)  1.91 us
  transfers between devices with their start and end apart: 5, of which 1 were waited for; matrix products, arithmetic and copies ran while one was open for 3% of the time, Pallas kernels for 7%

profile of v12, /device:TPU:1, one launch (start us, length us, event | category | flops | bytes accessed | tf_op | source)
XLA Modules:
  0.0 76.5 jit_solution(4044988339589635478)
XLA Ops:
  0.0 5.2 %collective-permute-start.1 = (bf16[800,800]{1,0:T(8,128)(2,1)}, bf16[800,800]{1,0:T(8,128)(2,1)S(1)}, u32[]{:S(2)}, u32[]{:S(2)}) collective-permute-start(bf16[800,800]{1,0:T(8,128)(2,1)} %refs_7_.1), channel_id=1, source_target_pairs={{0,3},{3,0},{1,2},{2,1},{4,7},{7,4},{5,6},{6,5},{8,11},{11,8},{9,1... | collective-permute-start | bytes 3840008 | tf_op jit(solution)/shard_map/ppermute | solution.py:150
  5.9 2.4 %shard_map.73 = bf16[128,8,128]{2,1,0:T(8,128)(2,1)} custom-call(s32[1]{0:T(128)S(6)} %copy.8.pair_ref, bf16[1,102400]{1,0:T(2,128)(2,1)} %row_ref.1), custom_call_target="tpu_custom_call" | custom-call | bytes 700000 | tf_op jit(solution)/shard_map/pallas_call | solution.py:153
  8.3 19.3 %all-to-all-start = ((bf16[64,16,128]{2,1,0:T(8,128)(2,1)}), bf16[64,16,128]{2,1,0:T(8,128)(2,1)S(1)}, u32[]{:S(2)}, u32[]{:S(2)}) async-start(bf16[64,16,128]{2,1,0:T(8,128)(2,1)} %bitcast.15), calls=%async_computation | async-start | bytes 524288 | tf_op jit(solution)/shard_map/all_to_all | solution.py:169
  27.6 3.4 %collective-permute-start.2 = (bf16[800,800]{1,0:T(8,128)(2,1)}, bf16[800,800]{1,0:T(8,128)(2,1)S(1)}, u32[]{:S(2)}, u32[]{:S(2)}) collective-permute-start(bf16[800,800]{1,0:T(8,128)(2,1)} %refs_7_.1), channel_id=1, source_target_pairs={{0,4},{4,0},{1,5},{5,1},{2,6},{6,2},{3,7},{7,3},{8,12},{12,8},{9,1... | collective-permute-start | bytes 3840008 | tf_op jit(solution)/shard_map/ppermute | solution.py:189
  31.0 1.2 %slice.3 = bf16[1,1,1]{2,1,0:T(2,128)(2,1)} slice(bf16[128,8,128]{2,1,0:T(8,128)(2,1)} %shard_map.73), slice={[0:1], [7:8], [0:1]} | slice | bytes 4 | tf_op jit(solution)/shard_map/slice | solution.py:173
  32.9 0.1 pad_add_fusion.places_ref.refs_0_
  33.0 0.8 fusion.kept_ref
  33.8 0.0 all-to-all-done
  33.8 1.9 %collective-permute-start = (bf16[64,2,8,128]{3,2,1,0:T(8,128)(2,1)S(1)}, bf16[64,2,8,128]{3,2,1,0:T(8,128)(2,1)S(1)}, u32[]{:S(2)}, u32[]{:S(2)}) collective-permute-start(bf16[64,2,8,128]{3,2,1,0:T(8,128)(2,1)S(1)} %bitcast.12), channel_id=1, source_target_pairs={{0,1},{1,0},{2,3},{3,2},{4,5},{5,4},{6,7},{7,6},{8,9},{9,8},{10,11... | collective-permute-start | bytes 786440 | tf_op jit(solution)/shard_map/ppermute | solution.py:176
  35.7 0.0 copy-start.1
  35.7 0.7 copy-done.1
  36.4 0.0 copy-start.2
  36.4 1.4 %copy-done.2 = bf16[800,800]{1,0:T(8,128)(2,1)S(1)} copy-done((bf16[800,800]{1,0:T(8,128)(2,1)S(1)}, bf16[800,800]{1,0:T(8,128)(2,1)}, u32[]{:S(2)}) %copy-start.2) | copy-done | bytes 1280024
  37.7 0.0 copy-start.3
  37.7 0.7 copy-done.3
  38.4 1.2 %shard_map.74 = (bf16[64,800]{1,0:T(8,128)(2,1)S(1)}, bf16[64,800]{1,0:T(8,128)(2,1)S(1)}, f32[64,800]{1,0:T(8,128)S(1)}) custom-call(s32[4]{0:T(128)S(1)} %pad_add_fusion.places_ref.refs_0_, s32[128]{0:T(128)S(1)} %copy-done.3, s32[800]{0:T(1024)S(1)} %copy-done.1, bf16[64,2,8,128]{3,2,1,0:T(8,128)(2,1)S(1)} %bitcast.13, bf16[800,800]{1,0:T(8,128)(2,1)S(1)} %copy-done.2), custom_call_target="tpu_custom_call" | custom-call | flops 7200000000 | bytes 24000000 | tf_op jit(solution)/shard_map/pallas_call | solution.py:188
  39.6 0.0 collective-permute-done.1.refs_9_
  39.6 3.3 %collective-permute-start.3 = (bf16[800,800]{1,0:T(8,128)(2,1)S(1)}, bf16[800,800]{1,0:T(8,128)(2,1)S(1)}, u32[]{:S(2)}, u32[]{:S(2)}) collective-permute-start(bf16[800,800]{1,0:T(8,128)(2,1)S(1)} %collective-permute-done.1.refs_9_), channel_id=1, source_target_pairs={{0,4},{4,0},{1,5},{5,1},{2,6},{6,2},{3,7},{7,3},{8,12},{12,8},{9,1... | collective-permute-start | bytes 3840008 | tf_op jit(solution)/shard_map/ppermute | solution.py:191
  43.0 0.0 collective-permute-done.refs_3_
  43.0 0.0 collective-permute-done.2.refs_8_
  43.0 1.9 %shard_map.75 = (bf16[128,800]{1,0:T(8,128)(2,1)S(1)}, f32[896,128]{1,0:T(8,128)S(1)}, f32[128,800]{1,0:T(8,128)S(1)}) custom-call(s32[4]{0:T(128)S(1)} %pad_add_fusion.places_ref.refs_0_, s32[128]{0:T(128)S(1)} %copy-done.3, s32[800]{0:T(1024)S(1)} %copy-done.1, bf16[64,2,8,128]{3,2,1,0:T(8,128)(2,1)S(1)} %collective-permute-done.refs_3_, ...), custom_call_target="tpu_custom_call" | custom-call | flops 12000000000 | bytes 40000000 | tf_op jit(solution)/shard_map/pallas_call | solution.py:200
  44.9 0.9 %collective-permute-done.3.block_ref = bf16[800,800]{1,0:T(8,128)(2,1)S(1)} collective-permute-done((bf16[800,800]{1,0:T(8,128)(2,1)S(1)}, bf16[800,800]{1,0:T(8,128)(2,1)S(1)}, u32[]{:S(2)}, u32[]{:S(2)}) %collective-permute-start.3) | collective-permute-done | bytes 1280032 | tf_op jit(solution)/shard_map/ppermute | solution.py:191
  45.8 0.4 shard_map.76
  46.2 0.0 copy-start
  46.2 0.1 multiply_convert_fusion
  46.3 28.6 %all_to_all.10 = f16[128,7,2,128]{3,2,1,0:T(2,128)(2,1)S(1)} all-to-all(f16[128,7,2,128]{3,2,1,0:T(2,128)(2,1)S(1)} %bitcast.14), channel_id=1, replica_groups={{288,296,304,312,256,264,272,280,352,360,368,376,320,328,336,344,416,42..., dimensions={0} | all-to-all | bytes 917504 | tf_op jit(solution)/shard_map/all_to_all | solution.py:208
  74.9 0.4 convert_reduce_fusion.sums_ref
  75.3 0.0 copy-done
  75.3 1.3 %shard_map.77 = bf16[1,3200]{1,0:T(2,128)(2,1)} custom-call(s32[4]{0:T(128)S(1)} %pad_add_fusion.places_ref.refs_0_, f32[2,7,2,128]{3,2,1,0:T(2,128)S(1)} %convert_reduce_fusion.sums_ref, f32[4,800]{1,0:T(4,128)S(1)} %fusion.kept_ref, bf16[1,3200]{1,0:T(2,128)(2,1)S(1)} %copy-done), custom_call_target="tpu_custom_call" | custom-call | bytes 50000 | tf_op jit(solution)/shard_map/pallas_call | solution.py:213
Async XLA Ops:
  0.0 39.6 %collective-permute-start.1 = (bf16[800,800]{1,0:T(8,128)(2,1)}, bf16[800,800]{1,0:T(8,128)(2,1)S(1)}, u32[]{:S(2)}, u32[]{:S(2)}) collective-permute-start(bf16[800,800]{1,0:T(8,128)(2,1)} %refs_7_.1), channel_id=1, source_target_pairs={{0,3},{3,0},{1,2},{2,1},{4,7},{7,4},{5,6},{6,5},{8,11},{11,8},{9,1... | collective-permute-start | bytes 3840008 | tf_op jit(solution)/shard_map/ppermute | solution.py:150
  8.3 25.5 %all-to-all-start = ((bf16[64,16,128]{2,1,0:T(8,128)(2,1)}), bf16[64,16,128]{2,1,0:T(8,128)(2,1)S(1)}, u32[]{:S(2)}, u32[]{:S(2)}) async-start(bf16[64,16,128]{2,1,0:T(8,128)(2,1)} %bitcast.15), calls=%async_computation | async-start | bytes 524288 | tf_op jit(solution)/shard_map/all_to_all | solution.py:169
  27.6 15.4 %collective-permute-start.2 = (bf16[800,800]{1,0:T(8,128)(2,1)}, bf16[800,800]{1,0:T(8,128)(2,1)S(1)}, u32[]{:S(2)}, u32[]{:S(2)}) collective-permute-start(bf16[800,800]{1,0:T(8,128)(2,1)} %refs_7_.1), channel_id=1, source_target_pairs={{0,4},{4,0},{1,5},{5,1},{2,6},{6,2},{3,7},{7,3},{8,12},{12,8},{9,1... | collective-permute-start | bytes 3840008 | tf_op jit(solution)/shard_map/ppermute | solution.py:189
  33.8 9.2 %collective-permute-start = (bf16[64,2,8,128]{3,2,1,0:T(8,128)(2,1)S(1)}, bf16[64,2,8,128]{3,2,1,0:T(8,128)(2,1)S(1)}, u32[]{:S(2)}, u32[]{:S(2)}) collective-permute-start(bf16[64,2,8,128]{3,2,1,0:T(8,128)(2,1)S(1)} %bitcast.12), channel_id=1, source_target_pairs={{0,1},{1,0},{2,3},{3,2},{4,5},{5,4},{6,7},{7,6},{8,9},{9,8},{10,11... | collective-permute-start | bytes 786440 | tf_op jit(solution)/shard_map/ppermute | solution.py:176
  35.7 0.7 copy-start.1
  36.4 1.4 %copy-start.2 = (bf16[800,800]{1,0:T(8,128)(2,1)S(1)}, bf16[800,800]{1,0:T(8,128)(2,1)}, u32[]{:S(2)}) copy-start(bf16[800,800]{1,0:T(8,128)(2,1)} %refs_7_.1) | copy-start | bytes 3840004
  37.7 0.7 copy-start.3
  39.6 6.2 %collective-permute-start.3 = (bf16[800,800]{1,0:T(8,128)(2,1)S(1)}, bf16[800,800]{1,0:T(8,128)(2,1)S(1)}, u32[]{:S(2)}, u32[]{:S(2)}) collective-permute-start(bf16[800,800]{1,0:T(8,128)(2,1)S(1)} %collective-permute-done.1.refs_9_), channel_id=1, source_target_pairs={{0,4},{4,0},{1,5},{5,1},{2,6},{6,2},{3,7},{7,3},{8,12},{12,8},{9,1... | collective-permute-start | bytes 3840008 | tf_op jit(solution)/shard_map/ppermute | solution.py:191
  46.2 29.0 %copy-start = (bf16[1,3200]{1,0:T(2,128)(2,1)S(1)}, bf16[1,3200]{1,0:T(2,128)(2,1)}, u32[]{:S(2)}) copy-start(bf16[1,3200]{1,0:T(2,128)(2,1)} %old_ref.1) | copy-start | bytes 19204

commit v13 on v12

--- a/solution.py
+++ b/solution.py
@@ -14,8 +14,8 @@
 LANES = 128
 TILES = 7
 WIDE = TILES * LANES
-FIRST_Z = 4
-ROLLED = [(z + FIRST_Z) % 8 * 8 + (y + 4) % 8 for z in range(8) for y in range(8)]
+ORDER_Z = (4, 0, 1, 2, 3, 5, 6, 7)
+ROLLED = [z * 8 + (y + 4) % 8 for z in ORDER_Z for y in range(8)]
 SCALE = 64.0
 
 VMEM = pl.BlockSpec(memory_space=pltpu.VMEM)
@@ -44,7 +44,7 @@
 
     def put(z):
         part = cut.at[pl.ds(z * rows, rows)]
-        return pltpu.make_async_copy(part, out_ref.at[pl.ds((z - FIRST_Z) % 8 * rows, rows)], out_sems.at[z])
+        return pltpu.make_async_copy(part, out_ref.at[pl.ds(ORDER_Z.index(z) * rows, rows)], out_sems.at[z])
 
     label = pltpu.make_async_copy(pair_ref, pair, pair_sem)
     label.start()

time: 77 us -> 76.9 us (level)
  no operation moved by 1% of the time
where the time goes in v13:
time: 76.9 us; the launch traced here: 76.4 us
  starting transfers between devices  33.3 us (43%)
  blocking collectives  28.4 us (37%)
  Pallas kernels  7.16 us (9%)
  local copies, waits for them, and re-layouts  3.93 us (5%)
  between operations  1.46 us (2%)
  other arithmetic  1.31 us (2%)
  waiting for transfers between devices  0.9 us (1%)
    all_to_all x1, blocking collectives, per_device(): lax.all_to_all(part, ('x0', 'z', 'y'), 0, 0, axis_index_groups=[ROLLED +...  28.4 us
    all_to_all x1, starting transfers between devices, per_device(): lax.all_to_all(cut.reshape(zy, 16, LANES), ('z', 'y'), 0, 0, axis_index_g...  19.2 us
    ppermute x1, starting transfers between devices, per_device(): lax.ppermute(integrals, ('x1', 'x0'), [(0, 3), (3, 0), (1, 2), (2, 1)])  5.21 us
    ppermute x1, starting transfers between devices, per_device(): partner2 = lax.ppermute(partner, 'core', other_core)  3.54 us
    ppermute x1, starting transfers between devices, per_device(): block2 = lax.ppermute(block, 'core', other_core)  3.43 us
    unnamed x8, local copies, waits for them, and re-layouts  2.7 us
    pallas_call x1, Pallas kernels, per_device(): pl.pallas_call(functools.partial(cut_body, steps), in_specs=[pl.BlockSpec...  2.39 us
    ppermute x1, starting transfers between devices, per_device(): there = lax.ppermute(mine, 'x0', other_x0)  1.91 us
  transfers between devices with their start and end apart: 5, of which 1 were waited for; matrix products, arithmetic and copies ran while one was open for 3% of the time, Pallas kernels for 7%

profile of v13, /device:TPU:1, one launch (start us, length us, event | category | flops | bytes accessed | tf_op | source)
XLA Modules:
  0.0 76.4 jit_solution(3539198726847414030)
XLA Ops:
  0.0 5.2 %collective-permute-start.1 = (bf16[800,800]{1,0:T(8,128)(2,1)}, bf16[800,800]{1,0:T(8,128)(2,1)S(1)}, u32[]{:S(2)}, u32[]{:S(2)}) collective-permute-start(bf16[800,800]{1,0:T(8,128)(2,1)} %refs_7_.1), channel_id=1, source_target_pairs={{0,3},{3,0},{1,2},{2,1},{4,7},{7,4},{5,6},{6,5},{8,11},{11,8},{9,1... | collective-permute-start | bytes 3840008 | tf_op jit(solution)/shard_map/ppermute | solution.py:150
  5.9 2.4 %shard_map.73 = bf16[128,8,128]{2,1,0:T(8,128)(2,1)} custom-call(s32[1]{0:T(128)S(6)} %copy.8.pair_ref, bf16[1,102400]{1,0:T(2,128)(2,1)} %row_ref.1), custom_call_target="tpu_custom_call" | custom-call | bytes 700000 | tf_op jit(solution)/shard_map/pallas_call | solution.py:153
  8.3 19.2 %all-to-all-start = ((bf16[64,16,128]{2,1,0:T(8,128)(2,1)}), bf16[64,16,128]{2,1,0:T(8,128)(2,1)S(1)}, u32[]{:S(2)}, u32[]{:S(2)}) async-start(bf16[64,16,128]{2,1,0:T(8,128)(2,1)} %bitcast.15), calls=%async_computation | async-start | bytes 524288 | tf_op jit(solution)/shard_map/all_to_all | solution.py:169
  27.5 3.4 %collective-permute-start.2 = (bf16[800,800]{1,0:T(8,128)(2,1)}, bf16[800,800]{1,0:T(8,128)(2,1)S(1)}, u32[]{:S(2)}, u32[]{:S(2)}) collective-permute-start(bf16[800,800]{1,0:T(8,128)(2,1)} %refs_7_.1), channel_id=1, source_target_pairs={{0,4},{4,0},{1,5},{5,1},{2,6},{6,2},{3,7},{7,3},{8,12},{12,8},{9,1... | collective-permute-start | bytes 3840008 | tf_op jit(solution)/shard_map/ppermute | solution.py:189
  30.9 1.2 %slice.3 = bf16[1,1,1]{2,1,0:T(2,128)(2,1)} slice(bf16[128,8,128]{2,1,0:T(8,128)(2,1)} %shard_map.73), slice={[0:1], [7:8], [0:1]} | slice | bytes 4 | tf_op jit(solution)/shard_map/slice | solution.py:173
  32.8 0.1 pad_add_fusion.places_ref.refs_0_
  32.9 0.8 fusion.kept_ref
  33.7 0.0 all-to-all-done
  33.7 1.9 %collective-permute-start = (bf16[64,2,8,128]{3,2,1,0:T(8,128)(2,1)S(1)}, bf16[64,2,8,128]{3,2,1,0:T(8,128)(2,1)S(1)}, u32[]{:S(2)}, u32[]{:S(2)}) collective-permute-start(bf16[64,2,8,128]{3,2,1,0:T(8,128)(2,1)S(1)} %bitcast.12), channel_id=1, source_target_pairs={{0,1},{1,0},{2,3},{3,2},{4,5},{5,4},{6,7},{7,6},{8,9},{9,8},{10,11... | collective-permute-start | bytes 786440 | tf_op jit(solution)/shard_map/ppermute | solution.py:176
  35.6 0.0 copy-start.1
  35.6 0.7 copy-done.1
  36.3 0.0 copy-start.2
  36.3 1.4 %copy-done.2 = bf16[800,800]{1,0:T(8,128)(2,1)S(1)} copy-done((bf16[800,800]{1,0:T(8,128)(2,1)S(1)}, bf16[800,800]{1,0:T(8,128)(2,1)}, u32[]{:S(2)}) %copy-start.2) | copy-done | bytes 1280024
  37.6 0.0 copy-start.3
  37.6 0.7 copy-done.3
  38.3 1.2 %shard_map.74 = (bf16[64,800]{1,0:T(8,128)(2,1)S(1)}, bf16[64,800]{1,0:T(8,128)(2,1)S(1)}, f32[64,800]{1,0:T(8,128)S(1)}) custom-call(s32[4]{0:T(128)S(1)} %pad_add_fusion.places_ref.refs_0_, s32[128]{0:T(128)S(1)} %copy-done.3, s32[800]{0:T(1024)S(1)} %copy-done.1, bf16[64,2,8,128]{3,2,1,0:T(8,128)(2,1)S(1)} %bitcast.13, bf16[800,800]{1,0:T(8,128)(2,1)S(1)} %copy-done.2), custom_call_target="tpu_custom_call" | custom-call | flops 7200000000 | bytes 24000000 | tf_op jit(solution)/shard_map/pallas_call | solution.py:188
  39.5 0.0 collective-permute-done.1.refs_9_
  39.5 3.5 %collective-permute-start.3 = (bf16[800,800]{1,0:T(8,128)(2,1)S(1)}, bf16[800,800]{1,0:T(8,128)(2,1)S(1)}, u32[]{:S(2)}, u32[]{:S(2)}) collective-permute-start(bf16[800,800]{1,0:T(8,128)(2,1)S(1)} %collective-permute-done.1.refs_9_), channel_id=1, source_target_pairs={{0,4},{4,0},{1,5},{5,1},{2,6},{6,2},{3,7},{7,3},{8,12},{12,8},{9,1... | collective-permute-start | bytes 3840008 | tf_op jit(solution)/shard_map/ppermute | solution.py:191
  43.0 0.0 collective-permute-done.refs_3_
  43.1 0.0 collective-permute-done.2.refs_8_
  43.1 1.9 %shard_map.75 = (bf16[128,800]{1,0:T(8,128)(2,1)S(1)}, f32[896,128]{1,0:T(8,128)S(1)}, f32[128,800]{1,0:T(8,128)S(1)}) custom-call(s32[4]{0:T(128)S(1)} %pad_add_fusion.places_ref.refs_0_, s32[128]{0:T(128)S(1)} %copy-done.3, s32[800]{0:T(1024)S(1)} %copy-done.1, bf16[64,2,8,128]{3,2,1,0:T(8,128)(2,1)S(1)} %collective-permute-done.refs_3_, ...), custom_call_target="tpu_custom_call" | custom-call | flops 12000000000 | bytes 40000000 | tf_op jit(solution)/shard_map/pallas_call | solution.py:200
  45.0 0.9 %collective-permute-done.3.block_ref = bf16[800,800]{1,0:T(8,128)(2,1)S(1)} collective-permute-done((bf16[800,800]{1,0:T(8,128)(2,1)S(1)}, bf16[800,800]{1,0:T(8,128)(2,1)S(1)}, u32[]{:S(2)}, u32[]{:S(2)}) %collective-permute-start.3) | collective-permute-done | bytes 1280032 | tf_op jit(solution)/shard_map/ppermute | solution.py:191
  45.9 0.4 shard_map.76
  46.3 0.0 copy-start
  46.3 0.1 multiply_convert_fusion
  46.4 28.4 %all_to_all.10 = f16[128,7,2,128]{3,2,1,0:T(2,128)(2,1)S(1)} all-to-all(f16[128,7,2,128]{3,2,1,0:T(2,128)(2,1)S(1)} %bitcast.14), channel_id=1, replica_groups={{288,296,304,312,256,264,272,280,32,40,48,56,0,8,16,24,96,104,112,120,6..., dimensions={0} | all-to-all | bytes 917504 | tf_op jit(solution)/shard_map/all_to_all | solution.py:208
  74.7 0.4 convert_reduce_fusion.sums_ref
  75.1 0.0 copy-done
  75.1 1.3 %shard_map.77 = bf16[1,3200]{1,0:T(2,128)(2,1)} custom-call(s32[4]{0:T(128)S(1)} %pad_add_fusion.places_ref.refs_0_, f32[2,7,2,128]{3,2,1,0:T(2,128)S(1)} %convert_reduce_fusion.sums_ref, f32[4,800]{1,0:T(4,128)S(1)} %fusion.kept_ref, bf16[1,3200]{1,0:T(2,128)(2,1)S(1)} %copy-done), custom_call_target="tpu_custom_call" | custom-call | bytes 50000 | tf_op jit(solution)/shard_map/pallas_call | solution.py:213
Async XLA Ops:
  0.0 39.5 %collective-permute-start.1 = (bf16[800,800]{1,0:T(8,128)(2,1)}, bf16[800,800]{1,0:T(8,128)(2,1)S(1)}, u32[]{:S(2)}, u32[]{:S(2)}) collective-permute-start(bf16[800,800]{1,0:T(8,128)(2,1)} %refs_7_.1), channel_id=1, source_target_pairs={{0,3},{3,0},{1,2},{2,1},{4,7},{7,4},{5,6},{6,5},{8,11},{11,8},{9,1... | collective-permute-start | bytes 3840008 | tf_op jit(solution)/shard_map/ppermute | solution.py:150
  8.3 25.4 %all-to-all-start = ((bf16[64,16,128]{2,1,0:T(8,128)(2,1)}), bf16[64,16,128]{2,1,0:T(8,128)(2,1)S(1)}, u32[]{:S(2)}, u32[]{:S(2)}) async-start(bf16[64,16,128]{2,1,0:T(8,128)(2,1)} %bitcast.15), calls=%async_computation | async-start | bytes 524288 | tf_op jit(solution)/shard_map/all_to_all | solution.py:169
  27.5 15.6 %collective-permute-start.2 = (bf16[800,800]{1,0:T(8,128)(2,1)}, bf16[800,800]{1,0:T(8,128)(2,1)S(1)}, u32[]{:S(2)}, u32[]{:S(2)}) collective-permute-start(bf16[800,800]{1,0:T(8,128)(2,1)} %refs_7_.1), channel_id=1, source_target_pairs={{0,4},{4,0},{1,5},{5,1},{2,6},{6,2},{3,7},{7,3},{8,12},{12,8},{9,1... | collective-permute-start | bytes 3840008 | tf_op jit(solution)/shard_map/ppermute | solution.py:189
  33.7 9.4 %collective-permute-start = (bf16[64,2,8,128]{3,2,1,0:T(8,128)(2,1)S(1)}, bf16[64,2,8,128]{3,2,1,0:T(8,128)(2,1)S(1)}, u32[]{:S(2)}, u32[]{:S(2)}) collective-permute-start(bf16[64,2,8,128]{3,2,1,0:T(8,128)(2,1)S(1)} %bitcast.12), channel_id=1, source_target_pairs={{0,1},{1,0},{2,3},{3,2},{4,5},{5,4},{6,7},{7,6},{8,9},{9,8},{10,11... | collective-permute-start | bytes 786440 | tf_op jit(solution)/shard_map/ppermute | solution.py:176
  35.6 0.7 copy-start.1
  36.3 1.4 %copy-start.2 = (bf16[800,800]{1,0:T(8,128)(2,1)S(1)}, bf16[800,800]{1,0:T(8,128)(2,1)}, u32[]{:S(2)}) copy-start(bf16[800,800]{1,0:T(8,128)(2,1)} %refs_7_.1) | copy-start | bytes 3840004
  37.6 0.7 copy-start.3
  39.5 6.4 %collective-permute-start.3 = (bf16[800,800]{1,0:T(8,128)(2,1)S(1)}, bf16[800,800]{1,0:T(8,128)(2,1)S(1)}, u32[]{:S(2)}, u32[]{:S(2)}) collective-permute-start(bf16[800,800]{1,0:T(8,128)(2,1)S(1)} %collective-permute-done.1.refs_9_), channel_id=1, source_target_pairs={{0,4},{4,0},{1,5},{5,1},{2,6},{6,2},{3,7},{7,3},{8,12},{12,8},{9,1... | collective-permute-start | bytes 3840008 | tf_op jit(solution)/shard_map/ppermute | solution.py:191
  46.3 28.8 %copy-start = (bf16[1,3200]{1,0:T(2,128)(2,1)S(1)}, bf16[1,3200]{1,0:T(2,128)(2,1)}, u32[]{:S(2)}) copy-start(bf16[1,3200]{1,0:T(2,128)(2,1)} %old_ref.1) | copy-start | bytes 19204

commit v14 on v13

--- a/solution.py
+++ b/solution.py
@@ -121,8 +121,8 @@
         out_ref[pl.ds(t, 2 * zy, stride=2 * TILES), :] = own_ref[pl.ds(t, 2 * zy, stride=TILES), :]
 
 
-def finish_body(places_ref, sums_ref, kept_ref, old_ref, out_ref):
-    swap = places_ref[2] == 1
+def finish_body(sums_ref, kept_ref, old_ref, out_ref):
+    swap = kept_ref[4:5, 0:LANES] > 0.5
     order = ((0, 0), (1, 0), (1, 1), (0, 1))
     for a in range(4):
         (s, h), (s2, h2) = order[a], order[(a + 2) % 4]
@@ -171,6 +171,7 @@
     )
     ab_irrep = jnp.bitwise_xor(upper_irrep[:, None], virt_irrep[None, :])
     kept = (ab_irrep == cut[0, TILES, 0].astype(jnp.int32)).astype(F32)
+    kept = jnp.concatenate([kept, jnp.broadcast_to(x1.astype(F32), (1, NV))])
     mine, kept = lax.optimization_barrier((mine, kept))
     mine = mine.reshape(zy, 2, 8, LANES)
     there = lax.ppermute(mine, "x0", other_x0)
@@ -209,8 +210,8 @@
         part, ("x0", "z", "y"), 0, 0, axis_index_groups=[ROLLED + [64 + i for i in ROLLED]], tiled=True
     )
     sums = jnp.sum(back.reshape(2, zy, TILES, 2, LANES).astype(F32), axis=1)
-    finish = call(finish_body, shape((1, 4 * NV), BF16), "svvv", 0, 50000)
-    return finish(places, sums, kept, residual_in)
+    finish = call(finish_body, shape((1, 4 * NV), BF16), "vvv", 0, 50000)
+    return finish(sums, kept, residual_in)
 
 
 def solution(mesh):

time: 76.9 us -> 76.4 us (level)
  no operation moved by 1% of the time
where the time goes in v14:
time: 76.4 us; the launch traced here: 75.8 us
  starting transfers between devices  33.3 us (44%)
  blocking collectives  28.4 us (37%)
  Pallas kernels  6.61 us (9%)
  local copies, waits for them, and re-layouts  3.94 us (5%)
  between operations  1.47 us (2%)
  other arithmetic  1.31 us (2%)
  waiting for transfers between devices  0.9 us (1%)
    all_to_all x1, blocking collectives, per_device(): lax.all_to_all(part, ('x0', 'z', 'y'), 0, 0, axis_index_groups=[ROLLED +...  28.4 us
    all_to_all x1, starting transfers between devices, per_device(): lax.all_to_all(cut.reshape(zy, 16, LANES), ('z', 'y'), 0, 0, axis_index_g...  19.2 us
    ppermute x1, starting transfers between devices, per_device(): lax.ppermute(integrals, ('x1', 'x0'), [(0, 3), (3, 0), (1, 2), (2, 1)])  5.21 us
    ppermute x1, starting transfers between devices, per_device(): partner2 = lax.ppermute(partner, 'core', other_core)  3.52 us
    ppermute x1, starting transfers between devices, per_device(): block2 = lax.ppermute(block, 'core', other_core)  3.43 us
    unnamed x8, local copies, waits for them, and re-layouts  2.7 us
    pallas_call x1, Pallas kernels, per_device(): pl.pallas_call(functools.partial(cut_body, steps), in_specs=[pl.BlockSpec...  2.39 us
    ppermute x1, starting transfers between devices, per_device(): there = lax.ppermute(mine, 'x0', other_x0)  1.91 us
  transfers between devices with their start and end apart: 5, of which 1 were waited for; matrix products, arithmetic and copies ran while one was open for 3% of the time, Pallas kernels for 7%

profile of v14, /device:TPU:1, one launch (start us, length us, event | category | flops | bytes accessed | tf_op | source)
XLA Modules:
  0.0 75.8 jit_solution(7998335321125943819)
XLA Ops:
  0.0 5.2 %collective-permute-start.1 = (bf16[800,800]{1,0:T(8,128)(2,1)}, bf16[800,800]{1,0:T(8,128)(2,1)S(1)}, u32[]{:S(2)}, u32[]{:S(2)}) collective-permute-start(bf16[800,800]{1,0:T(8,128)(2,1)} %refs_7_.1), channel_id=1, source_target_pairs={{0,3},{3,0},{1,2},{2,1},{4,7},{7,4},{5,6},{6,5},{8,11},{11,8},{9,1... | collective-permute-start | bytes 3840008 | tf_op jit(solution)/shard_map/ppermute | solution.py:150
  5.9 2.4 %shard_map.73 = bf16[128,8,128]{2,1,0:T(8,128)(2,1)} custom-call(s32[1]{0:T(128)S(6)} %copy.8.pair_ref, bf16[1,102400]{1,0:T(2,128)(2,1)} %row_ref.1), custom_call_target="tpu_custom_call" | custom-call | bytes 700000 | tf_op jit(solution)/shard_map/pallas_call | solution.py:153
  8.3 19.2 %all-to-all-start = ((bf16[64,16,128]{2,1,0:T(8,128)(2,1)}), bf16[64,16,128]{2,1,0:T(8,128)(2,1)S(1)}, u32[]{:S(2)}, u32[]{:S(2)}) async-start(bf16[64,16,128]{2,1,0:T(8,128)(2,1)} %bitcast.15), calls=%async_computation | async-start | bytes 524288 | tf_op jit(solution)/shard_map/all_to_all | solution.py:169
  27.5 3.4 %collective-permute-start.2 = (bf16[800,800]{1,0:T(8,128)(2,1)}, bf16[800,800]{1,0:T(8,128)(2,1)S(1)}, u32[]{:S(2)}, u32[]{:S(2)}) collective-permute-start(bf16[800,800]{1,0:T(8,128)(2,1)} %refs_7_.1), channel_id=1, source_target_pairs={{0,4},{4,0},{1,5},{5,1},{2,6},{6,2},{3,7},{7,3},{8,12},{12,8},{9,1... | collective-permute-start | bytes 3840008 | tf_op jit(solution)/shard_map/ppermute | solution.py:190
  30.9 1.2 %slice.3 = bf16[1,1,1]{2,1,0:T(2,128)(2,1)} slice(bf16[128,8,128]{2,1,0:T(8,128)(2,1)} %shard_map.73), slice={[0:1], [7:8], [0:1]} | slice | bytes 4 | tf_op jit(solution)/shard_map/slice | solution.py:173
  32.8 0.8 %fusion = f32[4,800]{1,0:T(4,128)S(1)} fusion(s32[]{:T(128)S(6)} %convert.2, s32[800]{0:T(1024)} %refs_2_.1, s32[4]{0:T(128)} %param.12), kind=kLoop, calls=%fused_computation.3 | loop fusion | flops 9600 | bytes 16020 | tf_op jit(solution)/shard_map/convert_element_type | solution.py:173
  33.6 0.1 pad_add_fusion.places_ref.refs_0_
  33.7 0.0 all-to-all-done
  33.7 1.9 %collective-permute-start = (bf16[64,2,8,128]{3,2,1,0:T(8,128)(2,1)S(1)}, bf16[64,2,8,128]{3,2,1,0:T(8,128)(2,1)S(1)}, u32[]{:S(2)}, u32[]{:S(2)}) collective-permute-start(bf16[64,2,8,128]{3,2,1,0:T(8,128)(2,1)S(1)} %bitcast.12), channel_id=1, source_target_pairs={{0,1},{1,0},{2,3},{3,2},{4,5},{5,4},{6,7},{7,6},{8,9},{9,8},{10,11... | collective-permute-start | bytes 786440 | tf_op jit(solution)/shard_map/ppermute | solution.py:177
  35.6 0.0 copy-start.1
  35.6 0.7 copy-done.1
  36.3 0.0 copy-start.2
  36.3 1.4 %copy-done.2 = bf16[800,800]{1,0:T(8,128)(2,1)S(1)} copy-done((bf16[800,800]{1,0:T(8,128)(2,1)S(1)}, bf16[800,800]{1,0:T(8,128)(2,1)}, u32[]{:S(2)}) %copy-start.2) | copy-done | bytes 1280024
  37.6 0.0 copy-start.3
  37.6 0.7 copy-done.3
  38.3 1.2 %shard_map.74 = (bf16[64,800]{1,0:T(8,128)(2,1)S(1)}, bf16[64,800]{1,0:T(8,128)(2,1)S(1)}, f32[64,800]{1,0:T(8,128)S(1)}) custom-call(s32[4]{0:T(128)S(1)} %pad_add_fusion.places_ref.refs_0_, s32[128]{0:T(128)S(1)} %copy-done.3, s32[800]{0:T(1024)S(1)} %copy-done.1, bf16[64,2,8,128]{3,2,1,0:T(8,128)(2,1)S(1)} %bitcast.13, bf16[800,800]{1,0:T(8,128)(2,1)S(1)} %copy-done.2), custom_call_target="tpu_custom_call" | custom-call | flops 7200000000 | bytes 24000000 | tf_op jit(solution)/shard_map/pallas_call | solution.py:189
  39.5 0.0 collective-permute-done.1.refs_9_
  39.5 3.5 %collective-permute-start.3 = (bf16[800,800]{1,0:T(8,128)(2,1)S(1)}, bf16[800,800]{1,0:T(8,128)(2,1)S(1)}, u32[]{:S(2)}, u32[]{:S(2)}) collective-permute-start(bf16[800,800]{1,0:T(8,128)(2,1)S(1)} %collective-permute-done.1.refs_9_), channel_id=1, source_target_pairs={{0,4},{4,0},{1,5},{5,1},{2,6},{6,2},{3,7},{7,3},{8,12},{12,8},{9,1... | collective-permute-start | bytes 3840008 | tf_op jit(solution)/shard_map/ppermute | solution.py:192
  43.0 0.0 collective-permute-done.refs_3_
  43.1 0.0 collective-permute-done.2.refs_8_
  43.1 1.9 %shard_map.75 = (bf16[128,800]{1,0:T(8,128)(2,1)S(1)}, f32[896,128]{1,0:T(8,128)S(1)}, f32[128,800]{1,0:T(8,128)S(1)}) custom-call(s32[4]{0:T(128)S(1)} %pad_add_fusion.places_ref.refs_0_, s32[128]{0:T(128)S(1)} %copy-done.3, s32[800]{0:T(1024)S(1)} %copy-done.1, bf16[64,2,8,128]{3,2,1,0:T(8,128)(2,1)S(1)} %collective-permute-done.refs_3_, ...), custom_call_target="tpu_custom_call" | custom-call | flops 12000000000 | bytes 40000000 | tf_op jit(solution)/shard_map/pallas_call | solution.py:201
  45.0 0.9 %collective-permute-done.3.block_ref = bf16[800,800]{1,0:T(8,128)(2,1)S(1)} collective-permute-done((bf16[800,800]{1,0:T(8,128)(2,1)S(1)}, bf16[800,800]{1,0:T(8,128)(2,1)S(1)}, u32[]{:S(2)}, u32[]{:S(2)}) %collective-permute-start.3) | collective-permute-done | bytes 1280032 | tf_op jit(solution)/shard_map/ppermute | solution.py:192
  45.9 0.4 shard_map.76
  46.3 0.0 copy-start
  46.3 0.1 multiply_convert_fusion
  46.4 28.4 %all_to_all.10 = f16[128,7,2,128]{3,2,1,0:T(2,128)(2,1)S(1)} all-to-all(f16[128,7,2,128]{3,2,1,0:T(2,128)(2,1)S(1)} %bitcast.14), channel_id=1, replica_groups={{288,296,304,312,256,264,272,280,32,40,48,56,0,8,16,24,96,104,112,120,6..., dimensions={0} | all-to-all | bytes 917504 | tf_op jit(solution)/shard_map/all_to_all | solution.py:209
  74.7 0.4 convert_reduce_fusion.sums_ref
  75.1 0.0 copy-done
  75.1 0.7 shard_map.77
  (1 shorter events, 0.0 us)
Async XLA Ops:
  0.0 39.5 %collective-permute-start.1 = (bf16[800,800]{1,0:T(8,128)(2,1)}, bf16[800,800]{1,0:T(8,128)(2,1)S(1)}, u32[]{:S(2)}, u32[]{:S(2)}) collective-permute-start(bf16[800,800]{1,0:T(8,128)(2,1)} %refs_7_.1), channel_id=1, source_target_pairs={{0,3},{3,0},{1,2},{2,1},{4,7},{7,4},{5,6},{6,5},{8,11},{11,8},{9,1... | collective-permute-start | bytes 3840008 | tf_op jit(solution)/shard_map/ppermute | solution.py:150
  8.3 25.4 %all-to-all-start = ((bf16[64,16,128]{2,1,0:T(8,128)(2,1)}), bf16[64,16,128]{2,1,0:T(8,128)(2,1)S(1)}, u32[]{:S(2)}, u32[]{:S(2)}) async-start(bf16[64,16,128]{2,1,0:T(8,128)(2,1)} %bitcast.15), calls=%async_computation | async-start | bytes 524288 | tf_op jit(solution)/shard_map/all_to_all | solution.py:169
  27.5 15.6 %collective-permute-start.2 = (bf16[800,800]{1,0:T(8,128)(2,1)}, bf16[800,800]{1,0:T(8,128)(2,1)S(1)}, u32[]{:S(2)}, u32[]{:S(2)}) collective-permute-start(bf16[800,800]{1,0:T(8,128)(2,1)} %refs_7_.1), channel_id=1, source_target_pairs={{0,4},{4,0},{1,5},{5,1},{2,6},{6,2},{3,7},{7,3},{8,12},{12,8},{9,1... | collective-permute-start | bytes 3840008 | tf_op jit(solution)/shard_map/ppermute | solution.py:190
  33.7 9.4 %collective-permute-start = (bf16[64,2,8,128]{3,2,1,0:T(8,128)(2,1)S(1)}, bf16[64,2,8,128]{3,2,1,0:T(8,128)(2,1)S(1)}, u32[]{:S(2)}, u32[]{:S(2)}) collective-permute-start(bf16[64,2,8,128]{3,2,1,0:T(8,128)(2,1)S(1)} %bitcast.12), channel_id=1, source_target_pairs={{0,1},{1,0},{2,3},{3,2},{4,5},{5,4},{6,7},{7,6},{8,9},{9,8},{10,11... | collective-permute-start | bytes 786440 | tf_op jit(solution)/shard_map/ppermute | solution.py:177
  35.6 0.7 copy-start.1
  36.3 1.4 %copy-start.2 = (bf16[800,800]{1,0:T(8,128)(2,1)S(1)}, bf16[800,800]{1,0:T(8,128)(2,1)}, u32[]{:S(2)}) copy-start(bf16[800,800]{1,0:T(8,128)(2,1)} %refs_7_.1) | copy-start | bytes 3840004
  37.6 0.7 copy-start.3
  39.5 6.3 %collective-permute-start.3 = (bf16[800,800]{1,0:T(8,128)(2,1)S(1)}, bf16[800,800]{1,0:T(8,128)(2,1)S(1)}, u32[]{:S(2)}, u32[]{:S(2)}) collective-permute-start(bf16[800,800]{1,0:T(8,128)(2,1)S(1)} %collective-permute-done.1.refs_9_), channel_id=1, source_target_pairs={{0,4},{4,0},{1,5},{5,1},{2,6},{6,2},{3,7},{7,3},{8,12},{12,8},{9,1... | collective-permute-start | bytes 3840008 | tf_op jit(solution)/shard_map/ppermute | solution.py:192
  46.3 28.8 %copy-start = (bf16[1,3200]{1,0:T(2,128)(2,1)S(1)}, bf16[1,3200]{1,0:T(2,128)(2,1)}, u32[]{:S(2)}) copy-start(bf16[1,3200]{1,0:T(2,128)(2,1)} %old_ref.1) | copy-start | bytes 19204

commit v15 on v14

--- a/solution.py
+++ b/solution.py
@@ -14,7 +14,7 @@
 LANES = 128
 TILES = 7
 WIDE = TILES * LANES
-ORDER_Z = (4, 0, 1, 2, 3, 5, 6, 7)
+ORDER_Z = (5, 6, 7, 0, 1, 2, 3, 4)
 ROLLED = [z * 8 + (y + 4) % 8 for z in ORDER_Z for y in range(8)]
 SCALE = 64.0
 

time: 76.4 us -> 76.3 us (level)
    all_to_all x1, starting transfers between devices: 19.2 us -> 18.4 us  [per_device(): lax.all_to_all(cut.reshape(zy, 16, LANES), ('z', 'y'), 0, 0, axis_index_g...]
    ppermute x1, starting transfers between devices: 3.52 us -> 4.34 us  [per_device(): partner2 = lax.ppermute(partner, 'core', other_core)]
  transfers between devices with their start and end apart: 5 -> 5, of which waited for: 1 -> 2; matrix products, arithmetic and copies ran while one was open for 3% -> 3% of each run, Pallas kernels for 7% -> 7%
where the time goes in v15:
time: 76.3 us; the launch traced here: 75.8 us
  starting transfers between devices  33.2 us (44%)
  blocking collectives  28.3 us (37%)
  Pallas kernels  6.61 us (9%)
  local copies, waits for them, and re-layouts  3.94 us (5%)
  between operations  1.47 us (2%)
  other arithmetic  1.31 us (2%)
  waiting for transfers between devices  0.97 us (1%)
    all_to_all x1, blocking collectives, per_device(): lax.all_to_all(part, ('x0', 'z', 'y'), 0, 0, axis_index_groups=[ROLLED +...  28.3 us
    all_to_all x1, starting transfers between devices, per_device(): lax.all_to_all(cut.reshape(zy, 16, LANES), ('z', 'y'), 0, 0, axis_index_g...  18.4 us
    ppermute x1, starting transfers between devices, per_device(): lax.ppermute(integrals, ('x1', 'x0'), [(0, 3), (3, 0), (1, 2), (2, 1)])  5.21 us
    ppermute x1, starting transfers between devices, per_device(): partner2 = lax.ppermute(partner, 'core', other_core)  4.34 us
    ppermute x1, starting transfers between devices, per_device(): block2 = lax.ppermute(block, 'core', other_core)  3.43 us
    unnamed x8, local copies, waits for them, and re-layouts  2.7 us
    pallas_call x1, Pallas kernels, per_device(): pl.pallas_call(functools.partial(cut_body, steps), in_specs=[pl.BlockSpec...  2.38 us
    ppermute x1, starting transfers between devices, per_device(): there = lax.ppermute(mine, 'x0', other_x0)  1.91 us
  transfers between devices with their start and end apart: 5, of which 2 were waited for; matrix products, arithmetic and copies ran while one was open for 3% of the time, Pallas kernels for 7%

profile of v15, /device:TPU:1, one launch (start us, length us, event | category | flops | bytes accessed | tf_op | source)
XLA Modules:
  0.0 75.8 jit_solution(9496578216202241973)
XLA Ops:
  0.0 5.2 %collective-permute-start.1 = (bf16[800,800]{1,0:T(8,128)(2,1)}, bf16[800,800]{1,0:T(8,128)(2,1)S(1)}, u32[]{:S(2)}, u32[]{:S(2)}) collective-permute-start(bf16[800,800]{1,0:T(8,128)(2,1)} %refs_7_.1), channel_id=1, source_target_pairs={{0,3},{3,0},{1,2},{2,1},{4,7},{7,4},{5,6},{6,5},{8,11},{11,8},{9,1... | collective-permute-start | bytes 3840008 | tf_op jit(solution)/shard_map/ppermute | solution.py:150
  5.9 2.4 %shard_map.73 = bf16[128,8,128]{2,1,0:T(8,128)(2,1)} custom-call(s32[1]{0:T(128)S(6)} %copy.8.pair_ref, bf16[1,102400]{1,0:T(2,128)(2,1)} %row_ref.1), custom_call_target="tpu_custom_call" | custom-call | bytes 700000 | tf_op jit(solution)/shard_map/pallas_call | solution.py:153
  8.3 18.4 %all-to-all-start = ((bf16[64,16,128]{2,1,0:T(8,128)(2,1)}), bf16[64,16,128]{2,1,0:T(8,128)(2,1)S(1)}, u32[]{:S(2)}, u32[]{:S(2)}) async-start(bf16[64,16,128]{2,1,0:T(8,128)(2,1)} %bitcast.15), calls=%async_computation | async-start | bytes 524288 | tf_op jit(solution)/shard_map/all_to_all | solution.py:169
  26.6 3.4 %collective-permute-start.2 = (bf16[800,800]{1,0:T(8,128)(2,1)}, bf16[800,800]{1,0:T(8,128)(2,1)S(1)}, u32[]{:S(2)}, u32[]{:S(2)}) collective-permute-start(bf16[800,800]{1,0:T(8,128)(2,1)} %refs_7_.1), channel_id=1, source_target_pairs={{0,4},{4,0},{1,5},{5,1},{2,6},{6,2},{3,7},{7,3},{8,12},{12,8},{9,1... | collective-permute-start | bytes 3840008 | tf_op jit(solution)/shard_map/ppermute | solution.py:190
  30.1 1.2 %slice.3 = bf16[1,1,1]{2,1,0:T(2,128)(2,1)} slice(bf16[128,8,128]{2,1,0:T(8,128)(2,1)} %shard_map.73), slice={[0:1], [7:8], [0:1]} | slice | bytes 4 | tf_op jit(solution)/shard_map/slice | solution.py:173
  32.0 0.8 %fusion = f32[4,800]{1,0:T(4,128)S(1)} fusion(s32[]{:T(128)S(6)} %convert.2, s32[800]{0:T(1024)} %refs_2_.1, s32[4]{0:T(128)} %param.12), kind=kLoop, calls=%fused_computation.3 | loop fusion | flops 9600 | bytes 16020 | tf_op jit(solution)/shard_map/convert_element_type | solution.py:173
  32.7 0.1 pad_add_fusion.places_ref.refs_0_
  32.8 0.1 all-to-all-done
  32.9 1.9 %collective-permute-start = (bf16[64,2,8,128]{3,2,1,0:T(8,128)(2,1)S(1)}, bf16[64,2,8,128]{3,2,1,0:T(8,128)(2,1)S(1)}, u32[]{:S(2)}, u32[]{:S(2)}) collective-permute-start(bf16[64,2,8,128]{3,2,1,0:T(8,128)(2,1)S(1)} %bitcast.12), channel_id=1, source_target_pairs={{0,1},{1,0},{2,3},{3,2},{4,5},{5,4},{6,7},{7,6},{8,9},{9,8},{10,11... | collective-permute-start | bytes 786440 | tf_op jit(solution)/shard_map/ppermute | solution.py:177
  34.8 0.0 copy-start.1
  34.8 0.7 copy-done.1
  35.5 0.0 copy-start.2
  35.5 1.4 %copy-done.2 = bf16[800,800]{1,0:T(8,128)(2,1)S(1)} copy-done((bf16[800,800]{1,0:T(8,128)(2,1)S(1)}, bf16[800,800]{1,0:T(8,128)(2,1)}, u32[]{:S(2)}) %copy-start.2) | copy-done | bytes 1280024
  36.9 0.0 copy-start.3
  36.9 0.7 copy-done.3
  37.5 1.2 %shard_map.74 = (bf16[64,800]{1,0:T(8,128)(2,1)S(1)}, bf16[64,800]{1,0:T(8,128)(2,1)S(1)}, f32[64,800]{1,0:T(8,128)S(1)}) custom-call(s32[4]{0:T(128)S(1)} %pad_add_fusion.places_ref.refs_0_, s32[128]{0:T(128)S(1)} %copy-done.3, s32[800]{0:T(1024)S(1)} %copy-done.1, bf16[64,2,8,128]{3,2,1,0:T(8,128)(2,1)S(1)} %bitcast.13, bf16[800,800]{1,0:T(8,128)(2,1)S(1)} %copy-done.2), custom_call_target="tpu_custom_call" | custom-call | flops 7200000000 | bytes 24000000 | tf_op jit(solution)/shard_map/pallas_call | solution.py:189
  38.7 0.0 collective-permute-done.1.refs_9_
  38.8 4.3 %collective-permute-start.3 = (bf16[800,800]{1,0:T(8,128)(2,1)S(1)}, bf16[800,800]{1,0:T(8,128)(2,1)S(1)}, u32[]{:S(2)}, u32[]{:S(2)}) collective-permute-start(bf16[800,800]{1,0:T(8,128)(2,1)S(1)} %collective-permute-done.1.refs_9_), channel_id=1, source_target_pairs={{0,4},{4,0},{1,5},{5,1},{2,6},{6,2},{3,7},{7,3},{8,12},{12,8},{9,1... | collective-permute-start | bytes 3840008 | tf_op jit(solution)/shard_map/ppermute | solution.py:192
  43.1 0.0 collective-permute-done.refs_3_
  43.1 0.0 collective-permute-done.2.refs_8_
  43.1 1.9 %shard_map.75 = (bf16[128,800]{1,0:T(8,128)(2,1)S(1)}, f32[896,128]{1,0:T(8,128)S(1)}, f32[128,800]{1,0:T(8,128)S(1)}) custom-call(s32[4]{0:T(128)S(1)} %pad_add_fusion.places_ref.refs_0_, s32[128]{0:T(128)S(1)} %copy-done.3, s32[800]{0:T(1024)S(1)} %copy-done.1, bf16[64,2,8,128]{3,2,1,0:T(8,128)(2,1)S(1)} %collective-permute-done.refs_3_, ...), custom_call_target="tpu_custom_call" | custom-call | flops 12000000000 | bytes 40000000 | tf_op jit(solution)/shard_map/pallas_call | solution.py:201
  45.0 0.9 %collective-permute-done.3.block_ref = bf16[800,800]{1,0:T(8,128)(2,1)S(1)} collective-permute-done((bf16[800,800]{1,0:T(8,128)(2,1)S(1)}, bf16[800,800]{1,0:T(8,128)(2,1)S(1)}, u32[]{:S(2)}, u32[]{:S(2)}) %collective-permute-start.3) | collective-permute-done | bytes 1280032 | tf_op jit(solution)/shard_map/ppermute | solution.py:192
  45.9 0.4 shard_map.76
  46.3 0.0 copy-start
  46.4 0.1 multiply_convert_fusion
  46.5 28.3 %all_to_all.10 = f16[128,7,2,128]{3,2,1,0:T(2,128)(2,1)S(1)} all-to-all(f16[128,7,2,128]{3,2,1,0:T(2,128)(2,1)S(1)} %bitcast.14), channel_id=1, replica_groups={{352,360,368,376,320,328,336,344,416,424,432,440,384,392,400,408,480,48..., dimensions={0} | all-to-all | bytes 917504 | tf_op jit(solution)/shard_map/all_to_all | solution.py:209
  74.7 0.4 convert_reduce_fusion.sums_ref
  75.1 0.0 copy-done
  75.1 0.7 shard_map.77
  (1 shorter events, 0.0 us)
Async XLA Ops:
  0.0 38.7 %collective-permute-start.1 = (bf16[800,800]{1,0:T(8,128)(2,1)}, bf16[800,800]{1,0:T(8,128)(2,1)S(1)}, u32[]{:S(2)}, u32[]{:S(2)}) collective-permute-start(bf16[800,800]{1,0:T(8,128)(2,1)} %refs_7_.1), channel_id=1, source_target_pairs={{0,3},{3,0},{1,2},{2,1},{4,7},{7,4},{5,6},{6,5},{8,11},{11,8},{9,1... | collective-permute-start | bytes 3840008 | tf_op jit(solution)/shard_map/ppermute | solution.py:150
  8.3 24.7 %all-to-all-start = ((bf16[64,16,128]{2,1,0:T(8,128)(2,1)}), bf16[64,16,128]{2,1,0:T(8,128)(2,1)S(1)}, u32[]{:S(2)}, u32[]{:S(2)}) async-start(bf16[64,16,128]{2,1,0:T(8,128)(2,1)} %bitcast.15), calls=%async_computation | async-start | bytes 524288 | tf_op jit(solution)/shard_map/all_to_all | solution.py:169
  26.6 16.5 %collective-permute-start.2 = (bf16[800,800]{1,0:T(8,128)(2,1)}, bf16[800,800]{1,0:T(8,128)(2,1)S(1)}, u32[]{:S(2)}, u32[]{:S(2)}) collective-permute-start(bf16[800,800]{1,0:T(8,128)(2,1)} %refs_7_.1), channel_id=1, source_target_pairs={{0,4},{4,0},{1,5},{5,1},{2,6},{6,2},{3,7},{7,3},{8,12},{12,8},{9,1... | collective-permute-start | bytes 3840008 | tf_op jit(solution)/shard_map/ppermute | solution.py:190
  32.9 10.2 %collective-permute-start = (bf16[64,2,8,128]{3,2,1,0:T(8,128)(2,1)S(1)}, bf16[64,2,8,128]{3,2,1,0:T(8,128)(2,1)S(1)}, u32[]{:S(2)}, u32[]{:S(2)}) collective-permute-start(bf16[64,2,8,128]{3,2,1,0:T(8,128)(2,1)S(1)} %bitcast.12), channel_id=1, source_target_pairs={{0,1},{1,0},{2,3},{3,2},{4,5},{5,4},{6,7},{7,6},{8,9},{9,8},{10,11... | collective-permute-start | bytes 786440 | tf_op jit(solution)/shard_map/ppermute | solution.py:177
  34.8 0.7 copy-start.1
  35.5 1.4 %copy-start.2 = (bf16[800,800]{1,0:T(8,128)(2,1)S(1)}, bf16[800,800]{1,0:T(8,128)(2,1)}, u32[]{:S(2)}) copy-start(bf16[800,800]{1,0:T(8,128)(2,1)} %refs_7_.1) | copy-start | bytes 3840004
  36.9 0.7 copy-start.3
  38.8 7.2 %collective-permute-start.3 = (bf16[800,800]{1,0:T(8,128)(2,1)S(1)}, bf16[800,800]{1,0:T(8,128)(2,1)S(1)}, u32[]{:S(2)}, u32[]{:S(2)}) collective-permute-start(bf16[800,800]{1,0:T(8,128)(2,1)S(1)} %collective-permute-done.1.refs_9_), channel_id=1, source_target_pairs={{0,4},{4,0},{1,5},{5,1},{2,6},{6,2},{3,7},{7,3},{8,12},{12,8},{9,1... | collective-permute-start | bytes 3840008 | tf_op jit(solution)/shard_map/ppermute | solution.py:192
  46.3 28.8 %copy-start = (bf16[1,3200]{1,0:T(2,128)(2,1)S(1)}, bf16[1,3200]{1,0:T(2,128)(2,1)}, u32[]{:S(2)}) copy-start(bf16[1,3200]{1,0:T(2,128)(2,1)} %old_ref.1) | copy-start | bytes 19204

commit v16 on v15

--- a/solution.py
+++ b/solution.py
@@ -100,7 +100,7 @@
     places_ref, slab_ref, virt_ref, tiles_ref, lhs_ref, lhs2_ref, sums_ref = refs[:7]
     own_ref, own2_ref, block_ref = refs[7:10]
     rows2_ref, own_sums_ref, out_ref, flat, wide, rows, sums = refs[10:]
-    here = pl.multiple_of(places_ref[1] * zy, zy)
+    here = pl.multiple_of((1 - places_ref[1]) * zy, zy)
     there = pl.multiple_of(zy - here, zy)
     rows[pl.ds(here, zy), :] = lhs_ref[...]
     rows2_ref[pl.ds(here, zy), :] = lhs2_ref[...]
@@ -123,7 +123,7 @@
 
 def finish_body(sums_ref, kept_ref, old_ref, out_ref):
     swap = kept_ref[4:5, 0:LANES] > 0.5
-    order = ((0, 0), (1, 0), (1, 1), (0, 1))
+    order = ((1, 0), (0, 0), (0, 1), (1, 1))
     for a in range(4):
         (s, h), (s2, h2) = order[a], order[(a + 2) % 4]
         tiles = []
@@ -207,7 +207,7 @@
     part = ladder(rows2, partner2, sums, own_sums)
     part = (part * SCALE).astype(F16).reshape(2 * zy, TILES, 2, LANES)
     back = lax.all_to_all(
-        part, ("x0", "z", "y"), 0, 0, axis_index_groups=[ROLLED + [64 + i for i in ROLLED]], tiled=True
+        part, ("x0", "z", "y"), 0, 0, axis_index_groups=[[64 + i for i in ROLLED] + ROLLED], tiled=True
     )
     sums = jnp.sum(back.reshape(2, zy, TILES, 2, LANES).astype(F32), axis=1)
     finish = call(finish_body, shape((1, 4 * NV), BF16), "vvv", 0, 50000)

time: 76.3 us -> 75.9 us (level)
  no operation moved by 1% of the time
where the time goes in v16:
time: 75.9 us; the launch traced here: 75.4 us
  starting transfers between devices  33.2 us (44%)
  blocking collectives  27.9 us (37%)
  Pallas kernels  6.61 us (9%)
  local copies, waits for them, and re-layouts  3.94 us (5%)
  between operations  1.47 us (2%)
  other arithmetic  1.31 us (2%)
  waiting for transfers between devices  0.97 us (1%)
    all_to_all x1, blocking collectives, per_device(): lax.all_to_all(part, ('x0', 'z', 'y'), 0, 0, axis_index_groups=[[64 + i f...  27.9 us
    all_to_all x1, starting transfers between devices, per_device(): lax.all_to_all(cut.reshape(zy, 16, LANES), ('z', 'y'), 0, 0, axis_index_g...  18.4 us
    ppermute x1, starting transfers between devices, per_device(): lax.ppermute(integrals, ('x1', 'x0'), [(0, 3), (3, 0), (1, 2), (2, 1)])  5.21 us
    ppermute x1, starting transfers between devices, per_device(): partner2 = lax.ppermute(partner, 'core', other_core)  4.34 us
    ppermute x1, starting transfers between devices, per_device(): block2 = lax.ppermute(block, 'core', other_core)  3.43 us
    unnamed x8, local copies, waits for them, and re-layouts  2.7 us
    pallas_call x1, Pallas kernels, per_device(): pl.pallas_call(functools.partial(cut_body, steps), in_specs=[pl.BlockSpec...  2.38 us
    ppermute x1, starting transfers between devices, per_device(): there = lax.ppermute(mine, 'x0', other_x0)  1.91 us
  transfers between devices with their start and end apart: 5, of which 2 were waited for; matrix products, arithmetic and copies ran while one was open for 3% of the time, Pallas kernels for 7%

profile of v16, /device:TPU:1, one launch (start us, length us, event | category | flops | bytes accessed | tf_op | source)
XLA Modules:
  0.0 75.4 jit_solution(9297980461975973579)
XLA Ops:
  0.0 5.2 %collective-permute-start.1 = (bf16[800,800]{1,0:T(8,128)(2,1)}, bf16[800,800]{1,0:T(8,128)(2,1)S(1)}, u32[]{:S(2)}, u32[]{:S(2)}) collective-permute-start(bf16[800,800]{1,0:T(8,128)(2,1)} %refs_7_.1), channel_id=1, source_target_pairs={{0,3},{3,0},{1,2},{2,1},{4,7},{7,4},{5,6},{6,5},{8,11},{11,8},{9,1... | collective-permute-start | bytes 3840008 | tf_op jit(solution)/shard_map/ppermute | solution.py:150
  5.9 2.4 %shard_map.73 = bf16[128,8,128]{2,1,0:T(8,128)(2,1)} custom-call(s32[1]{0:T(128)S(6)} %copy.8.pair_ref, bf16[1,102400]{1,0:T(2,128)(2,1)} %row_ref.1), custom_call_target="tpu_custom_call" | custom-call | bytes 700000 | tf_op jit(solution)/shard_map/pallas_call | solution.py:153
  8.3 18.4 %all-to-all-start = ((bf16[64,16,128]{2,1,0:T(8,128)(2,1)}), bf16[64,16,128]{2,1,0:T(8,128)(2,1)S(1)}, u32[]{:S(2)}, u32[]{:S(2)}) async-start(bf16[64,16,128]{2,1,0:T(8,128)(2,1)} %bitcast.15), calls=%async_computation | async-start | bytes 524288 | tf_op jit(solution)/shard_map/all_to_all | solution.py:169
  26.6 3.4 %collective-permute-start.2 = (bf16[800,800]{1,0:T(8,128)(2,1)}, bf16[800,800]{1,0:T(8,128)(2,1)S(1)}, u32[]{:S(2)}, u32[]{:S(2)}) collective-permute-start(bf16[800,800]{1,0:T(8,128)(2,1)} %refs_7_.1), channel_id=1, source_target_pairs={{0,4},{4,0},{1,5},{5,1},{2,6},{6,2},{3,7},{7,3},{8,12},{12,8},{9,1... | collective-permute-start | bytes 3840008 | tf_op jit(solution)/shard_map/ppermute | solution.py:190
  30.1 1.2 %slice.3 = bf16[1,1,1]{2,1,0:T(2,128)(2,1)} slice(bf16[128,8,128]{2,1,0:T(8,128)(2,1)} %shard_map.73), slice={[0:1], [7:8], [0:1]} | slice | bytes 4 | tf_op jit(solution)/shard_map/slice | solution.py:173
  32.0 0.8 %fusion = f32[4,800]{1,0:T(4,128)S(1)} fusion(s32[]{:T(128)S(6)} %convert.2, s32[800]{0:T(1024)} %refs_2_.1, s32[4]{0:T(128)} %param.12), kind=kLoop, calls=%fused_computation.3 | loop fusion | flops 9600 | bytes 16020 | tf_op jit(solution)/shard_map/convert_element_type | solution.py:173
  32.7 0.1 pad_add_fusion.places_ref.refs_0_
  32.8 0.1 all-to-all-done
  32.9 1.9 %collective-permute-start = (bf16[64,2,8,128]{3,2,1,0:T(8,128)(2,1)S(1)}, bf16[64,2,8,128]{3,2,1,0:T(8,128)(2,1)S(1)}, u32[]{:S(2)}, u32[]{:S(2)}) collective-permute-start(bf16[64,2,8,128]{3,2,1,0:T(8,128)(2,1)S(1)} %bitcast.12), channel_id=1, source_target_pairs={{0,1},{1,0},{2,3},{3,2},{4,5},{5,4},{6,7},{7,6},{8,9},{9,8},{10,11... | collective-permute-start | bytes 786440 | tf_op jit(solution)/shard_map/ppermute | solution.py:177
  34.8 0.0 copy-start.1
  34.8 0.7 copy-done.1
  35.5 0.0 copy-start.2
  35.5 1.4 %copy-done.2 = bf16[800,800]{1,0:T(8,128)(2,1)S(1)} copy-done((bf16[800,800]{1,0:T(8,128)(2,1)S(1)}, bf16[800,800]{1,0:T(8,128)(2,1)}, u32[]{:S(2)}) %copy-start.2) | copy-done | bytes 1280024
  36.9 0.0 copy-start.3
  36.9 0.7 copy-done.3
  37.5 1.2 %shard_map.74 = (bf16[64,800]{1,0:T(8,128)(2,1)S(1)}, bf16[64,800]{1,0:T(8,128)(2,1)S(1)}, f32[64,800]{1,0:T(8,128)S(1)}) custom-call(s32[4]{0:T(128)S(1)} %pad_add_fusion.places_ref.refs_0_, s32[128]{0:T(128)S(1)} %copy-done.3, s32[800]{0:T(1024)S(1)} %copy-done.1, bf16[64,2,8,128]{3,2,1,0:T(8,128)(2,1)S(1)} %bitcast.13, bf16[800,800]{1,0:T(8,128)(2,1)S(1)} %copy-done.2), custom_call_target="tpu_custom_call" | custom-call | flops 7200000000 | bytes 24000000 | tf_op jit(solution)/shard_map/pallas_call | solution.py:189
  38.7 0.0 collective-permute-done.1.refs_9_
  38.8 4.3 %collective-permute-start.3 = (bf16[800,800]{1,0:T(8,128)(2,1)S(1)}, bf16[800,800]{1,0:T(8,128)(2,1)S(1)}, u32[]{:S(2)}, u32[]{:S(2)}) collective-permute-start(bf16[800,800]{1,0:T(8,128)(2,1)S(1)} %collective-permute-done.1.refs_9_), channel_id=1, source_target_pairs={{0,4},{4,0},{1,5},{5,1},{2,6},{6,2},{3,7},{7,3},{8,12},{12,8},{9,1... | collective-permute-start | bytes 3840008 | tf_op jit(solution)/shard_map/ppermute | solution.py:192
  43.1 0.0 collective-permute-done.refs_3_
  43.1 0.0 collective-permute-done.2.refs_8_
  43.1 1.9 %shard_map.75 = (bf16[128,800]{1,0:T(8,128)(2,1)S(1)}, f32[896,128]{1,0:T(8,128)S(1)}, f32[128,800]{1,0:T(8,128)S(1)}) custom-call(s32[4]{0:T(128)S(1)} %pad_add_fusion.places_ref.refs_0_, s32[128]{0:T(128)S(1)} %copy-done.3, s32[800]{0:T(1024)S(1)} %copy-done.1, bf16[64,2,8,128]{3,2,1,0:T(8,128)(2,1)S(1)} %collective-permute-done.refs_3_, ...), custom_call_target="tpu_custom_call" | custom-call | flops 12000000000 | bytes 40000000 | tf_op jit(solution)/shard_map/pallas_call | solution.py:201
  45.0 0.9 %collective-permute-done.3.block_ref = bf16[800,800]{1,0:T(8,128)(2,1)S(1)} collective-permute-done((bf16[800,800]{1,0:T(8,128)(2,1)S(1)}, bf16[800,800]{1,0:T(8,128)(2,1)S(1)}, u32[]{:S(2)}, u32[]{:S(2)}) %collective-permute-start.3) | collective-permute-done | bytes 1280032 | tf_op jit(solution)/shard_map/ppermute | solution.py:192
  45.9 0.4 shard_map.76
  46.3 0.0 copy-start
  46.4 0.1 multiply_convert_fusion
  46.5 27.9 %all_to_all.10 = f16[128,7,2,128]{3,2,1,0:T(2,128)(2,1)S(1)} all-to-all(f16[128,7,2,128]{3,2,1,0:T(2,128)(2,1)S(1)} %bitcast.14), channel_id=1, replica_groups={{353,361,369,377,321,329,337,345,417,425,433,441,385,393,401,409,481,48..., dimensions={0} | all-to-all | bytes 917504 | tf_op jit(solution)/shard_map/all_to_all | solution.py:209
  74.3 0.4 convert_reduce_fusion.sums_ref
  74.7 0.0 copy-done
  74.7 0.7 shard_map.77
  (1 shorter events, 0.0 us)
Async XLA Ops:
  0.0 38.7 %collective-permute-start.1 = (bf16[800,800]{1,0:T(8,128)(2,1)}, bf16[800,800]{1,0:T(8,128)(2,1)S(1)}, u32[]{:S(2)}, u32[]{:S(2)}) collective-permute-start(bf16[800,800]{1,0:T(8,128)(2,1)} %refs_7_.1), channel_id=1, source_target_pairs={{0,3},{3,0},{1,2},{2,1},{4,7},{7,4},{5,6},{6,5},{8,11},{11,8},{9,1... | collective-permute-start | bytes 3840008 | tf_op jit(solution)/shard_map/ppermute | solution.py:150
  8.3 24.7 %all-to-all-start = ((bf16[64,16,128]{2,1,0:T(8,128)(2,1)}), bf16[64,16,128]{2,1,0:T(8,128)(2,1)S(1)}, u32[]{:S(2)}, u32[]{:S(2)}) async-start(bf16[64,16,128]{2,1,0:T(8,128)(2,1)} %bitcast.15), calls=%async_computation | async-start | bytes 524288 | tf_op jit(solution)/shard_map/all_to_all | solution.py:169
  26.6 16.5 %collective-permute-start.2 = (bf16[800,800]{1,0:T(8,128)(2,1)}, bf16[800,800]{1,0:T(8,128)(2,1)S(1)}, u32[]{:S(2)}, u32[]{:S(2)}) collective-permute-start(bf16[800,800]{1,0:T(8,128)(2,1)} %refs_7_.1), channel_id=1, source_target_pairs={{0,4},{4,0},{1,5},{5,1},{2,6},{6,2},{3,7},{7,3},{8,12},{12,8},{9,1... | collective-permute-start | bytes 3840008 | tf_op jit(solution)/shard_map/ppermute | solution.py:190
  32.9 10.2 %collective-permute-start = (bf16[64,2,8,128]{3,2,1,0:T(8,128)(2,1)S(1)}, bf16[64,2,8,128]{3,2,1,0:T(8,128)(2,1)S(1)}, u32[]{:S(2)}, u32[]{:S(2)}) collective-permute-start(bf16[64,2,8,128]{3,2,1,0:T(8,128)(2,1)S(1)} %bitcast.12), channel_id=1, source_target_pairs={{0,1},{1,0},{2,3},{3,2},{4,5},{5,4},{6,7},{7,6},{8,9},{9,8},{10,11... | collective-permute-start | bytes 786440 | tf_op jit(solution)/shard_map/ppermute | solution.py:177
  34.8 0.7 copy-start.1
  35.5 1.4 %copy-start.2 = (bf16[800,800]{1,0:T(8,128)(2,1)S(1)}, bf16[800,800]{1,0:T(8,128)(2,1)}, u32[]{:S(2)}) copy-start(bf16[800,800]{1,0:T(8,128)(2,1)} %refs_7_.1) | copy-start | bytes 3840004
  36.9 0.7 copy-start.3
  38.8 7.2 %collective-permute-start.3 = (bf16[800,800]{1,0:T(8,128)(2,1)S(1)}, bf16[800,800]{1,0:T(8,128)(2,1)S(1)}, u32[]{:S(2)}, u32[]{:S(2)}) collective-permute-start(bf16[800,800]{1,0:T(8,128)(2,1)S(1)} %collective-permute-done.1.refs_9_), channel_id=1, source_target_pairs={{0,4},{4,0},{1,5},{5,1},{2,6},{6,2},{3,7},{7,3},{8,12},{12,8},{9,1... | collective-permute-start | bytes 3840008 | tf_op jit(solution)/shard_map/ppermute | solution.py:192
  46.3 28.3 %copy-start = (bf16[1,3200]{1,0:T(2,128)(2,1)S(1)}, bf16[1,3200]{1,0:T(2,128)(2,1)}, u32[]{:S(2)}) copy-start(bf16[1,3200]{1,0:T(2,128)(2,1)} %old_ref.1) | copy-start | bytes 19204

commit v17 on v16

--- a/solution.py
+++ b/solution.py
@@ -14,7 +14,7 @@
 LANES = 128
 TILES = 7
 WIDE = TILES * LANES
-ORDER_Z = (5, 6, 7, 0, 1, 2, 3, 4)
+ORDER_Z = (4, 5, 6, 7, 0, 1, 2, 3)
 ROLLED = [z * 8 + (y + 4) % 8 for z in ORDER_Z for y in range(8)]
 SCALE = 64.0
 

time: 75.9 us -> 76.3 us (level)
    ppermute x1, starting transfers between devices: 4.34 us -> 3.32 us  [per_device(): partner2 = lax.ppermute(partner, 'core', other_core)]
    all_to_all x1, starting transfers between devices: 18.4 us -> 19.3 us  [per_device(): lax.all_to_all(cut.reshape(zy, 16, LANES), ('z', 'y'), 0, 0, axis_index_g...]
  transfers between devices with their start and end apart: 5 -> 5, of which waited for: 2 -> 1; matrix products, arithmetic and copies ran while one was open for 3% -> 3% of each run, Pallas kernels for 7% -> 7%
where the time goes in v17:
time: 76.3 us; the launch traced here: 75.8 us
  starting transfers between devices  33.2 us (44%)
  blocking collectives  28.4 us (37%)
  Pallas kernels  6.62 us (9%)
  local copies, waits for them, and re-layouts  3.94 us (5%)
  between operations  1.47 us (2%)
  other arithmetic  1.31 us (2%)
  waiting for transfers between devices  0.9 us (1%)
    all_to_all x1, blocking collectives, per_device(): lax.all_to_all(part, ('x0', 'z', 'y'), 0, 0, axis_index_groups=[[64 + i f...  28.4 us
    all_to_all x1, starting transfers between devices, per_device(): lax.all_to_all(cut.reshape(zy, 16, LANES), ('z', 'y'), 0, 0, axis_index_g...  19.3 us
    ppermute x1, starting transfers between devices, per_device(): lax.ppermute(integrals, ('x1', 'x0'), [(0, 3), (3, 0), (1, 2), (2, 1)])  5.21 us
    ppermute x1, starting transfers between devices, per_device(): block2 = lax.ppermute(block, 'core', other_core)  3.43 us
    ppermute x1, starting transfers between devices, per_device(): partner2 = lax.ppermute(partner, 'core', other_core)  3.32 us
    unnamed x8, local copies, waits for them, and re-layouts  2.7 us
    pallas_call x1, Pallas kernels, per_device(): pl.pallas_call(functools.partial(cut_body, steps), in_specs=[pl.BlockSpec...  2.39 us
    ppermute x1, starting transfers between devices, per_device(): there = lax.ppermute(mine, 'x0', other_x0)  1.91 us
  transfers between devices with their start and end apart: 5, of which 1 were waited for; matrix products, arithmetic and copies ran while one was open for 3% of the time, Pallas kernels for 7%

profile of v17, /device:TPU:1, one launch (start us, length us, event | category | flops | bytes accessed | tf_op | source)
XLA Modules:
  0.0 75.8 jit_solution(14681268531588513227)
XLA Ops:
  0.0 5.2 %collective-permute-start.1 = (bf16[800,800]{1,0:T(8,128)(2,1)}, bf16[800,800]{1,0:T(8,128)(2,1)S(1)}, u32[]{:S(2)}, u32[]{:S(2)}) collective-permute-start(bf16[800,800]{1,0:T(8,128)(2,1)} %refs_7_.1), channel_id=1, source_target_pairs={{0,3},{3,0},{1,2},{2,1},{4,7},{7,4},{5,6},{6,5},{8,11},{11,8},{9,1... | collective-permute-start | bytes 3840008 | tf_op jit(solution)/shard_map/ppermute | solution.py:150
  5.9 2.4 %shard_map.73 = bf16[128,8,128]{2,1,0:T(8,128)(2,1)} custom-call(s32[1]{0:T(128)S(6)} %copy.8.pair_ref, bf16[1,102400]{1,0:T(2,128)(2,1)} %row_ref.1), custom_call_target="tpu_custom_call" | custom-call | bytes 700000 | tf_op jit(solution)/shard_map/pallas_call | solution.py:153
  8.3 19.3 %all-to-all-start = ((bf16[64,16,128]{2,1,0:T(8,128)(2,1)}), bf16[64,16,128]{2,1,0:T(8,128)(2,1)S(1)}, u32[]{:S(2)}, u32[]{:S(2)}) async-start(bf16[64,16,128]{2,1,0:T(8,128)(2,1)} %bitcast.15), calls=%async_computation | async-start | bytes 524288 | tf_op jit(solution)/shard_map/all_to_all | solution.py:169
  27.6 3.4 %collective-permute-start.2 = (bf16[800,800]{1,0:T(8,128)(2,1)}, bf16[800,800]{1,0:T(8,128)(2,1)S(1)}, u32[]{:S(2)}, u32[]{:S(2)}) collective-permute-start(bf16[800,800]{1,0:T(8,128)(2,1)} %refs_7_.1), channel_id=1, source_target_pairs={{0,4},{4,0},{1,5},{5,1},{2,6},{6,2},{3,7},{7,3},{8,12},{12,8},{9,1... | collective-permute-start | bytes 3840008 | tf_op jit(solution)/shard_map/ppermute | solution.py:190
  31.0 1.2 %slice.3 = bf16[1,1,1]{2,1,0:T(2,128)(2,1)} slice(bf16[128,8,128]{2,1,0:T(8,128)(2,1)} %shard_map.73), slice={[0:1], [7:8], [0:1]} | slice | bytes 4 | tf_op jit(solution)/shard_map/slice | solution.py:173
  32.9 0.8 %fusion = f32[4,800]{1,0:T(4,128)S(1)} fusion(s32[]{:T(128)S(6)} %convert.2, s32[800]{0:T(1024)} %refs_2_.1, s32[4]{0:T(128)} %param.12), kind=kLoop, calls=%fused_computation.3 | loop fusion | flops 9600 | bytes 16020 | tf_op jit(solution)/shard_map/convert_element_type | solution.py:173
  33.7 0.1 pad_add_fusion.places_ref.refs_0_
  33.8 0.0 all-to-all-done
  33.8 1.9 %collective-permute-start = (bf16[64,2,8,128]{3,2,1,0:T(8,128)(2,1)S(1)}, bf16[64,2,8,128]{3,2,1,0:T(8,128)(2,1)S(1)}, u32[]{:S(2)}, u32[]{:S(2)}) collective-permute-start(bf16[64,2,8,128]{3,2,1,0:T(8,128)(2,1)S(1)} %bitcast.12), channel_id=1, source_target_pairs={{0,1},{1,0},{2,3},{3,2},{4,5},{5,4},{6,7},{7,6},{8,9},{9,8},{10,11... | collective-permute-start | bytes 786440 | tf_op jit(solution)/shard_map/ppermute | solution.py:177
  35.7 0.0 copy-start.1
  35.7 0.7 copy-done.1
  36.4 0.0 copy-start.2
  36.4 1.4 %copy-done.2 = bf16[800,800]{1,0:T(8,128)(2,1)S(1)} copy-done((bf16[800,800]{1,0:T(8,128)(2,1)S(1)}, bf16[800,800]{1,0:T(8,128)(2,1)}, u32[]{:S(2)}) %copy-start.2) | copy-done | bytes 1280024
  37.8 0.0 copy-start.3
  37.8 0.7 copy-done.3
  38.4 1.2 %shard_map.74 = (bf16[64,800]{1,0:T(8,128)(2,1)S(1)}, bf16[64,800]{1,0:T(8,128)(2,1)S(1)}, f32[64,800]{1,0:T(8,128)S(1)}) custom-call(s32[4]{0:T(128)S(1)} %pad_add_fusion.places_ref.refs_0_, s32[128]{0:T(128)S(1)} %copy-done.3, s32[800]{0:T(1024)S(1)} %copy-done.1, bf16[64,2,8,128]{3,2,1,0:T(8,128)(2,1)S(1)} %bitcast.13, bf16[800,800]{1,0:T(8,128)(2,1)S(1)} %copy-done.2), custom_call_target="tpu_custom_call" | custom-call | flops 7200000000 | bytes 24000000 | tf_op jit(solution)/shard_map/pallas_call | solution.py:189
  39.6 0.0 collective-permute-done.1.refs_9_
  39.6 3.3 %collective-permute-start.3 = (bf16[800,800]{1,0:T(8,128)(2,1)S(1)}, bf16[800,800]{1,0:T(8,128)(2,1)S(1)}, u32[]{:S(2)}, u32[]{:S(2)}) collective-permute-start(bf16[800,800]{1,0:T(8,128)(2,1)S(1)} %collective-permute-done.1.refs_9_), channel_id=1, source_target_pairs={{0,4},{4,0},{1,5},{5,1},{2,6},{6,2},{3,7},{7,3},{8,12},{12,8},{9,1... | collective-permute-start | bytes 3840008 | tf_op jit(solution)/shard_map/ppermute | solution.py:192
  43.0 0.0 collective-permute-done.refs_3_
  43.0 0.0 collective-permute-done.2.refs_8_
  43.0 1.9 %shard_map.75 = (bf16[128,800]{1,0:T(8,128)(2,1)S(1)}, f32[896,128]{1,0:T(8,128)S(1)}, f32[128,800]{1,0:T(8,128)S(1)}) custom-call(s32[4]{0:T(128)S(1)} %pad_add_fusion.places_ref.refs_0_, s32[128]{0:T(128)S(1)} %copy-done.3, s32[800]{0:T(1024)S(1)} %copy-done.1, bf16[64,2,8,128]{3,2,1,0:T(8,128)(2,1)S(1)} %collective-permute-done.refs_3_, ...), custom_call_target="tpu_custom_call" | custom-call | flops 12000000000 | bytes 40000000 | tf_op jit(solution)/shard_map/pallas_call | solution.py:201
  44.9 0.9 %collective-permute-done.3.block_ref = bf16[800,800]{1,0:T(8,128)(2,1)S(1)} collective-permute-done((bf16[800,800]{1,0:T(8,128)(2,1)S(1)}, bf16[800,800]{1,0:T(8,128)(2,1)S(1)}, u32[]{:S(2)}, u32[]{:S(2)}) %collective-permute-start.3) | collective-permute-done | bytes 1280032 | tf_op jit(solution)/shard_map/ppermute | solution.py:192
  45.8 0.4 shard_map.76
  46.2 0.0 copy-start
  46.2 0.1 multiply_convert_fusion
  46.3 28.4 %all_to_all.10 = f16[128,7,2,128]{3,2,1,0:T(2,128)(2,1)S(1)} all-to-all(f16[128,7,2,128]{3,2,1,0:T(2,128)(2,1)S(1)} %bitcast.14), channel_id=1, replica_groups={{289,297,305,313,257,265,273,281,353,361,369,377,321,329,337,345,417,42..., dimensions={0} | all-to-all | bytes 917504 | tf_op jit(solution)/shard_map/all_to_all | solution.py:209
  74.7 0.4 convert_reduce_fusion.sums_ref
  75.1 0.0 copy-done
  75.1 0.7 shard_map.77
  (1 shorter events, 0.0 us)
Async XLA Ops:
  0.0 39.6 %collective-permute-start.1 = (bf16[800,800]{1,0:T(8,128)(2,1)}, bf16[800,800]{1,0:T(8,128)(2,1)S(1)}, u32[]{:S(2)}, u32[]{:S(2)}) collective-permute-start(bf16[800,800]{1,0:T(8,128)(2,1)} %refs_7_.1), channel_id=1, source_target_pairs={{0,3},{3,0},{1,2},{2,1},{4,7},{7,4},{5,6},{6,5},{8,11},{11,8},{9,1... | collective-permute-start | bytes 3840008 | tf_op jit(solution)/shard_map/ppermute | solution.py:150
  8.3 25.5 %all-to-all-start = ((bf16[64,16,128]{2,1,0:T(8,128)(2,1)}), bf16[64,16,128]{2,1,0:T(8,128)(2,1)S(1)}, u32[]{:S(2)}, u32[]{:S(2)}) async-start(bf16[64,16,128]{2,1,0:T(8,128)(2,1)} %bitcast.15), calls=%async_computation | async-start | bytes 524288 | tf_op jit(solution)/shard_map/all_to_all | solution.py:169
  27.6 15.4 %collective-permute-start.2 = (bf16[800,800]{1,0:T(8,128)(2,1)}, bf16[800,800]{1,0:T(8,128)(2,1)S(1)}, u32[]{:S(2)}, u32[]{:S(2)}) collective-permute-start(bf16[800,800]{1,0:T(8,128)(2,1)} %refs_7_.1), channel_id=1, source_target_pairs={{0,4},{4,0},{1,5},{5,1},{2,6},{6,2},{3,7},{7,3},{8,12},{12,8},{9,1... | collective-permute-start | bytes 3840008 | tf_op jit(solution)/shard_map/ppermute | solution.py:190
  33.8 9.2 %collective-permute-start = (bf16[64,2,8,128]{3,2,1,0:T(8,128)(2,1)S(1)}, bf16[64,2,8,128]{3,2,1,0:T(8,128)(2,1)S(1)}, u32[]{:S(2)}, u32[]{:S(2)}) collective-permute-start(bf16[64,2,8,128]{3,2,1,0:T(8,128)(2,1)S(1)} %bitcast.12), channel_id=1, source_target_pairs={{0,1},{1,0},{2,3},{3,2},{4,5},{5,4},{6,7},{7,6},{8,9},{9,8},{10,11... | collective-permute-start | bytes 786440 | tf_op jit(solution)/shard_map/ppermute | solution.py:177
  35.7 0.7 copy-start.1
  36.4 1.4 %copy-start.2 = (bf16[800,800]{1,0:T(8,128)(2,1)S(1)}, bf16[800,800]{1,0:T(8,128)(2,1)}, u32[]{:S(2)}) copy-start(bf16[800,800]{1,0:T(8,128)(2,1)} %refs_7_.1) | copy-start | bytes 3840004
  37.8 0.7 copy-start.3
  39.6 6.1 %collective-permute-start.3 = (bf16[800,800]{1,0:T(8,128)(2,1)S(1)}, bf16[800,800]{1,0:T(8,128)(2,1)S(1)}, u32[]{:S(2)}, u32[]{:S(2)}) collective-permute-start(bf16[800,800]{1,0:T(8,128)(2,1)S(1)} %collective-permute-done.1.refs_9_), channel_id=1, source_target_pairs={{0,4},{4,0},{1,5},{5,1},{2,6},{6,2},{3,7},{7,3},{8,12},{12,8},{9,1... | collective-permute-start | bytes 3840008 | tf_op jit(solution)/shard_map/ppermute | solution.py:192
  46.2 28.9 %copy-start = (bf16[1,3200]{1,0:T(2,128)(2,1)S(1)}, bf16[1,3200]{1,0:T(2,128)(2,1)}, u32[]{:S(2)}) copy-start(bf16[1,3200]{1,0:T(2,128)(2,1)} %old_ref.1) | copy-start | bytes 19204
